TPU v7x, 32 devices: a whole 2x2x4 slice. The times are simulated.
32 devices in a mesh: lon: 16 (over z, x, core), lat: 2 (over y).
Axes of the slice: x: 2, y: 2, z: 4, core: 2. Of those that a mesh axis runs over, the one named last changes fastest.
Arguments:
- tokens: bfloat16 [32, 1024, 768], P('lat', 'lon'), may hold values from -6 to 6
- qkv_weight: bfloat16 [768, 2304], replicated, may hold values from -0.21875 to 0.21875
- out_weight: bfloat16 [768, 768], replicated, may hold values from -0.5 to 0.5
- bias_table: float32 [465, 6], replicated, may hold values from -6 to 256
- position_index: int32 [128, 128], replicated, may hold values from 0 to 464
- region_label: int32 [32, 1024], P('lat', 'lon'), may hold values from 0 to 3
Outputs:
- updated: bfloat16 [32, 1024, 768], P('lat', 'lon')
All inputs are finite; a program needn't handle non-finite values.
Results may differ from a plain program's by a relative error of at most 0.007.
Values may be sent and summed in bfloat16 or wider, within the bound.
No kernel may reach another device: no remote copies, remote signals or barrier semaphores. Data moves between devices by JAX's collectives and lax.ppermute only.
A program may use at most 64 MiB of HBM per device.

v0:
```python
import jax
import jax.numpy as jnp
from jax import lax
from jax.sharding import PartitionSpec as P

HEADS = 6
WLAT = 8
WLON = 16


def from_behind(block, axis, distance):
    devices = range(lax.axis_size(axis))
    route = [((i - distance) % len(devices), i) for i in devices]
    return lax.ppermute(block, axis, route)


def normalize(values):
    floats = values.astype(jnp.float32)
    center = jnp.mean(floats, axis=-1, keepdims=True)
    spread = jnp.mean(jnp.square(floats - center), axis=-1, keepdims=True)
    return ((floats - center) * lax.rsqrt(spread + 1e-05)).astype(jnp.bfloat16)


def bias_lookup(bias_table, position_index):
    cells = position_index.shape[0]
    entries = bias_table.shape[0]
    blocks = position_index.reshape(8, cells * cells // 8)

    def one_block(indices):
        columns = lax.broadcasted_iota(jnp.int32, (indices.shape[0], entries), 1)
        onehot = (indices[:, None] == columns).astype(jnp.float32)
        return lax.dot_general(
            bias_table,
            onehot,
            (((0,), (1,)), ((), ())),
            precision=lax.Precision.HIGHEST,
            preferred_element_type=jnp.float32,
        )

    looked = lax.map(one_block, blocks)
    looked = looked.transpose(1, 0, 2).reshape(HEADS, cells, cells)
    return lax.optimization_barrier(looked)


def attend(qkv, labels, bias_heads, out_weight):
    row_count, column_count, triple = qkv.shape
    feature_count = triple // 3
    head_size = feature_count // HEADS
    band_count = row_count // WLAT
    strip_count = column_count // WLON
    windows = qkv.reshape(band_count, WLAT, strip_count, WLON, triple).transpose(0, 2, 1, 3, 4)
    windows = windows.reshape(band_count * strip_count, WLAT * WLON, triple)
    queries = windows[:, :, :feature_count].reshape(-1, WLAT * WLON, HEADS, head_size)
    key_part = windows[:, :, feature_count : 2 * feature_count].reshape(
        -1, WLAT * WLON, HEADS, head_size
    )
    values = windows[:, :, 2 * feature_count :].reshape(-1, WLAT * WLON, HEADS, head_size)
    label_windows = labels.reshape(band_count, WLAT, strip_count, WLON).transpose(0, 2, 1, 3)
    label_windows = label_windows.reshape(band_count * strip_count, WLAT * WLON)
    matching = (label_windows[:, :, None] == label_windows[:, None, :])[:, None]
    scores = jnp.einsum("wqhd,wkhd->whqk", queries, key_part, preferred_element_type=jnp.float32)
    scores = scores * (1.0 / jnp.sqrt(jnp.float32(head_size))) + bias_heads[None]
    largest = jnp.max(jnp.where(matching, scores, -jnp.inf), axis=-1, keepdims=True)
    numerators = jnp.exp(jnp.where(matching, scores - largest, -jnp.inf))
    weights = (numerators / jnp.sum(numerators, axis=-1, keepdims=True)).astype(jnp.bfloat16)
    attended = jnp.einsum(
        "whqk,wkhd->wqhd", weights, values, preferred_element_type=jnp.float32
    ).astype(jnp.bfloat16)
    attended = attended.reshape(band_count, strip_count, WLAT, WLON, feature_count).transpose(
        0, 2, 1, 3, 4
    )
    attended = attended.reshape(row_count, column_count, feature_count)
    return jnp.dot(attended, out_weight, preferred_element_type=jnp.float32).astype(jnp.bfloat16)


def move_ahead(source):
    half_lat = WLAT // 2
    half_lon = WLON // 2
    columns = from_behind(source[:, :half_lon], "lon", -1)
    widened = jnp.concatenate([source[:, half_lon:], columns], axis=1)
    lower_band = from_behind(widened[:half_lat], "lat", -1)
    return jnp.concatenate([widened[half_lat:], lower_band], axis=0)


def move_behind(source):
    half_lat = WLAT // 2
    half_lon = WLON // 2
    columns = from_behind(source[:, -half_lon:], "lon", 1)
    widened = jnp.concatenate([columns, source[:, :-half_lon]], axis=1)
    upper_band = from_behind(widened[-half_lat:], "lat", 1)
    return jnp.concatenate([upper_band, widened[:-half_lat]], axis=0)


def shards(tokens, qkv_weight, out_weight, bias_table, position_index, region_label):
    bias_heads = bias_lookup(bias_table, position_index)
    normed = normalize(tokens)
    shifted = move_ahead(normed)
    qkv = jnp.dot(shifted, qkv_weight, preferred_element_type=jnp.float32).astype(jnp.bfloat16)
    branch = attend(qkv, region_label, bias_heads, out_weight)
    returned = move_behind(branch)
    return (tokens.astype(jnp.float32) + returned.astype(jnp.float32)).astype(jnp.bfloat16)


def solution(mesh):
    in_specs = (P("lat", "lon", None), P(), P(), P(), P(), P("lat", "lon"))
    out_specs = P("lat", "lon", None)
    return jax.shard_map(shards, mesh=mesh, in_specs=in_specs, out_specs=out_specs, check_vma=False)
```

profile of v0, /device:TPU:0, one launch (start us, length us, event | category | flops | bytes accessed | tf_op | source)
XLA Modules:
  0.0 112.5 jit_solution(9841738544950421242)
XLA Ops:
  0.0 0.0 copy-start
  0.0 0.0 copy-start.1
  0.0 1.8 %convert_reduce_fusion = f32[16,64]{1,0:T(8,128)S(1)} fusion(bf16[16,64,768]{2,1,0:T(8,128)(2,1)} %param.8), kind=kLoop, calls=%fused_computation.10 | loop fusion | flops 1571840 | bytes 1576960 | tf_op jit(solution)/shard_map/reduce_sum | solution.py:19
  1.9 0.2 copy-done.1
  2.0 0.6 fusion.8
  2.6 0.4 fusion.9
  3.1 0.7 slice.45
  3.7 5.4 %collective-permute-start = (bf16[16,8,768]{2,1,0:T(8,128)(2,1)}, bf16[16,8,768]{2,1,0:T(8,128)(2,1)}, u32[]{:S(2)}, u32[]{:S(2)}) collective-permute-start(bf16[16,8,768]{2,1,0:T(8,128)(2,1)} %slice.45), channel_id=1, source_target_pairs={{2,0},{4,2},{6,4},{8,6},{10,8},{12,10},{14,12},{16,14},{18,16},{20... | collective-permute-start | bytes 589832 | tf_op jit(solution)/shard_map/ppermute | solution.py:14
  9.2 1.2 %slice.44 = bf16[16,56,768]{2,1,0:T(8,128)(2,1)} slice(bf16[16,64,768]{2,1,0:T(8,128)(2,1)S(1)} %fusion.9), slice={[0:16], [8:64], [0:768]} | slice | bytes 2752512 | tf_op jit(solution)/shard_map/slice | solution.py:80
  10.3 0.0 copy-start.5
  10.3 1.5 %reshape.56 = s32[8,2048]{1,0:T(8,128)} reshape(s32[128,128]{1,0:T(8,128)} %param.12) | data formatting | bytes 131072 | tf_op jit(solution)/shard_map/reshape | solution.py:27
  11.8 0.8 collective-permute-done
  12.7 1.8 %pad_maximum_fusion.2 = bf16[4,64,768]{2,1,0:T(8,128)(2,1)} fusion(bf16[16,8,768]{2,1,0:T(8,128)(2,1)} %collective-permute-done, bf16[16,56,768]{2,1,0:T(8,128)(2,1)} %slice.44), kind=kLoop, calls=%fused_computation.40 | loop fusion | flops 786432 | bytes 1966080 | tf_op jit(solution)/shard_map/concatenate | solution.py:80
  14.4 1.5 %collective-permute-start.1 = (bf16[4,64,768]{2,1,0:T(8,128)(2,1)}, bf16[4,64,768]{2,1,0:T(8,128)(2,1)}, u32[]{:S(2)}, u32[]{:S(2)}) collective-permute-start(bf16[4,64,768]{2,1,0:T(8,128)(2,1)} %pad_maximum_fusion.2), channel_id=1, source_target_pairs={{1,0},{0,1},{3,2},{2,3},{5,4},{4,5},{7,6},{6,7},{9,8},{8,9},{11,10... | collective-permute-start | bytes 1179656 | tf_op jit(solution)/shard_map/ppermute | solution.py:14
  16.0 0.0 copy-done.5
  16.0 29.5 %while.10 = (s32[]{:T(128)}, f32[8,6,2048]{2,1,0:T(8,128)}, s32[8,2048]{1,0:T(8,128)}, f32[465,6]{0,1:T(8,128)S(1)}, s32[]{:T(128)}) while((s32[]{:T(128)}, f32[8,6,2048]{2,1,0:T(8,128)}, s32[8,2048]{1,0:T(8,128)}, f32[465,6]{0,1:T(8,128)S(1)}, s32[]{:T(128)}) %tuple.24), condition=%wide.region_3.4_spmd, body=%wide.region_2.3_spmd.sunk | while | flops 69519360 | bytes 101849 | solution.py:40
  16.0 0.8 constant_dynamic-slice_fusion.2
  16.8 2.8 %fusion.43 = f32[8,6,2048]{2,1,0:T(8,128)} fusion(f32[8,6,2048]{2,1,0:T(8,128)} %get-tuple-element.72, s32[]{:T(128)} %get-tuple-element.71, f32[465,6]{0,1:T(8,128)S(1)} %get-tuple-element.79, s32[2048]{0:T(1024)S(1)} %bitcast.51), kind=kOutput, calls=%fused_computation.3.clone.1 | convolution fusion | flops 69519360 | bytes 85400 | tf_op jit(solution)/shard_map/while/body/eval_jaxpr/dot_general | solution.py:32
  19.7 0.8 constant_dynamic-slice_fusion.2
  20.5 2.8 %fusion.43 = f32[8,6,2048]{2,1,0:T(8,128)} fusion(f32[8,6,2048]{2,1,0:T(8,128)} %get-tuple-element.72, s32[]{:T(128)} %get-tuple-element.71, f32[465,6]{0,1:T(8,128)S(1)} %get-tuple-element.79, s32[2048]{0:T(1024)S(1)} %bitcast.51), kind=kOutput, calls=%fused_computation.3.clone.1 | convolution fusion | flops 69519360 | bytes 85400 | tf_op jit(solution)/shard_map/while/body/eval_jaxpr/dot_general | solution.py:32
  23.3 0.8 constant_dynamic-slice_fusion.2
  24.2 2.8 %fusion.43 = f32[8,6,2048]{2,1,0:T(8,128)} fusion(f32[8,6,2048]{2,1,0:T(8,128)} %get-tuple-element.72, s32[]{:T(128)} %get-tuple-element.71, f32[465,6]{0,1:T(8,128)S(1)} %get-tuple-element.79, s32[2048]{0:T(1024)S(1)} %bitcast.51), kind=kOutput, calls=%fused_computation.3.clone.1 | convolution fusion | flops 69519360 | bytes 85400 | tf_op jit(solution)/shard_map/while/body/eval_jaxpr/dot_general | solution.py:32
  27.0 0.8 constant_dynamic-slice_fusion.2
  27.9 2.8 %fusion.43 = f32[8,6,2048]{2,1,0:T(8,128)} fusion(f32[8,6,2048]{2,1,0:T(8,128)} %get-tuple-element.72, s32[]{:T(128)} %get-tuple-element.71, f32[465,6]{0,1:T(8,128)S(1)} %get-tuple-element.79, s32[2048]{0:T(1024)S(1)} %bitcast.51), kind=kOutput, calls=%fused_computation.3.clone.1 | convolution fusion | flops 69519360 | bytes 85400 | tf_op jit(solution)/shard_map/while/body/eval_jaxpr/dot_general | solution.py:32
  30.7 0.8 constant_dynamic-slice_fusion.2
  31.6 2.8 %fusion.43 = f32[8,6,2048]{2,1,0:T(8,128)} fusion(f32[8,6,2048]{2,1,0:T(8,128)} %get-tuple-element.72, s32[]{:T(128)} %get-tuple-element.71, f32[465,6]{0,1:T(8,128)S(1)} %get-tuple-element.79, s32[2048]{0:T(1024)S(1)} %bitcast.51), kind=kOutput, calls=%fused_computation.3.clone.1 | convolution fusion | flops 69519360 | bytes 85400 | tf_op jit(solution)/shard_map/while/body/eval_jaxpr/dot_general | solution.py:32
  34.4 0.8 constant_dynamic-slice_fusion.2
  35.2 2.8 %fusion.43 = f32[8,6,2048]{2,1,0:T(8,128)} fusion(f32[8,6,2048]{2,1,0:T(8,128)} %get-tuple-element.72, s32[]{:T(128)} %get-tuple-element.71, f32[465,6]{0,1:T(8,128)S(1)} %get-tuple-element.79, s32[2048]{0:T(1024)S(1)} %bitcast.51), kind=kOutput, calls=%fused_computation.3.clone.1 | convolution fusion | flops 69519360 | bytes 85400 | tf_op jit(solution)/shard_map/while/body/eval_jaxpr/dot_general | solution.py:32
  38.1 0.8 constant_dynamic-slice_fusion.2
  38.9 2.8 %fusion.43 = f32[8,6,2048]{2,1,0:T(8,128)} fusion(f32[8,6,2048]{2,1,0:T(8,128)} %get-tuple-element.72, s32[]{:T(128)} %get-tuple-element.71, f32[465,6]{0,1:T(8,128)S(1)} %get-tuple-element.79, s32[2048]{0:T(1024)S(1)} %bitcast.51), kind=kOutput, calls=%fused_computation.3.clone.1 | convolution fusion | flops 69519360 | bytes 85400 | tf_op jit(solution)/shard_map/while/body/eval_jaxpr/dot_general | solution.py:32
  41.8 0.8 constant_dynamic-slice_fusion.2
  42.6 2.8 %fusion.43 = f32[8,6,2048]{2,1,0:T(8,128)} fusion(f32[8,6,2048]{2,1,0:T(8,128)} %get-tuple-element.72, s32[]{:T(128)} %get-tuple-element.71, f32[465,6]{0,1:T(8,128)S(1)} %get-tuple-element.79, s32[2048]{0:T(1024)S(1)} %bitcast.51), kind=kOutput, calls=%fused_computation.3.clone.1 | convolution fusion | flops 69519360 | bytes 85400 | tf_op jit(solution)/shard_map/while/body/eval_jaxpr/dot_general | solution.py:32
  45.5 2.0 %copy.27 = f32[6,8,2048]{2,1,0:T(8,128)} copy(f32[6,8,2048]{2,0,1:T(8,128)} %bitcast.50) | data formatting | bytes 786432 | tf_op jit(solution)/shard_map/transpose | solution.py:41
  47.5 1.8 %reshape.57 = f32[6,128,128]{2,1,0:T(8,128)} reshape(f32[6,8,2048]{2,1,0:T(8,128)} %copy.27) | data formatting | bytes 786432 | tf_op jit(solution)/shard_map/reshape | solution.py:41
  49.3 1.9 %copy.28 = f32[6,128,128]{1,2,0:T(8,128)} copy(f32[6,128,128]{2,1,0:T(8,128)} %reshape.57) | data formatting | bytes 786432 | tf_op jit(solution)/shard_map/optimization_barrier | solution.py:42
  51.2 0.0 copy-done.3
  51.2 0.7 reshape.53
  51.9 1.4 %copy.36 = s32[2,8,4,16]{3,1,2,0:T(8,128)} copy(s32[2,8,4,16]{3,2,1,0:T(4,128)} %reshape.53) | data formatting | bytes 8192 | tf_op jit(solution)/shard_map/reshape | solution.py:58
  53.3 0.8 eq.29
  54.1 0.9 broadcast_compare_fusion
  55.0 1.3 %fusion.24 = bf16[12,64,768]{2,1,0:T(8,128)(2,1)S(1)} fusion(bf16[16,56,768]{2,1,0:T(8,128)(2,1)} %slice.44, bf16[16,8,768]{2,1,0:T(8,128)(2,1)} %collective-permute-done), kind=kLoop, calls=%fused_computation.37 | loop fusion | flops 2359296 | bytes 2752512 | tf_op jit(solution)/shard_map/concatenate | solution.py:80
  56.3 0.0 collective-permute-done.1
  56.3 0.0 copy-done
  56.3 5.5 %convolution_convert_fusion = bf16[16,64,2304]{2,1,0:T(8,128)(2,1)S(1)} fusion(bf16[768,2304]{1,0:T(8,128)(2,1)S(1)} %copy-done, bf16[4,64,768]{2,1,0:T(8,128)(2,1)} %collective-permute-done.1, bf16[12,64,768]{2,1,0:T(8,128)(2,1)S(1)} %fusion.24), kind=kOutput, calls=%fused_computation.7 | convolution fusion | flops 3627024384 | bytes 9830400 | tf_op jit(solution)/shard_map/dot_general | solution.py:98
  61.8 0.4 copy.20
  62.3 2.3 %fusion.29 = (bf16[8,128,768]{2,1,0:T(8,128)(2,1)}, bf16[8,128,768]{2,1,0:T(8,128)(2,1)}, bf16[8,128,768]{2,1,0:T(8,128)(2,1)}) fusion(bf16[8,128,2304]{2,1,0:T(8,128)(2,1)S(1)} %bitcast.43), kind=kLoop, calls=%fused_computation.48 | loop fusion | bytes 9437184 | tf_op jit(solution)/shard_map/slice | solution.py:54
  64.6 2.6 %copy.23 = bf16[8,128,768]{1,2,0:T(8,128)(2,1)} copy(bf16[8,128,768]{2,1,0:T(8,128)(2,1)} %get-tuple-element.37) | data formatting | bytes 3145728 | tf_op jit(solution)/shard_map/slice | solution.py:53
  67.2 2.6 %copy.24 = bf16[8,128,768]{1,2,0:T(8,128)(2,1)} copy(bf16[8,128,768]{2,1,0:T(8,128)(2,1)} %get-tuple-element.36) | data formatting | bytes 3145728 | tf_op jit(solution)/shard_map/slice | solution.py:54
  69.8 2.6 %copy.21 = bf16[8,128,768]{1,2,0:T(8,128)(2,1)} copy(bf16[8,128,768]{2,1,0:T(8,128)(2,1)} %get-tuple-element.38) | data formatting | bytes 3145728 | tf_op jit(solution)/shard_map/slice | solution.py:57
  72.3 7.4 %fusion.30 = (f32[8,6,128]{2,1,0:T(8,128)}, f32[8,6,128,128]{2,3,1,0:T(8,128)}) fusion(f32[6,128,128]{1,2,0:T(8,128)} %copy.28, pred[8,128,128]{1,2,0:T(8,128)(4,1)} %broadcast_compare_fusion, bf16[8,128,6,128]{1,3,2,0:T(8,128)(2,1)} %bitcast.46, bf16[8,128,6,128]{1,3,2,0:T(8,128)(2,1)} %bitcast.47), kind=kOutput, calls=%fused_computation.49 | convolution fusion | flops 408944768 | bytes 6840320 | tf_op jit(solution)/shard_map/sub | solution.py:64
  79.7 4.1 %fusion.23 = bf16[8,128,6,128]{1,3,2,0:T(8,128)(2,1)} fusion(bf16[8,128,6,128]{1,3,2,0:T(8,128)(2,1)} %bitcast.48, f32[8,6,128,128]{2,3,1,0:T(8,128)} %get-tuple-element.40, f32[8,6,128]{2,1,0:T(8,128)} %get-tuple-element.39), kind=kOutput, calls=%fused_computation.36 | convolution fusion | flops 203685888 | bytes 6316032 | tf_op jit(solution)/shard_map/whqk,wkhd->wqhd/dot_general | solution.py:66
  83.8 3.9 %copy.30 = bf16[8,128,6,128]{3,2,1,0:T(8,128)(2,1)} copy(bf16[8,128,6,128]{1,3,2,0:T(8,128)(2,1)} %fusion.23) | data formatting | bytes 3145728 | tf_op jit(solution)/shard_map/convert_element_type | solution.py:68
  87.7 4.4 %reshape.58 = bf16[2,4,8,16,768]{4,3,2,1,0:T(8,128)(2,1)} reshape(bf16[8,128,6,128]{3,2,1,0:T(8,128)(2,1)} %copy.30) | data formatting | bytes 3145728 | tf_op jit(solution)/shard_map/reshape | solution.py:69
  92.0 1.7 %copy.31 = bf16[2,8,4,16,768]{4,3,2,1,0:T(8,128)(2,1)S(1)} copy(bf16[2,8,4,16,768]{4,3,1,2,0:T(8,128)(2,1)} %bitcast.44) | data formatting | bytes 3145728 | tf_op jit(solution)/shard_map/transpose | solution.py:69
  93.7 0.1 copy-done.4
  93.8 1.4 %convolution_convert_fusion.1 = bf16[16,64,768]{2,1,0:T(8,128)(2,1)S(1)} fusion(bf16[16,64,768]{2,1,0:T(8,128)(2,1)S(1)} %bitcast.49, bf16[768,768]{1,0:T(8,128)(2,1)S(1)} %copy-done.4), kind=kOutput, calls=%fused_computation.22 | convolution fusion | flops 1208745984 | bytes 4325376 | tf_op jit(solution)/shard_map/dot_general | solution.py:73
  95.2 0.1 collective-permute-start.2
  95.3 0.1 slice.52
  95.4 0.0 copy-start.2
  95.4 7.7 %collective-permute-done.2 = bf16[16,8,768]{2,1,0:T(8,128)(2,1)S(1)} collective-permute-done((bf16[16,8,768]{2,1,0:T(8,128)(2,1)S(1)}, bf16[16,8,768]{2,1,0:T(8,128)(2,1)S(1)}, u32[]{:S(2)}, u32[]{:S(2)}) %collective-permute-start.2) | collective-permute-done | bytes 196640 | tf_op jit(solution)/shard_map/ppermute | solution.py:14
  103.1 0.6 collective-permute-start.3
  103.6 7.3 %collective-permute-done.3 = bf16[4,64,768]{2,1,0:T(8,128)(2,1)S(1)} collective-permute-done((bf16[4,64,768]{2,1,0:T(8,128)(2,1)S(1)}, bf16[4,64,768]{2,1,0:T(8,128)(2,1)S(1)}, u32[]{:S(2)}, u32[]{:S(2)}) %collective-permute-start.3) | collective-permute-done | bytes 393248 | tf_op jit(solution)/shard_map/ppermute | solution.py:14
  110.9 0.0 copy-done.2
  110.9 1.6 %fusion.10 = bf16[16,64,768]{2,1,0:T(8,128)(2,1)} fusion(bf16[16,64,768]{2,1,0:T(8,128)(2,1)S(1)} %copy-done.2, bf16[16,56,768]{2,1,0:T(8,128)(2,1)S(1)} %slice.52, bf16[16,8,768]{2,1,0:T(8,128)(2,1)S(1)} %collective-permute-done.2, bf16[4,64,768]{2,1,0:T(8,128)(2,1)S(1)} %collective-permute-done.3), kind=kLoop, calls=%fused_computation.16 | loop fusion | flops 7077888 | bytes 5111808 | tf_op jit(solution)/shard_map/convert_element_type | solution.py:101
  (7 shorter events, 0.1 us)
Async XLA Ops:
  0.0 56.3 %copy-start = (bf16[768,2304]{1,0:T(8,128)(2,1)S(1)}, bf16[768,2304]{1,0:T(8,128)(2,1)}, u32[]{:S(2)}) copy-start(bf16[768,2304]{1,0:T(8,128)(2,1)} %param.9) | copy-start | bytes 10616836
  0.0 2.0 %copy-start.1 = (bf16[16,64,768]{2,1,0:T(8,128)(2,1)S(1)}, bf16[16,64,768]{2,1,0:T(8,128)(2,1)}, u32[]{:S(2)}) copy-start(bf16[16,64,768]{2,1,0:T(8,128)(2,1)} %param.8) | copy-start | bytes 4718596
  3.7 8.9 %collective-permute-start = (bf16[16,8,768]{2,1,0:T(8,128)(2,1)}, bf16[16,8,768]{2,1,0:T(8,128)(2,1)}, u32[]{:S(2)}, u32[]{:S(2)}) collective-permute-start(bf16[16,8,768]{2,1,0:T(8,128)(2,1)} %slice.45), channel_id=1, source_target_pairs={{2,0},{4,2},{6,4},{8,6},{10,8},{12,10},{14,12},{16,14},{18,16},{20... | collective-permute-start | bytes 589832 | tf_op jit(solution)/shard_map/ppermute | solution.py:14
  10.3 5.6 %copy-start.5 = (f32[465,6]{0,1:T(8,128)S(1)}, f32[465,6]{0,1:T(8,128)}, u32[]{:S(2)}) copy-start(f32[465,6]{0,1:T(8,128)} %param.11) | copy-start | bytes 33484
  14.4 41.9 %collective-permute-start.1 = (bf16[4,64,768]{2,1,0:T(8,128)(2,1)}, bf16[4,64,768]{2,1,0:T(8,128)(2,1)}, u32[]{:S(2)}, u32[]{:S(2)}) collective-permute-start(bf16[4,64,768]{2,1,0:T(8,128)(2,1)} %pad_maximum_fusion.2), channel_id=1, source_target_pairs={{1,0},{0,1},{3,2},{2,3},{5,4},{4,5},{7,6},{6,7},{9,8},{8,9},{11,10... | collective-permute-start | bytes 1179656 | tf_op jit(solution)/shard_map/ppermute | solution.py:14
  45.5 5.8 %copy-start.3 = (s32[16,64]{1,0:T(8,128)S(1)}, s32[16,64]{1,0:T(8,128)}, u32[]{:S(2)}) copy-start(s32[16,64]{1,0:T(8,128)} %param.13) | copy-start | bytes 12292
  92.0 1.7 %copy-start.4 = (bf16[768,768]{1,0:T(8,128)(2,1)S(1)}, bf16[768,768]{1,0:T(8,128)(2,1)}, u32[]{:S(2)}) copy-start(bf16[768,768]{1,0:T(8,128)(2,1)} %param.10) | copy-start | bytes 3538948
  95.2 7.8 %collective-permute-start.2 = (bf16[16,8,768]{2,1,0:T(8,128)(2,1)S(1)}, bf16[16,8,768]{2,1,0:T(8,128)(2,1)S(1)}, u32[]{:S(2)}, u32[]{:S(2)}) collective-permute-start(bf16[16,8,768]{2,1,0:T(8,128)(2,1)S(1)} %slice.51), channel_id=1, source_target_pairs={{30,0},{0,2},{2,4},{4,6},{6,8},{8,10},{10,12},{12,14},{14,16},{16,... | collective-permute-start | bytes 589832 | tf_op jit(solution)/shard_map/ppermute | solution.py:14
  95.4 15.6 %copy-start.2 = (bf16[16,64,768]{2,1,0:T(8,128)(2,1)S(1)}, bf16[16,64,768]{2,1,0:T(8,128)(2,1)}, u32[]{:S(2)}) copy-start(bf16[16,64,768]{2,1,0:T(8,128)(2,1)} %param.8) | copy-start | bytes 4718596
  103.1 7.8 %collective-permute-start.3 = (bf16[4,64,768]{2,1,0:T(8,128)(2,1)S(1)}, bf16[4,64,768]{2,1,0:T(8,128)(2,1)S(1)}, u32[]{:S(2)}, u32[]{:S(2)}) collective-permute-start(bf16[4,64,768]{2,1,0:T(8,128)(2,1)S(1)} %pad_maximum_fusion.1), channel_id=1, source_target_pairs={{1,0},{0,1},{3,2},{2,3},{5,4},{4,5},{7,6},{6,7},{9,8},{8,9},{11,10... | collective-permute-start | bytes 1179656 | tf_op jit(solution)/shard_map/ppermute | solution.py:14
where the time goes:
time: 114 us; the launch traced here: 113 us
  matrix products  41 us (36%)
  local copies, waits for them, and re-layouts  39.6 us (35%)
  waiting for transfers between devices  15.8 us (14%)
  other arithmetic  8.42 us (7%)
  starting transfers between devices  7.56 us (7%)
    dot_general x8, matrix products, one_block(): lax.dot_general(bias_table, onehot, (((0,), (1,)), ((), ())), precision=l...  22.7 us
    ppermute x4, waiting for transfers between devices, from_behind(): return lax.ppermute(block, axis, route)  15.8 us
    ppermute x4, starting transfers between devices, from_behind(): return lax.ppermute(block, axis, route)  7.56 us
    sub x1, matrix products, attend(): numerators = jnp.exp(jnp.where(matching, scores - largest, -jnp.inf))  7.37 us
    dynamic_slice x8, local copies, waits for them, and re-layouts, bias_lookup(): looked = lax.map(one_block, blocks)  6.78 us
    dot_general x1, matrix products, shards(): jnp.dot(shifted, qkv_weight, preferred_element_type=jnp.float32)  5.5 us
    slice x2, local copies, waits for them, and re-layouts, attend(): windows[:, :, feature_count:2 * feature_count]  4.92 us
    reshape x1, local copies, waits for them, and re-layouts, attend(): attended.reshape(band_count, strip_count, WLAT, WLON, feature_count)  4.36 us
  transfers between devices with their start and end apart: 4, of which 3 were waited for; matrix products, arithmetic and copies ran while one was open for 38% of the time, Pallas kernels for 0%

commit v1 on v0

v1 whole, which is shorter than its diff:
```python
import functools

import jax
import jax.numpy as jnp
from jax import lax
from jax.experimental import pallas as pl
from jax.experimental.pallas import tpu as pltpu
from jax.sharding import PartitionSpec as P

HEADS = 6
HEAD = 128
WLAT = 8
WLON = 16
WIN = WLAT * WLON
HALF_LAT = WLAT // 2
HALF_LON = WLON // 2
LOG2E = 1.4426950408889634
SCALE = LOG2E / HEAD**0.5
EXCLUDED = -1e30
VMEM_LIMIT = 24 * 2**20
VMEM = pl.BlockSpec(memory_space=pltpu.VMEM)

TOP, MIDDLE, BOTTOM = (HALF_LAT, WLAT), (0, WLAT), (0, HALF_LAT)
LEFT, INNER, RIGHT = (HALF_LON, WLON), (0, WLON), (0, HALF_LON)


def moved(block, axis, distance):
    count = lax.axis_size(axis)
    route = [((i - distance) % count, i) for i in range(count)]
    return lax.ppermute(block, axis, route)


def lat_halo(first, last):
    if lax.axis_size("lat") == 2:
        both = moved(jnp.concatenate([last, first], axis=0), "lat", 1)
        return both[:HALF_LAT], both[HALF_LAT:]
    return moved(last, "lat", 1), moved(first, "lat", -1)


def bias_kernel(table_ref, index_ref, out_ref):
    table = table_ref[...]
    for row in range(0, WIN, 8):
        index = index_ref[row : row + 8, :]
        low, high = index & 127, index >> 7
        for head in range(HEADS):
            value = jnp.zeros((8, WIN), jnp.float32)
            for part in range(4):
                source = jnp.broadcast_to(table[head : head + 1, part * 128 : part * 128 + 128], (8, 128))
                taken = jnp.take_along_axis(source, low, axis=1)
                value = jnp.where(high == part, taken, value)
            out_ref[head, row : row + 8, :] = value * LOG2E


def bias_lookup(bias_table, position_index):
    table = jnp.pad(bias_table.T, ((0, 8 - HEADS), (0, 512 - bias_table.shape[0])))
    return pl.pallas_call(
        bias_kernel,
        out_shape=jax.ShapeDtypeStruct((HEADS, WIN, WIN), jnp.float32),
        in_specs=[VMEM, VMEM],
        out_specs=VMEM,
        compiler_params=pltpu.CompilerParams(vmem_limit_bytes=VMEM_LIMIT),
        cost_estimate=pl.CostEstimate(flops=10**6, bytes_accessed=10**6, transcendentals=0),
    )(table, position_index)


def window_kernel(parts, x_ref, label_ref, bias_ref, qkv_weight_ref, out_weight_ref, out_ref, keys_ref, queries_ref, attended_ref):
    feature = x_ref.shape[-1]
    counts = [(r[1] - r[0]) * (c[1] - c[0]) for r, c in parts]
    starts = [sum(counts[:i]) for i in range(len(parts))]
    for w, (rows, columns) in enumerate(parts):
        floats = x_ref[w].astype(jnp.float32)
        center = jnp.mean(floats, axis=-1, keepdims=True)
        floats = floats - center
        spread = jnp.mean(jnp.square(floats), axis=-1, keepdims=True)
        normed = floats * lax.rsqrt(spread + 1e-05)
        keys_ref[w * WIN : (w + 1) * WIN, :] = normed.reshape(WIN, feature).astype(jnp.bfloat16)
        own = normed[rows[0] : rows[1], columns[0] : columns[1]].reshape(counts[w], feature)
        queries_ref[starts[w] : starts[w] + counts[w], :] = own.astype(jnp.bfloat16)

    def own_rows(array, w):
        rows, columns = parts[w]
        if array.shape[0] == counts[w]:
            return array
        array = array.reshape(WLAT, WLON, array.shape[-1])
        return array[rows[0] : rows[1], columns[0] : columns[1]].reshape(counts[w], array.shape[-1])

    labels = label_ref[...].astype(jnp.float32)
    label_columns = labels.T
    excluded = []
    for w in range(len(parts)):
        same = label_columns[:, w : w + 1] == labels[w : w + 1, :]
        excluded.append(own_rows(jnp.where(same, 0.0, EXCLUDED), w))

    def project(source_ref, first):
        weight = qkv_weight_ref[:, first : first + 2 * HEAD]
        return jnp.dot(source_ref[...], weight, preferred_element_type=jnp.float32).astype(jnp.bfloat16)

    for pair in range(HEADS // 2):
        queries = project(queries_ref, pair * 2 * HEAD)
        keys = project(keys_ref, feature + pair * 2 * HEAD)
        values = project(keys_ref, 2 * feature + pair * 2 * HEAD)
        for w in range(len(parts)):
            mine = slice(starts[w], starts[w] + counts[w])
            whole = slice(w * WIN, (w + 1) * WIN)
            for side in range(2):
                head = pair * 2 + side
                lanes = slice(side * HEAD, (side + 1) * HEAD)
                scores = lax.dot_general(
                    queries[mine, lanes], keys[whole, lanes], (((1,), (1,)), ((), ())), preferred_element_type=jnp.float32
                )
                scores = scores * SCALE + (own_rows(bias_ref[head], w) + excluded[w])
                numerators = jnp.exp2(scores - jnp.max(scores, axis=-1, keepdims=True))
                total = jnp.sum(numerators, axis=-1, keepdims=True)
                summed = jnp.dot(numerators.astype(jnp.bfloat16), values[whole, lanes], preferred_element_type=jnp.float32)
                attended_ref[mine, head * HEAD : (head + 1) * HEAD] = (summed / total).astype(jnp.bfloat16)

    branch = jnp.dot(attended_ref[...], out_weight_ref[...], preferred_element_type=jnp.float32).astype(jnp.bfloat16)
    for w, (rows, columns) in enumerate(parts):
        mine = slice(starts[w], starts[w] + counts[w])
        own = x_ref[w].astype(jnp.float32)[rows[0] : rows[1], columns[0] : columns[1]].reshape(counts[w], feature)
        out_ref[mine, :] = (own + branch[mine].astype(jnp.float32)).astype(jnp.bfloat16)


def attend(windows, labels, bias, qkv_weight, out_weight, parts):
    feature = windows[0].shape[-1]
    x = jnp.stack(windows)
    labels = jnp.pad(jnp.stack(labels), ((0, 8 - len(labels)), (0, 0)))
    sizes = [(r[1] - r[0], c[1] - c[0]) for r, c in parts]
    total = sum(r * c for r, c in sizes)
    flops = 2 * feature * feature * (2 * len(parts) * WIN + 2 * total) + 4 * total * WIN * feature
    updated = pl.pallas_call(
        functools.partial(window_kernel, parts),
        out_shape=jax.ShapeDtypeStruct((total, feature), jnp.bfloat16),
        in_specs=[VMEM] * 5,
        out_specs=VMEM,
        scratch_shapes=[
            pltpu.VMEM((len(parts) * WIN, feature), jnp.bfloat16),
            pltpu.VMEM((total, feature), jnp.bfloat16),
            pltpu.VMEM((total, feature), jnp.bfloat16),
        ],
        compiler_params=pltpu.CompilerParams(vmem_limit_bytes=VMEM_LIMIT),
        cost_estimate=pl.CostEstimate(flops=flops, bytes_accessed=10**6, transcendentals=total * WIN * HEADS),
    )(x, labels, bias, qkv_weight, out_weight)
    blocks, start = [], 0
    for r, c in sizes:
        blocks.append(updated[start : start + r * c].reshape(r, c, feature))
        start += r * c
    return blocks


def shards(tokens, qkv_weight, out_weight, bias_table, position_index, region_label):
    row_count, column_count, feature = tokens.shape
    bands, strips = row_count // WLAT, column_count // WLON
    lat_rows = [(row_count - HALF_LAT, row_count), (0, HALF_LAT)]
    label_windows = region_label.reshape(bands, WLAT, strips, WLON).transpose(0, 2, 1, 3).reshape(bands, strips, WIN)

    first, last = tokens[:HALF_LAT], tokens[-HALF_LAT:]
    ends = lambda block: jnp.concatenate([block[:, :HALF_LON], block[:, -HALF_LON:]], axis=1)
    above_ends, below_ends = lat_halo(ends(first), ends(last))
    above, below = lat_halo(first[:, HALF_LON:-HALF_LON], last[:, HALF_LON:-HALF_LON])
    label_above = moved(label_windows[-1:], "lat", 1)
    labels = jnp.concatenate([label_above, label_windows], axis=0)

    column = lambda part: jnp.concatenate([above_ends[:, part], tokens[:, part], below_ends[:, part]], axis=0)
    own_left, own_right = column(slice(None, HALF_LON)), column(slice(-HALF_LON, None))
    from_left = moved(own_right, "lon", 1)
    from_right = moved(own_left, "lon", -1)
    label_left = moved(labels[:, -1:], "lon", 1)
    labels = jnp.concatenate([label_left, labels], axis=1)

    bias = bias_lookup(bias_table, position_index)
    call = functools.partial(attend, bias=bias, qkv_weight=qkv_weight, out_weight=out_weight)

    inner_rows = [slice(HALF_LAT + b * WLAT, HALF_LAT + (b + 1) * WLAT) for b in range(bands - 1)]
    inner_columns = [slice(HALF_LON + s * WLON, HALF_LON + (s + 1) * WLON) for s in range(strips - 1)]
    grid = {}

    def work(places):
        windows, names, parts = [], [], []
        for b, s in places:
            rows = TOP if b == 0 else BOTTOM if b == bands else MIDDLE
            columns = LEFT if s == 0 else RIGHT if s == strips else INNER
            if s in (0, strips):
                block = jnp.concatenate([from_left, own_left] if s == 0 else [own_right, from_right], axis=1)
                window = block[b * WLAT : (b + 1) * WLAT]
            elif b in (0, bands):
                part = inner_columns[s - 1]
                halo = slice((s - 1) * WLON, s * WLON)
                pieces = [above[:, halo], first[:, part]] if b == 0 else [last[:, part], below[:, halo]]
                window = jnp.concatenate(pieces, axis=0)
            else:
                window = tokens[inner_rows[b - 1], inner_columns[s - 1]]
            windows.append(window)
            names.append(labels[b, s])
            parts.append((rows, columns))
        for place, block in zip(places, call(windows, names, parts=tuple(parts))):
            grid[place] = block

    for b in range(1, bands):
        work([(b, s) for s in range(1, strips)])
    work([(b, s) for b in range(bands + 1) for s in (0, strips)])
    work([(b, s) for b in (0, bands) for s in range(1, strips)])
    return jnp.concatenate(
        [jnp.concatenate([grid[b, s] for s in range(strips + 1)], axis=1) for b in range(bands + 1)], axis=0
    )


def solution(mesh):
    in_specs = (P("lat", "lon", None), P(), P(), P(), P(), P("lat", "lon"))
    out_specs = P("lat", "lon", None)
    return jax.shard_map(shards, mesh=mesh, in_specs=in_specs, out_specs=out_specs, check_vma=False)
```

time: 114 us -> 63.1 us (0.55)
  matrix products: 41 us -> 0 us
  Pallas kernels: 0 us -> 29 us
  local copies, waits for them, and re-layouts: 39.6 us -> 15 us
  waiting for transfers between devices: 15.8 us -> 6.56 us
  other arithmetic: 8.42 us -> 4.23 us
    dot_general x11 -> x0, matrix products: 33.7 us -> none  [the longest x8 22.7 us: one_block(): lax.dot_general(bias_table, onehot, (((0,), (1,)), ((), ())), precision=l...]
    pallas_call x0 -> x4, Pallas kernels: none -> 29 us  [the longest x3 28.5 us: attend(): pl.pallas_call(functools.partial(window_kernel, parts), out_shape=jax.Sha...]
    reshape x6 -> x2, local copies, waits for them, and re-layouts: 10.1 us -> 0.86 us  [shards(): region_label.reshape(bands, WLAT, strips, WLON).transpose(0, 2, 1, 3)]
    ppermute x4 -> x6, waiting for transfers between devices: 15.8 us -> 6.56 us  [moved(): return lax.ppermute(block, axis, route)]
    sub x1 -> x0, matrix products: 7.37 us -> none  [attend(): numerators = jnp.exp(jnp.where(matching, scores - largest, -jnp.inf))]
    dynamic_slice x8 -> x0, local copies, waits for them, and re-layouts: 6.78 us -> none  [bias_lookup(): looked = lax.map(one_block, blocks)]
    slice x8 -> x11, local copies, waits for them, and re-layouts: 12 us -> 7.25 us  [the longest x1 1.26 us: work(): below[:, halo]]
    unnamed x12 -> x45, local copies, waits for them, and re-layouts: 0.28 us -> 4.72 us
  transfers between devices with their start and end apart: 4 -> 6, of which waited for: 3 -> 2; matrix products, arithmetic and copies ran while one was open for 38% -> 17% of each run, Pallas kernels for 0% -> 28%
where the time goes in v1:
time: 63.1 us; the launch traced here: 62.6 us
  Pallas kernels  29 us (46%)
  local copies, waits for them, and re-layouts  15 us (24%)
  starting transfers between devices  7.29 us (12%)
  waiting for transfers between devices  6.56 us (10%)
  other arithmetic  4.23 us (7%)
    pallas_call x3, Pallas kernels, attend(): pl.pallas_call(functools.partial(window_kernel, parts), out_shape=jax.Sha...  28.5 us
    ppermute x6, starting transfers between devices, moved(): return lax.ppermute(block, axis, route)  7.29 us
    ppermute x6, waiting for transfers between devices, moved(): return lax.ppermute(block, axis, route)  6.56 us
    unnamed x45, local copies, waits for them, and re-layouts  4.72 us
    concatenate x2, other arithmetic, lat_halo(): both = moved(jnp.concatenate([last, first], axis=0), 'lat', 1)  1.56 us
    another operation x5, local copies, waits for them, and re-layouts, attend(): labels = jnp.pad(jnp.stack(labels), ((0, 8 - len(labels)), (0, 0)))  1.34 us
    concatenate x1, other arithmetic, shards(): jnp.concatenate([jnp.concatenate([grid[b, s] for s in range(strips + 1)],...  1.32 us
  transfers between devices with their start and end apart: 6, of which 2 were waited for; matrix products, arithmetic and copies ran while one was open for 17% of the time, Pallas kernels for 28%

profile of v1, /device:TPU:0, one launch (start us, length us, event | category | flops | bytes accessed | tf_op | source)
XLA Modules:
  0.0 62.6 jit_solution(8303050737786754634)
XLA Ops:
  0.0 0.9 %fusion.17 = (bf16[4,8,768]{2,1,0:T(8,128)(2,1)S(1)}, bf16[4,8,768]{2,1,0:T(8,128)(2,1)S(1)}, bf16[4,8,768]{2,1,0:T(8,128)(2,1)S(1)}, bf16[4,8,768]{2,1,0:T(8,128)(2,1)S(1)}) fusion(bf16[16,64,768]{2,1,0:T(8,128)(2,1)} %param.6), kind=kLoop, calls=%fused_computation.76 | loop fusion | bytes 393216 | tf_op jit(solution)/shard_map/slice | solution.py:158
  0.9 0.7 %maximum_maximum_fusion.1 = bf16[8,16,768]{2,1,0:T(8,128)(2,1)} fusion(bf16[4,8,768]{2,1,0:T(8,128)(2,1)S(1)} %get-tuple-element.19, bf16[4,8,768]{2,1,0:T(8,128)(2,1)S(1)} %get-tuple-element.20, bf16[4,8,768]{2,1,0:T(8,128)(2,1)S(1)} %get-tuple-element.21, bf16[4,8,768]{2,1,0:T(8,128)(2,1)S(1)} %get-tuple-element.18), kind=kLoop, calls=%fused_computation.19 | loop fusion | flops 786432 | bytes 393216 | tf_op jit(solution)/shard_map/concatenate | solution.py:35
  1.6 3.0 %collective-permute-start = (bf16[8,16,768]{2,1,0:T(8,128)(2,1)}, bf16[8,16,768]{2,1,0:T(8,128)(2,1)}, u32[]{:S(2)}, u32[]{:S(2)}) collective-permute-start(bf16[8,16,768]{2,1,0:T(8,128)(2,1)} %maximum_maximum_fusion.1), channel_id=1, source_target_pairs={{1,0},{0,1},{3,2},{2,3},{5,4},{4,5},{7,6},{6,7},{9,8},{8,9},{11,10... | collective-permute-start | bytes 589832 | tf_op jit(solution)/shard_map/ppermute | solution.py:30
  4.5 0.8 %reshape.52 = s32[2,8,4,16]{3,2,1,0:T(4,128)S(1)} reshape(s32[16,64]{1,0:T(8,128)} %param.11) | data formatting | bytes 8192 | tf_op jit(solution)/shard_map/reshape | solution.py:155
  5.3 0.7 %slice.243 = s32[1,4,128]{2,1,0:T(4,128)} reshape(s32[1,4,8,16]{3,2,1,0:T(8,128)S(1)} %copy.7) | data formatting | bytes 4096 | tf_op jit(solution)/shard_map/slice | solution.py:161
  6.0 0.0 copy-start.4
  6.0 0.0 collective-permute-start.3
  6.0 1.2 %fusion.15 = (bf16[4,48,768]{2,1,0:T(8,128)(2,1)S(1)}, bf16[4,48,768]{2,1,0:T(8,128)(2,1)S(1)}) fusion(bf16[16,64,768]{2,1,0:T(8,128)(2,1)} %param.6), kind=kLoop, calls=%fused_computation.74 | loop fusion | bytes 1179648 | tf_op jit(solution)/shard_map/slice | solution.py:160
  7.2 0.9 %pad_maximum_fusion.2 = bf16[8,48,768]{2,1,0:T(8,128)(2,1)} fusion(bf16[4,48,768]{2,1,0:T(8,128)(2,1)S(1)} %get-tuple-element.15, bf16[4,48,768]{2,1,0:T(8,128)(2,1)S(1)} %get-tuple-element.14), kind=kLoop, calls=%fused_computation.3 | loop fusion | flops 294912 | bytes 1179648 | tf_op jit(solution)/shard_map/concatenate | solution.py:35
  8.1 1.9 %collective-permute-start.5 = (bf16[8,48,768]{2,1,0:T(8,128)(2,1)}, bf16[8,48,768]{2,1,0:T(8,128)(2,1)}, u32[]{:S(2)}, u32[]{:S(2)}) collective-permute-start(bf16[8,48,768]{2,1,0:T(8,128)(2,1)} %pad_maximum_fusion.2), channel_id=1, source_target_pairs={{1,0},{0,1},{3,2},{2,3},{5,4},{4,5},{7,6},{6,7},{9,8},{8,9},{11,10... | collective-permute-start | bytes 1769480 | tf_op jit(solution)/shard_map/ppermute | solution.py:30
  10.0 0.0 copy-done.4
  10.0 0.0 copy-start.14
  10.0 0.0 copy-start
  10.0 0.8 %fusion.14 = (bf16[4,16,768]{2,1,0:T(8,128)(2,1)}, bf16[4,16,768]{2,1,0:T(8,128)(2,1)}, bf16[4,16,768]{2,1,0:T(8,128)(2,1)}, bf16[4,16,768]{2,1,0:T(8,128)(2,1)}...) fusion(bf16[16,64,768]{2,1,0:T(8,128)(2,1)S(1)} %copy-done.4), kind=kLoop, calls=%fused_computation.73 | loop fusion | bytes 1179648 | tf_op jit(solution)/shard_map/slice | solution.py:189
  10.8 0.0 copy-start.3
  10.8 0.8 %slice_bitcast_fusion.8 = (bf16[1,8,16,768]{3,2,1,0:T(8,128)(2,1)S(1)}, bf16[1,8,16,768]{3,2,1,0:T(8,128)(2,1)}, bf16[1,8,16,768]{3,2,1,0:T(8,128)(2,1)}) fusion(bf16[16,64,768]{2,1,0:T(8,128)(2,1)S(1)} %copy-done.4), kind=kLoop, calls=%fused_computation.34 | loop fusion | bytes 1179648 | tf_op jit(solution)/shard_map/stack | solution.py:126
  11.6 0.1 reshape.53
  11.7 0.6 slice_bitcast_fusion.17
  12.3 0.0 copy-done.14
  12.3 0.0 copy-done
  12.3 0.5 shard_map.64.bias_ref
  12.9 1.1 %pad_maximum_fusion.3.x_ref = bf16[3,8,16,768]{3,2,1,0:T(8,128)(2,1)S(1)} fusion(bf16[1,8,16,768]{3,2,1,0:T(8,128)(2,1)} %get-tuple-element.6, bf16[1,8,16,768]{3,2,1,0:T(8,128)(2,1)} %get-tuple-element.7, bf16[1,8,16,768]{3,2,1,0:T(8,128)(2,1)S(1)} %get-tuple-element.5), kind=kLoop, calls=%fused_computation.4 | loop fusion | flops 589824 | bytes 1179648 | tf_op jit(solution)/shard_map/stack | solution.py:126
  14.0 0.0 copy-done.3
  14.0 0.0 copy-start.1
  14.0 2.0 %copy-done.1 = bf16[768,2304]{1,0:T(8,128)(2,1)S(1)} copy-done((bf16[768,2304]{1,0:T(8,128)(2,1)S(1)}, bf16[768,2304]{1,0:T(8,128)(2,1)}, u32[]{:S(2)}) %copy-start.1) | copy-done | bytes 3538968
  16.0 6.5 %shard_map.67 = bf16[384,768]{1,0:T(8,128)(2,1)S(1)} custom-call(bf16[3,8,16,768]{3,2,1,0:T(8,128)(2,1)S(1)} %pad_maximum_fusion.3.x_ref, s32[8,128]{1,0:T(8,128)S(1)} %pad.18.label_ref, f32[6,128,128]{2,1,0:T(8,128)S(1)} %shard_map.64.bias_ref, bf16[768,2304]{1,0:T(8,128)(2,1)S(1)} %copy-done.1, bf16[768,768]{1,0:T(8,128)(2,1)S(1)} %copy-done.3), custom_call_target="tpu_custom_call" | custom-call | flops 1962934272 | bytes 1000000 | tf_op jit(solution)/shard_map/pallas_call | solution.py:131
  22.5 0.8 %fusion.19 = (bf16[128,768]{1,0:T(8,128)(2,1)S(1)}, bf16[128,768]{1,0:T(8,128)(2,1)}, bf16[128,768]{1,0:T(8,128)(2,1)}) fusion(bf16[384,768]{1,0:T(8,128)(2,1)S(1)} %shard_map.67), kind=kLoop, calls=%fused_computation.78 | loop fusion | bytes 1179648 | tf_op jit(solution)/shard_map/slice | solution.py:146
  23.2 0.7 %fusion.16 = (bf16[16,8,768]{2,1,0:T(8,128)(2,1)S(1)}, bf16[16,8,768]{2,1,0:T(8,128)(2,1)}) fusion(bf16[16,64,768]{2,1,0:T(8,128)(2,1)S(1)} %copy-done.4), kind=kLoop, calls=%fused_computation.75 | loop fusion | bytes 786432 | tf_op jit(solution)/shard_map/slice | solution.py:164
  23.9 0.0 copy-start.5
  23.9 0.0 collective-permute-done.3
  23.9 0.1 collective-permute-start.4
  24.0 0.7 %stack.78 = s32[6,128]{1,0:T(8,128)S(1)} concatenate(s32[1,128]{1,0:T(1,128)S(1)} %get-tuple-element.55, s32[1,128]{1,0:T(1,128)S(1)} %get-tuple-element.54, s32[1,128]{1,0:T(1,128)S(1)} %get-tuple-element.53, s32[1,128]{1,0:T(1,128)} %get-tuple-element.50, s32[1,128]{1,0:T(1,128)} %get-tuple-element.49, s32[1,128]{1,0:T(1,128)} %get-tuple-element.48), dimensions={0} | concatenate | bytes 6144 | tf_op jit(solution)/shard_map/stack | solution.py:127
  24.7 0.0 collective-permute-done
  24.7 0.9 %fusion.21 = (bf16[4,8,768]{2,1,0:T(8,128)(2,1)S(1)}, bf16[4,8,768]{2,1,0:T(8,128)(2,1)S(1)}, bf16[4,8,768]{2,1,0:T(8,128)(2,1)S(1)}, bf16[4,8,768]{2,1,0:T(8,128)(2,1)S(1)}) fusion(bf16[8,16,768]{2,1,0:T(8,128)(2,1)} %collective-permute-done), kind=kLoop, calls=%fused_computation.80 | loop fusion | bytes 393216 | tf_op jit(solution)/shard_map/slice | solution.py:164
  25.7 1.6 %collective-permute-start.1 = (bf16[24,8,768]{2,1,0:T(8,128)(2,1)S(1)}, bf16[24,8,768]{2,1,0:T(8,128)(2,1)S(1)}, u32[]{:S(2)}, u32[]{:S(2)}) collective-permute-start(bf16[24,8,768]{2,1,0:T(8,128)(2,1)S(1)} %pad_maximum_fusion.4), channel_id=1, source_target_pairs={{30,0},{0,2},{2,4},{4,6},{6,8},{8,10},{10,12},{12,14},{14,16},{16,... | collective-permute-start | bytes 884744 | tf_op jit(solution)/shard_map/ppermute | solution.py:30
  27.3 2.4 %collective-permute-done.4 = s32[3,1,128]{2,1,0:T(1,128)S(1)} collective-permute-done((s32[3,1,128]{2,1,0:T(1,128)S(1)}, s32[3,1,128]{2,1,0:T(1,128)S(1)}, u32[]{:S(2)}, u32[]{:S(2)}) %collective-permute-start.4) | collective-permute-done | bytes 1568 | tf_op jit(solution)/shard_map/ppermute | solution.py:30
  29.7 0.0 copy-done.5
  29.8 0.7 %collective-permute-start.2 = (bf16[24,8,768]{2,1,0:T(8,128)(2,1)S(1)}, bf16[24,8,768]{2,1,0:T(8,128)(2,1)S(1)}, u32[]{:S(2)}, u32[]{:S(2)}) collective-permute-start(bf16[24,8,768]{2,1,0:T(8,128)(2,1)S(1)} %pad_maximum_fusion.5), channel_id=1, source_target_pairs={{2,0},{4,2},{6,4},{8,6},{10,8},{12,10},{14,12},{16,14},{18,16},{20... | collective-permute-start | bytes 884744 | tf_op jit(solution)/shard_map/ppermute | solution.py:30
  30.5 4.2 %collective-permute-done.1 = bf16[24,8,768]{2,1,0:T(8,128)(2,1)S(1)} collective-permute-done((bf16[24,8,768]{2,1,0:T(8,128)(2,1)S(1)}, bf16[24,8,768]{2,1,0:T(8,128)(2,1)S(1)}, u32[]{:S(2)}, u32[]{:S(2)}) %collective-permute-start.1) | collective-permute-done | bytes 294944 | tf_op jit(solution)/shard_map/ppermute | solution.py:30
  34.7 0.0 copy-start.2
  34.8 0.0 collective-permute-done.2
  34.9 1.8 %copy-done.2 = bf16[768,2304]{1,0:T(8,128)(2,1)S(1)} copy-done((bf16[768,2304]{1,0:T(8,128)(2,1)S(1)}, bf16[768,2304]{1,0:T(8,128)(2,1)}, u32[]{:S(2)}) %copy-start.2) | copy-done | bytes 3538968
  36.7 0.0 copy-start.7
  36.7 0.0 copy-start.6
  36.7 10.8 %shard_map.65 = bf16[256,768]{1,0:T(8,128)(2,1)S(1)} custom-call(bf16[6,8,16,768]{3,2,1,0:T(8,128)(2,1)S(1)} %fusion.x_ref, s32[8,128]{1,0:T(8,128)S(1)} %pad.15.label_ref, f32[6,128,128]{2,1,0:T(8,128)S(1)} %shard_map.64.bias_ref, bf16[768,2304]{1,0:T(8,128)(2,1)S(1)} %copy-done.2, bf16[768,768]{1,0:T(8,128)(2,1)S(1)} %copy-done.3), custom_call_target="tpu_custom_call" | custom-call | flops 2516582400 | bytes 1000000 | tf_op jit(solution)/shard_map/pallas_call | solution.py:131
  47.5 0.0 copy-done.7
  47.5 0.0 copy-done.6
  47.5 0.0 copy-start.13
  47.6 0.0 copy-start.12
  47.6 0.0 copy-start.11
  47.6 0.0 copy-start.10
  47.6 0.0 copy-start.9
  47.6 0.0 collective-permute-done.5
  47.7 1.3 %fusion.20 = (bf16[4,16,768]{2,1,0:T(8,128)(2,1)S(1)}, bf16[4,16,768]{2,1,0:T(8,128)(2,1)S(1)}, bf16[4,16,768]{2,1,0:T(8,128)(2,1)S(1)}, bf16[4,16,768]{2,1,0:T(...) fusion(bf16[8,48,768]{2,1,0:T(8,128)(2,1)} %collective-permute-done.5), kind=kLoop, calls=%fused_computation.79 | loop fusion | bytes 1179648 | tf_op jit(solution)/shard_map/slice | solution.py:189
  48.9 0.0 copy-start.8
  48.9 0.0 copy-done.13
  49.0 0.0 copy-done.12
  49.0 0.0 copy-done.11
  49.0 0.0 copy-done.10
  49.1 0.0 copy-done.9
  49.1 0.7 %copy-done.8 = bf16[4,16,768]{2,1,0:T(8,128)(2,1)S(1)} copy-done((bf16[4,16,768]{2,1,0:T(8,128)(2,1)S(1)}, bf16[4,16,768]{2,1,0:T(8,128)(2,1)}, u32[]{:S(2)}) %copy-start.8) | copy-done | bytes 98328
  49.8 11.3 %shard_map.66 = bf16[384,768]{1,0:T(8,128)(2,1)S(1)} custom-call(bf16[6,8,16,768]{3,2,1,0:T(8,128)(2,1)S(1)} %fusion.11.x_ref, s32[8,128]{1,0:T(8,128)S(1)} %pad.17.label_ref, f32[6,128,128]{2,1,0:T(8,128)S(1)} %shard_map.64.bias_ref, bf16[768,2304]{1,0:T(8,128)(2,1)S(1)} %copy-done.2, bf16[768,768]{1,0:T(8,128)(2,1)S(1)} %copy-done.3), custom_call_target="tpu_custom_call" | custom-call | flops 2868903936 | bytes 1000000 | tf_op jit(solution)/shard_map/pallas_call | solution.py:131
  61.3 1.3 %pad_maximum_fusion = bf16[16,64,768]{2,1,0:T(8,128)(2,1)} fusion(bf16[4,64,768]{2,1,0:T(8,128)(2,1)S(1)} %get-tuple-element.38, bf16[8,64,768]{2,1,0:T(8,128)(2,1)S(1)} %fusion.12, bf16[4,64,768]{2,1,0:T(8,128)(2,1)S(1)} %get-tuple-element.37), kind=kLoop, calls=%fused_computation | loop fusion | flops 1572864 | bytes 3145728 | tf_op jit(solution)/shard_map/concatenate | solution.py:203
  (41 shorter events, 0.6 us)
Async XLA Ops:
  1.6 23.2 %collective-permute-start = (bf16[8,16,768]{2,1,0:T(8,128)(2,1)}, bf16[8,16,768]{2,1,0:T(8,128)(2,1)}, u32[]{:S(2)}, u32[]{:S(2)}) collective-permute-start(bf16[8,16,768]{2,1,0:T(8,128)(2,1)} %maximum_maximum_fusion.1), channel_id=1, source_target_pairs={{1,0},{0,1},{3,2},{2,3},{5,4},{4,5},{7,6},{6,7},{9,8},{8,9},{11,10... | collective-permute-start | bytes 589832 | tf_op jit(solution)/shard_map/ppermute | solution.py:30
  6.0 4.0 %copy-start.4 = (bf16[16,64,768]{2,1,0:T(8,128)(2,1)S(1)}, bf16[16,64,768]{2,1,0:T(8,128)(2,1)}, u32[]{:S(2)}) copy-start(bf16[16,64,768]{2,1,0:T(8,128)(2,1)} %param.6) | copy-start | bytes 4718596
  6.0 17.9 %collective-permute-start.3 = (s32[1,4,128]{2,1,0:T(4,128)}, s32[1,4,128]{2,1,0:T(4,128)S(1)}, u32[]{:S(2)}, u32[]{:S(2)}) collective-permute-start(s32[1,4,128]{2,1,0:T(4,128)} %slice.243), channel_id=1, source_target_pairs={{1,0},{0,1},{3,2},{2,3},{5,4},{4,5},{7,6},{6,7},{9,8},{8,9},{11,10... | collective-permute-start | bytes 6152 | tf_op jit(solution)/shard_map/ppermute | solution.py:30
  8.1 39.6 %collective-permute-start.5 = (bf16[8,48,768]{2,1,0:T(8,128)(2,1)}, bf16[8,48,768]{2,1,0:T(8,128)(2,1)}, u32[]{:S(2)}, u32[]{:S(2)}) collective-permute-start(bf16[8,48,768]{2,1,0:T(8,128)(2,1)} %pad_maximum_fusion.2), channel_id=1, source_target_pairs={{1,0},{0,1},{3,2},{2,3},{5,4},{4,5},{7,6},{6,7},{9,8},{8,9},{11,10... | collective-permute-start | bytes 1769480 | tf_op jit(solution)/shard_map/ppermute | solution.py:30
  10.0 2.3 %copy-start.14 = (f32[465,6]{0,1:T(8,128)S(1)}, f32[465,6]{0,1:T(8,128)}, u32[]{:S(2)}) copy-start(f32[465,6]{0,1:T(8,128)} %param.9) | copy-start | bytes 33484
  10.0 2.3 %copy-start = (s32[128,128]{1,0:T(8,128)S(1)}, s32[128,128]{1,0:T(8,128)}, u32[]{:S(2)}) copy-start(s32[128,128]{1,0:T(8,128)} %index_ref.1) | copy-start | bytes 196612
  10.8 3.1 %copy-start.3 = (bf16[768,768]{1,0:T(8,128)(2,1)S(1)}, bf16[768,768]{1,0:T(8,128)(2,1)}, u32[]{:S(2)}) copy-start(bf16[768,768]{1,0:T(8,128)(2,1)} %out_weight_ref.5) | copy-start | bytes 3538948
  14.0 2.0 %copy-start.1 = (bf16[768,2304]{1,0:T(8,128)(2,1)S(1)}, bf16[768,2304]{1,0:T(8,128)(2,1)}, u32[]{:S(2)}) copy-start(bf16[768,2304]{1,0:T(8,128)(2,1)} %qkv_weight_ref.5) | copy-start | bytes 10616836
  23.9 5.8 %copy-start.5 = (bf16[16,8,768]{2,1,0:T(8,128)(2,1)S(1)}, bf16[16,8,768]{2,1,0:T(8,128)(2,1)}, u32[]{:S(2)}) copy-start(bf16[16,8,768]{2,1,0:T(8,128)(2,1)} %get-tuple-element.17) | copy-start | bytes 589828
  23.9 5.8 %collective-permute-start.4 = (s32[3,1,128]{2,1,0:T(1,128)S(1)}, s32[3,1,128]{2,1,0:T(1,128)S(1)}, u32[]{:S(2)}, u32[]{:S(2)}) collective-permute-start(s32[3,1,128]{2,1,0:T(1,128)S(1)} %pad_add_fusion.1), channel_id=1, source_target_pairs={{30,0},{0,2},{2,4},{4,6},{6,8},{8,10},{10,12},{12,14},{14,16},{16,... | collective-permute-start | bytes 4616 | tf_op jit(solution)/shard_map/ppermute | solution.py:30
  25.7 9.0 %collective-permute-start.1 = (bf16[24,8,768]{2,1,0:T(8,128)(2,1)S(1)}, bf16[24,8,768]{2,1,0:T(8,128)(2,1)S(1)}, u32[]{:S(2)}, u32[]{:S(2)}) collective-permute-start(bf16[24,8,768]{2,1,0:T(8,128)(2,1)S(1)} %pad_maximum_fusion.4), channel_id=1, source_target_pairs={{30,0},{0,2},{2,4},{4,6},{6,8},{8,10},{10,12},{12,14},{14,16},{16,... | collective-permute-start | bytes 884744 | tf_op jit(solution)/shard_map/ppermute | solution.py:30
  29.8 5.0 %collective-permute-start.2 = (bf16[24,8,768]{2,1,0:T(8,128)(2,1)S(1)}, bf16[24,8,768]{2,1,0:T(8,128)(2,1)S(1)}, u32[]{:S(2)}, u32[]{:S(2)}) collective-permute-start(bf16[24,8,768]{2,1,0:T(8,128)(2,1)S(1)} %pad_maximum_fusion.5), channel_id=1, source_target_pairs={{2,0},{4,2},{6,4},{8,6},{10,8},{12,10},{14,12},{16,14},{18,16},{20... | collective-permute-start | bytes 884744 | tf_op jit(solution)/shard_map/ppermute | solution.py:30
  34.7 2.0 %copy-start.2 = (bf16[768,2304]{1,0:T(8,128)(2,1)S(1)}, bf16[768,2304]{1,0:T(8,128)(2,1)}, u32[]{:S(2)}) copy-start(bf16[768,2304]{1,0:T(8,128)(2,1)} %qkv_weight_ref.5) | copy-start | bytes 10616836
  36.7 10.8 %copy-start.7 = (bf16[128,768]{1,0:T(8,128)(2,1)S(1)}, bf16[128,768]{1,0:T(8,128)(2,1)}, u32[]{:S(2)}) copy-start(bf16[128,768]{1,0:T(8,128)(2,1)} %get-tuple-element.30) | copy-start | bytes 589828
  36.7 10.8 %copy-start.6 = (bf16[128,768]{1,0:T(8,128)(2,1)S(1)}, bf16[128,768]{1,0:T(8,128)(2,1)}, u32[]{:S(2)}) copy-start(bf16[128,768]{1,0:T(8,128)(2,1)} %get-tuple-element.29) | copy-start | bytes 589828
  47.5 1.4 %copy-start.13 = (bf16[4,16,768]{2,1,0:T(8,128)(2,1)S(1)}, bf16[4,16,768]{2,1,0:T(8,128)(2,1)}, u32[]{:S(2)}) copy-start(bf16[4,16,768]{2,1,0:T(8,128)(2,1)} %get-tuple-element.13) | copy-start | bytes 294916
  47.6 1.4 %copy-start.12 = (bf16[4,16,768]{2,1,0:T(8,128)(2,1)S(1)}, bf16[4,16,768]{2,1,0:T(8,128)(2,1)}, u32[]{:S(2)}) copy-start(bf16[4,16,768]{2,1,0:T(8,128)(2,1)} %get-tuple-element.12) | copy-start | bytes 294916
  47.6 1.4 %copy-start.11 = (bf16[4,16,768]{2,1,0:T(8,128)(2,1)S(1)}, bf16[4,16,768]{2,1,0:T(8,128)(2,1)}, u32[]{:S(2)}) copy-start(bf16[4,16,768]{2,1,0:T(8,128)(2,1)} %get-tuple-element.11) | copy-start | bytes 294916
  47.6 1.4 %copy-start.10 = (bf16[4,16,768]{2,1,0:T(8,128)(2,1)S(1)}, bf16[4,16,768]{2,1,0:T(8,128)(2,1)}, u32[]{:S(2)}) copy-start(bf16[4,16,768]{2,1,0:T(8,128)(2,1)} %get-tuple-element.10) | copy-start | bytes 294916
  47.6 1.4 %copy-start.9 = (bf16[4,16,768]{2,1,0:T(8,128)(2,1)S(1)}, bf16[4,16,768]{2,1,0:T(8,128)(2,1)}, u32[]{:S(2)}) copy-start(bf16[4,16,768]{2,1,0:T(8,128)(2,1)} %get-tuple-element.9) | copy-start | bytes 294916
  48.9 0.9 %copy-start.8 = (bf16[4,16,768]{2,1,0:T(8,128)(2,1)S(1)}, bf16[4,16,768]{2,1,0:T(8,128)(2,1)}, u32[]{:S(2)}) copy-start(bf16[4,16,768]{2,1,0:T(8,128)(2,1)} %get-tuple-element.8) | copy-start | bytes 294916

commit v2 on v0

v2 whole, which is shorter than its diff:
```python
import functools

import jax
import jax.numpy as jnp
from jax import lax
from jax.experimental import pallas as pl
from jax.experimental.pallas import tpu as pltpu
from jax.sharding import PartitionSpec as P

HEADS = 6
HEAD = 128
WLAT = 8
WLON = 16
WIN = WLAT * WLON
HALF_LAT = WLAT // 2
HALF_LON = WLON // 2
LOG2E = 1.4426950408889634
SCALE = LOG2E / HEAD**0.5
EXCLUDED = -1e30
VMEM_LIMIT = 24 * 2**20
VMEM = pl.BlockSpec(memory_space=pltpu.VMEM)
HBM = pl.BlockSpec(memory_space=pl.ANY)
F32 = jnp.float32
BF16 = jnp.bfloat16


def moved(block, axis, distance):
    count = lax.axis_size(axis)
    route = [((i - distance) % count, i) for i in range(count)]
    return lax.ppermute(block, axis, route)


def lat_exchange(message):
    if lax.axis_size("lat") == 2:
        return moved(message, "lat", 1)
    return jnp.concatenate([moved(message[:HALF_LAT], "lat", -1), moved(message[HALF_LAT:], "lat", 1)], axis=0)


def run(kernel, outs, operands, flops=10**6, exponentials=0, scratch=(), specs=None, out_specs=None, aliases=None, side=False):
    return pl.pallas_call(
        kernel,
        out_shape=outs,
        in_specs=specs or [VMEM] * len(operands),
        out_specs=out_specs or [VMEM] * len(outs),
        scratch_shapes=scratch,
        input_output_aliases=aliases or {},
        compiler_params=pltpu.CompilerParams(vmem_limit_bytes=VMEM_LIMIT),
        cost_estimate=pl.CostEstimate(flops=flops, bytes_accessed=10**6, transcendentals=exponentials),
    )(*operands)


def shape(*extent, dtype=BF16):
    return jax.ShapeDtypeStruct(extent, dtype)


def normalize(floats):
    floats = floats - jnp.mean(floats, axis=-1, keepdims=True)
    return floats * lax.rsqrt(jnp.mean(jnp.square(floats), axis=-1, keepdims=True) + 1e-05)


def label_rows(labels, strips):
    rows, columns = labels.shape
    labels = labels.astype(BF16)
    source = lax.broadcasted_iota(jnp.int32, (columns, WIN), 0)
    cell = lax.broadcasted_iota(jnp.int32, (columns, WIN), 1)
    at_row = lax.broadcasted_iota(jnp.int32, (rows, WIN), 0) % WLAT == lax.broadcasted_iota(jnp.int32, (rows, WIN), 1) // WLON
    place = lax.broadcasted_iota(jnp.int32, (rows // WLAT * strips, WIN), 0)
    result = jnp.zeros((rows // WLAT * strips, WIN), F32)
    for strip in range(strips):
        spread = jnp.dot(labels, (source == strip * WLON + cell % WLON).astype(BF16), preferred_element_type=F32)
        spread = jnp.where(at_row, spread, 0.0)
        for band in range(rows // WLAT):
            row = jnp.sum(spread[band * WLAT : (band + 1) * WLAT], axis=0, keepdims=True)
            result = jnp.where(place == band * strips + strip, row, result)
    return result


def message_kernel(strips, tokens_ref, label_ref, ends_ref, inner_ref, rows_ref, edge_ref, sems):
    row_count, column_count, feature = tokens_ref.shape
    copies = [
        pltpu.make_async_copy(tokens_ref.at[pl.ds(0, HALF_LAT)], edge_ref.at[pl.ds(0, HALF_LAT)], sems.at[0]),
        pltpu.make_async_copy(tokens_ref.at[pl.ds(row_count - HALF_LAT, HALF_LAT)], edge_ref.at[pl.ds(HALF_LAT, HALF_LAT)], sems.at[1]),
    ]
    for copy in copies:
        copy.start()
    rows = label_rows(label_ref[...], strips)
    rows_ref[...] = rows
    padded = jnp.concatenate([rows, jnp.zeros((2 * HALF_LON - rows.shape[0], WIN), F32)], axis=0)
    ends_ref[WLAT] = jnp.concatenate([padded, jnp.zeros((2 * HALF_LON, feature - WIN), F32)], axis=1).astype(BF16)
    for copy in copies:
        copy.wait()
    for row in range(WLAT):
        floats = edge_ref[row].astype(F32)
        ends_ref[row] = jnp.concatenate([floats[:HALF_LON], floats[-HALF_LON:]], axis=0).astype(BF16)
        inner_ref[row] = floats[HALF_LON:-HALF_LON].astype(BF16)


def bias_kernel(table_ref, index_ref, out_ref):
    table = table_ref[...]
    for row in range(0, WIN, 8):
        index = index_ref[row : row + 8, :]
        low, high = index & 127, index >> 7
        for head in range(HEADS):
            value = jnp.zeros((8, WIN), F32)
            for part in range(4):
                source = jnp.broadcast_to(table[head : head + 1, part * 128 : part * 128 + 128], (8, 128))
                value = jnp.where(high == part, jnp.take_along_axis(source, low, axis=1), value)
            out_ref[head, row : row + 8, :] = value * LOG2E


def column_kernel(strips, tokens_ref, ends_ref, rows_ref, left_ref, right_ref, labels_ref):
    row_count, column_count, feature = tokens_ref.shape
    for row in range(row_count + WLAT):
        if row < HALF_LAT or row >= row_count + HALF_LAT:
            floats = ends_ref[(row + HALF_LAT) if row < HALF_LAT else row - row_count - HALF_LAT].astype(F32)
            left, right = floats[:HALF_LON], floats[HALF_LON:]
        else:
            left = tokens_ref[row - HALF_LAT, :WLON, :].astype(F32)[:HALF_LON]
            right = tokens_ref[row - HALF_LAT, column_count - WLON :, :].astype(F32)[HALF_LON:]
        left_ref[row] = left.astype(BF16)
        right_ref[row] = right.astype(BF16)
    own = rows_ref[...]
    above = ends_ref[WLAT].astype(F32)[own.shape[0] - strips : own.shape[0], :WIN]
    labels = jnp.concatenate([above, own, jnp.zeros((16 - strips - own.shape[0], WIN), F32)], axis=0)
    labels_ref[...] = labels
    filler = jnp.zeros((HALF_LON, feature - 2 * WIN), F32)
    right_ref[row_count + WLAT] = jnp.concatenate([labels[:8], labels[8:], filler], axis=1).astype(BF16)


def excluded(columns, row):
    return jnp.where(columns == row, 0.0, EXCLUDED)


def attention(entries):
    scores = []
    for queries, keys, _, bias, _ in entries:
        product = lax.dot_general(queries(), keys(), (((1,), (1,)), ((), ())), preferred_element_type=F32)
        scores.append(product * SCALE + bias())
    numerators = [jnp.exp2(score - jnp.max(score, axis=-1, keepdims=True)) for score in scores]
    for (_, _, values, _, store), numerator in zip(entries, numerators):
        total = jnp.sum(numerator, axis=-1, keepdims=True)
        summed = jnp.dot(numerator.astype(BF16), values(), preferred_element_type=F32)
        store((summed * (1.0 / total)).astype(BF16))


def project(source, weight_ref, first, count):
    return jnp.dot(source, weight_ref[:, first : first + count], preferred_element_type=F32).astype(BF16)


def out_project(attended_ref, weight_ref):
    return jnp.dot(attended_ref[...], weight_ref[...], preferred_element_type=F32).astype(BF16).astype(F32)


def lanes(head):
    return slice(head * HEAD, (head + 1) * HEAD)


def storer(ref, rows, head):
    def store(value):
        ref[rows, lanes(head)] = value

    return store


def inner_kernel(strips, tokens_ref, rows_ref, bias_ref, qkv_weight_ref, out_weight_ref, out_ref, cells_ref, qkv_ref, attended_ref):
    row_count, column_count, feature = tokens_ref.shape
    floats = []
    for strip in range(strips - 1):
        columns = slice(HALF_LON + strip * WLON, HALF_LON + (strip + 1) * WLON)
        window = tokens_ref[HALF_LAT : HALF_LAT + WLAT, :, :].astype(F32)[:, columns].reshape(WIN, feature)
        floats.append(window)
        cells_ref[strip * WIN : (strip + 1) * WIN, :] = normalize(window).astype(BF16)
    qkv_ref[...] = project(cells_ref[...], qkv_weight_ref, 0, 3 * feature)
    labels = rows_ref[...]
    label_columns = labels.T
    entries = []
    for strip in range(strips - 1):
        mine = slice(strip * WIN, (strip + 1) * WIN)
        mask = excluded(label_columns[:, strip : strip + 1], labels[strip : strip + 1])
        for head in range(HEADS):
            entries.append(
                (
                    lambda mine=mine, head=head: qkv_ref[mine, lanes(head)],
                    lambda mine=mine, head=head: qkv_ref[mine, lanes(HEADS + head)],
                    lambda mine=mine, head=head: qkv_ref[mine, lanes(2 * HEADS + head)],
                    lambda mask=mask, head=head: bias_ref[head] + mask,
                    storer(attended_ref, mine, head),
                )
            )
    attention(entries)
    branch = out_project(attended_ref, out_weight_ref)
    for strip in range(strips - 1):
        mine = slice(strip * WIN, (strip + 1) * WIN)
        out_ref[mine, :] = (floats[strip] + branch[mine]).astype(BF16)


def rows_kernel(strips, tokens_ref, qkv_weight_ref, order_ref, out_ref, cells_ref):
    row_count, column_count, feature = tokens_ref.shape
    half = HALF_LAT * WLON
    for side, first in enumerate((0, row_count - HALF_LAT)):
        floats = tokens_ref[first : first + HALF_LAT, :, :].astype(F32)
        for strip in range(strips - 1):
            block = floats[:, HALF_LON + strip * WLON : HALF_LON + (strip + 1) * WLON].reshape(half, feature)
            start = (side * (strips - 1) + strip) * half
            cells_ref[start : start + half, :] = normalize(block).astype(BF16)
    out_ref[...] = project(cells_ref[...], qkv_weight_ref, 0, 3 * feature)


def side_kernel(strips, tokens_ref, from_left_ref, from_right_ref, ends_ref, labels_ref, bias_ref, qkv_weight_ref, out_weight_ref,
                inner_ref, out_ref, corner_ref, cells_ref, own_ref, queries_ref, keys_ref, attended_ref, block_ref, sem):
    row_count, column_count, feature = tokens_ref.shape
    bands = row_count // WLAT
    labels = labels_ref[...]
    received = from_left_ref[row_count + WLAT].astype(F32)
    label_columns = labels.T
    left_columns = (received[:, :WIN].T, received[:, WIN : 2 * WIN].T)
    windows = []
    start = 0
    for band in range(bands + 1):
        count = HALF_LON * (WLAT if 0 < band < bands else HALF_LAT)
        for side in range(2):
            windows.append((band, side, start, count))
            start += count
    tokens_of = {}
    for at, (band, side, start, count) in enumerate(windows):
        halo, own = [], []
        for row in range(band * WLAT, (band + 1) * WLAT):
            if row < HALF_LAT or row >= row_count + HALF_LAT:
                floats = ends_ref[(row + HALF_LAT) if row < HALF_LAT else row - row_count - HALF_LAT].astype(F32)
                own.append(floats[HALF_LON:] if side else floats[:HALF_LON])
            elif side:
                own.append(tokens_ref[row - HALF_LAT, column_count - WLON :, :].astype(F32)[HALF_LON:])
            else:
                own.append(tokens_ref[row - HALF_LAT, :WLON, :].astype(F32)[:HALF_LON])
            halo.append((from_right_ref if side else from_left_ref)[row].astype(F32))
        mine = slice(HALF_LAT if band == 0 else 0, HALF_LAT if band == bands else WLAT)
        tokens_of[band, side] = own[mine]
        own = normalize(jnp.stack(own))
        halo = normalize(jnp.stack(halo))
        window = jnp.concatenate([own, halo] if side else [halo, own], axis=1)
        cells_ref[at * WIN : (at + 1) * WIN, :] = window.reshape(WIN, feature).astype(BF16)
        own_ref[start : start + count, :] = own[mine].reshape(count, feature).astype(BF16)
    queries_ref[...] = project(own_ref[...], qkv_weight_ref, 0, feature)
    keys_ref[...] = project(cells_ref[...], qkv_weight_ref, feature, 2 * feature)

    def own_rows(array, band, side):
        array = array.reshape(WLAT, WLON, WIN)
        array = array[HALF_LAT if band == 0 else 0 : HALF_LAT if band == bands else WLAT]
        array = array[:, :HALF_LON] if side else array[:, HALF_LON:]
        return array.reshape(-1, WIN)

    entries = []
    for at, (band, side, start, count) in enumerate(windows):
        mine, whole = slice(start, start + count), slice(at * WIN, (at + 1) * WIN)
        place = band * strips + strips - 1
        if side:
            mask = excluded(label_columns[:, place : place + 1], labels[place : place + 1])
        else:
            group, place = divmod(place, 8)
            row = received[place : place + 1, group * WIN : (group + 1) * WIN]
            mask = excluded(left_columns[group][:, place : place + 1], row)
        mask = own_rows(mask, band, side)
        for head in range(HEADS):
            entries.append(
                (
                    lambda mine=mine, head=head: queries_ref[mine, lanes(head)],
                    lambda whole=whole, head=head: keys_ref[whole, lanes(head)],
                    lambda whole=whole, head=head: keys_ref[whole, lanes(HEADS + head)],
                    lambda mask=mask, head=head, band=band, side=side: own_rows(bias_ref[head], band, side) + mask,
                    storer(attended_ref, mine, head),
                )
            )
    attention(entries)
    branch = out_project(attended_ref, out_weight_ref)
    blocks = {}
    for band, side, start, count in windows:
        for row, own in enumerate(tokens_of[band, side]):
            at = start + row * HALF_LON
            blocks[band, side, row] = own + branch[at : at + HALF_LON]
    for row in range(WLAT):
        middle = [inner_ref[strip * WIN + row * WLON : strip * WIN + (row + 1) * WLON, :].astype(F32) for strip in range(strips - 1)]
        block_ref[row] = jnp.concatenate([blocks[1, 0, row]] + middle + [blocks[1, 1, row]], axis=0).astype(BF16)
    copy = pltpu.make_async_copy(block_ref, out_ref.at[pl.ds(HALF_LAT, WLAT)], sem)
    copy.start()
    for band, first in ((0, 0), (bands, HALF_LAT)):
        for row in range(HALF_LAT):
            corner_ref[first + row] = jnp.concatenate([blocks[band, 0, row], blocks[band, 1, row]], axis=0).astype(BF16)
    copy.wait()


def last_kernel(strips, tokens_ref, halo_ref, own_ref, labels_ref, bias_ref, qkv_weight_ref, out_weight_ref, corner_ref, partial_ref,
                out_ref, cells_ref, keys_ref, attended_ref, block_ref, sems):
    row_count, column_count, feature = tokens_ref.shape
    bands = row_count // WLAT
    half = HALF_LAT * WLON
    for side in range(2):
        floats = halo_ref[HALF_LAT * (1 - side) : HALF_LAT * (2 - side)].astype(F32)
        for strip in range(strips - 1):
            block = floats[:, strip * WLON : (strip + 1) * WLON].reshape(half, feature)
            start = (side * (strips - 1) + strip) * half
            cells_ref[start : start + half, :] = normalize(block).astype(BF16)
    keys_ref[...] = project(cells_ref[...], qkv_weight_ref, feature, 2 * feature)
    labels = labels_ref[...]
    label_columns = labels.T
    entries = []
    for side in range(2):
        for strip in range(strips - 1):
            start = (side * (strips - 1) + strip) * half
            mine = slice(start, start + half)
            rows = slice(0, half) if side else slice(half, WIN)
            place = side * bands * strips + strip
            mask = excluded(label_columns[rows, place : place + 1], labels[place : place + 1])

            def both(head, mine=mine, side=side):
                own, halo = own_ref[mine, lanes(HEADS + head)], keys_ref[mine, lanes(head)]
                return jnp.concatenate([own, halo] if side else [halo, own], axis=0)

            for head in range(HEADS):
                entries.append(
                    (
                        lambda mine=mine, head=head: own_ref[mine, lanes(head)],
                        lambda head=head, both=both: both(head),
                        lambda head=head, both=both: both(HEADS + head),
                        lambda mask=mask, head=head, rows=rows: bias_ref[head, rows, :] + mask,
                        storer(attended_ref, mine, head),
                    )
                )
    attention(entries)
    branch = out_project(attended_ref, out_weight_ref)
    copies = []
    for side, first in enumerate((0, row_count - HALF_LAT)):
        for row in range(HALF_LAT):
            corner = corner_ref[side * HALF_LAT + row].astype(F32)
            middle = []
            for strip in range(strips - 1):
                start = (side * (strips - 1) + strip) * half + row * WLON
                middle.append(branch[start : start + WLON])
            floats = tokens_ref[first + row].astype(F32)[HALF_LON:-HALF_LON] + jnp.concatenate(middle, axis=0)
            block_ref[side * HALF_LAT + row] = jnp.concatenate([corner[:HALF_LON], floats, corner[HALF_LON:]], axis=0).astype(BF16)
        copies.append(
            pltpu.make_async_copy(
                block_ref.at[pl.ds(side * HALF_LAT, HALF_LAT)], out_ref.at[pl.ds(first, HALF_LAT)], sems.at[side]
            )
        )
        copies[-1].start()
    for copy in copies:
        copy.wait()


def shards(tokens, qkv_weight, out_weight, bias_table, position_index, region_label):
    row_count, column_count, feature = tokens.shape
    bands, strips = row_count // WLAT, column_count // WLON
    inner_columns = column_count - WLON
    whole = shape(*tokens.shape)
    dma = pltpu.SemaphoreType.DMA

    ends, inner_rows, rows = run(
        functools.partial(message_kernel, strips),
        [shape(WLAT + 1, WLON, feature), shape(WLAT, inner_columns, feature), shape(bands * strips, WIN, dtype=F32)],
        [tokens, region_label],
        specs=[HBM, VMEM],
        scratch=[pltpu.VMEM((WLAT, column_count, feature), BF16), dma((2,))],
    )
    ends = lat_exchange(ends)
    inner_rows = lat_exchange(inner_rows)

    table = jnp.pad(bias_table.T, ((0, 8 - HEADS), (0, 512 - bias_table.shape[0])))
    (bias,) = run(bias_kernel, [shape(HEADS, WIN, WIN, dtype=F32)], [table, position_index])

    inner_cells = (strips - 1) * WIN
    (inner,) = run(
        functools.partial(inner_kernel, strips),
        [shape(inner_cells, feature)],
        [tokens, rows, bias, qkv_weight, out_weight],
        flops=8 * inner_cells * feature * feature,
        exponentials=inner_cells * WIN * HEADS,
        scratch=[pltpu.VMEM((inner_cells, width), BF16) for width in (feature, 3 * feature, feature)],
    )
    left, right, labels = run(
        functools.partial(column_kernel, strips),
        [shape(row_count + WLAT, HALF_LON, feature), shape(row_count + WLAT + 1, HALF_LON, feature), shape(16, WIN, dtype=F32)],
        [tokens, ends, rows],
    )
    from_left = moved(right, "lon", 1)
    from_right = moved(left, "lon", -1)

    row_cells = (strips - 1) * WIN
    (row_qkv,) = run(
        functools.partial(rows_kernel, strips),
        [shape(row_cells, 3 * feature)],
        [tokens, qkv_weight, labels],
        flops=6 * row_cells * feature * feature,
        scratch=[pltpu.VMEM((row_cells, feature), BF16)],
    )
    side_windows = 2 * (bands + 1)
    side_cells = 2 * HALF_LON * row_count
    out, corner = run(
        functools.partial(side_kernel, strips),
        [whole, shape(WLAT, WLON, feature)],
        [tokens, from_left, from_right, ends, labels, bias, qkv_weight, out_weight, inner],
        flops=4 * (side_cells + side_windows * WIN) * feature * feature,
        exponentials=side_cells * WIN * HEADS,
        out_specs=[HBM, VMEM],
        scratch=[
            pltpu.VMEM((side_windows * WIN, feature), BF16),
            pltpu.VMEM((side_cells, feature), BF16),
            pltpu.VMEM((side_cells, feature), BF16),
            pltpu.VMEM((side_windows * WIN, 2 * feature), BF16),
            pltpu.VMEM((side_cells, feature), BF16),
            pltpu.VMEM((WLAT, column_count, feature), BF16),
            dma(()),
        ],
    )
    (out,) = run(
        functools.partial(last_kernel, strips),
        [whole],
        [tokens, inner_rows, row_qkv, labels, bias, qkv_weight, out_weight, corner, out],
        flops=6 * row_cells * feature * feature,
        exponentials=row_cells * WIN * HEADS,
        specs=[VMEM] * 8 + [HBM],
        out_specs=[HBM],
        aliases={8: 0},
        scratch=[
            pltpu.VMEM((row_cells, feature), BF16),
            pltpu.VMEM((row_cells, 2 * feature), BF16),
            pltpu.VMEM((row_cells, feature), BF16),
            pltpu.VMEM((WLAT, column_count, feature), BF16),
            dma((2,)),
        ],
    )
    return out


def solution(mesh):
    in_specs = (P("lat", "lon", None), P(), P(), P(), P(), P("lat", "lon"))
    out_specs = P("lat", "lon", None)
    return jax.shard_map(shards, mesh=mesh, in_specs=in_specs, out_specs=out_specs, check_vma=False)
```

time: 114 us -> 33.6 us (0.29); the launches traced: 113 us -> 33.3 us
  matrix products: 41 us -> 0 us
  local copies, waits for them, and re-layouts: 39.6 us -> 4.13 us
  Pallas kernels: 0 us -> 15.3 us
  waiting for transfers between devices: 15.8 us -> 6.18 us
  other arithmetic: 8.42 us -> 0 us
    dot_general x11 -> x0, matrix products: 33.7 us -> none  [the longest x8 22.7 us: one_block(): lax.dot_general(bias_table, onehot, (((0,), (1,)), ((), ())), precision=l...]
    pallas_call x0 -> x7, Pallas kernels: none -> 15.3 us  [run(): pl.pallas_call(kernel, out_shape=outs, in_specs=specs or [VMEM] * len(ope...]
    slice x8 -> x0, local copies, waits for them, and re-layouts: 12 us -> none  [the longest x2 4.92 us: attend(): windows[:, :, feature_count:2 * feature_count]]
    reshape x6 -> x0, local copies, waits for them, and re-layouts: 10.1 us -> none  [the longest x1 4.36 us: attend(): attended.reshape(band_count, strip_count, WLAT, WLON, feature_count)]
    ppermute x4, waiting for transfers between devices: 15.8 us -> 6.18 us  [moved(): return lax.ppermute(block, axis, route)]
    sub x1 -> x0, matrix products: 7.37 us -> none  [attend(): numerators = jnp.exp(jnp.where(matching, scores - largest, -jnp.inf))]
    dynamic_slice x8 -> x0, local copies, waits for them, and re-layouts: 6.78 us -> none  [bias_lookup(): looked = lax.map(one_block, blocks)]
    convert_element_type x1 -> x0, local copies, waits for them, and re-layouts: 3.88 us -> none  [attend(): attended = jnp.einsum('whqk,wkhd->wqhd', weights, values, preferred_eleme...]
  transfers between devices with their start and end apart: 4 -> 4, of which waited for: 3 -> 1; matrix products, arithmetic and copies ran while one was open for 38% -> 0% of each run, Pallas kernels for 0% -> 32%
where the time goes in v2:
time: 33.6 us; the launch traced here: 33.3 us
  Pallas kernels  15.3 us (46%)
  starting transfers between devices  7.63 us (23%)
  waiting for transfers between devices  6.18 us (18%)
  local copies, waits for them, and re-layouts  4.13 us (12%)
    pallas_call x7, Pallas kernels, run(): pl.pallas_call(kernel, out_shape=outs, in_specs=specs or [VMEM] * len(ope...  15.3 us
    ppermute x4, starting transfers between devices, moved(): return lax.ppermute(block, axis, route)  7.63 us
    ppermute x4, waiting for transfers between devices, moved(): return lax.ppermute(block, axis, route)  6.18 us
    unnamed x16, local copies, waits for them, and re-layouts  4.12 us
  transfers between devices with their start and end apart: 4, of which 1 were waited for; matrix products, arithmetic and copies ran while one was open for 0% of the time, Pallas kernels for 32%

profile of v2, /device:TPU:0, one launch (start us, length us, event | category | flops | bytes accessed | tf_op | source)
XLA Modules:
  0.0 33.3 jit_solution(16937925007993317584)
XLA Ops:
  0.0 0.0 copy-start
  0.0 1.4 %copy-done = bf16[16,64,768]{2,1,0:T(8,128)(2,1)S(1)} copy-done((bf16[16,64,768]{2,1,0:T(8,128)(2,1)S(1)}, bf16[16,64,768]{2,1,0:T(8,128)(2,1)}, u32[]{:S(2)}) %copy-start) | copy-done | bytes 1572888
  1.4 0.0 copy-start.6
  1.4 0.7 %copy-done.6 = s32[16,64]{1,0:T(8,128)S(1)} copy-done((s32[16,64]{1,0:T(8,128)S(1)}, s32[16,64]{1,0:T(8,128)}, u32[]{:S(2)}) %copy-start.6) | copy-done | bytes 4120
  2.1 0.0 copy-start.7
  2.1 0.0 copy-start.5
  2.1 0.0 copy-start.1
  2.1 0.0 copy-start.4
  2.1 0.6 %shard_map.64 = (bf16[9,16,768]{2,1,0:T(8,128)(2,1)S(1)}, bf16[8,48,768]{2,1,0:T(8,128)(2,1)S(1)}, f32[8,128]{1,0:T(8,128)S(1)}) custom-call(bf16[16,64,768]{2,1,0:T(8,128)(2,1)S(1)} %copy-done, s32[16,64]{1,0:T(8,128)S(1)} %copy-done.6), custom_call_target="tpu_custom_call" | custom-call | flops 1000000 | bytes 1000000 | tf_op jit(solution)/shard_map/pallas_call | solution.py:40
  2.7 3.0 %collective-permute-start.1 = (bf16[9,16,768]{2,1,0:T(8,128)(2,1)S(1)}, bf16[9,16,768]{2,1,0:T(8,128)(2,1)S(1)}, u32[]{:S(2)}, u32[]{:S(2)}) collective-permute-start(bf16[9,16,768]{2,1,0:T(8,128)(2,1)S(1)} %get-tuple-element.14), channel_id=1, source_target_pairs={{1,0},{0,1},{3,2},{2,3},{5,4},{4,5},{7,6},{6,7},{9,8},{8,9},{11,10... | collective-permute-start | bytes 663560 | tf_op jit(solution)/shard_map/ppermute | solution.py:30
  5.7 0.1 collective-permute-start
  5.8 6.2 %collective-permute-done.1.ends_ref = bf16[9,16,768]{2,1,0:T(8,128)(2,1)S(1)} collective-permute-done((bf16[9,16,768]{2,1,0:T(8,128)(2,1)S(1)}, bf16[9,16,768]{2,1,0:T(8,128)(2,1)S(1)}, u32[]{:S(2)}, u32[]{:S(2)}) %collective-permute-start.1) | collective-permute-done | bytes 221216 | tf_op jit(solution)/shard_map/ppermute | solution.py:30
  12.0 0.1 collective-permute-start.2
  12.1 0.0 copy-done.7
  12.1 0.0 copy-done.5
  12.1 0.5 %shard_map.67.bias_ref = f32[6,128,128]{2,1,0:T(8,128)S(1)} custom-call(f32[8,512]{1,0:T(8,128)S(1)} %pad.4.table_ref, s32[128,128]{1,0:T(8,128)S(1)} %copy-done.5), custom_call_target="tpu_custom_call" | custom-call | flops 1000000 | bytes 1000000 | tf_op jit(solution)/shard_map/pallas_call | solution.py:40
  12.7 4.5 %collective-permute-start.3 = (bf16[24,8,768]{2,1,0:T(8,128)(2,1)S(1)}, bf16[24,8,768]{2,1,0:T(8,128)(2,1)S(1)}, u32[]{:S(2)}, u32[]{:S(2)}) collective-permute-start(bf16[24,8,768]{2,1,0:T(8,128)(2,1)S(1)} %get-tuple-element.18), channel_id=1, source_target_pairs={{2,0},{4,2},{6,4},{8,6},{10,8},{12,10},{14,12},{16,14},{18,16},{20... | collective-permute-start | bytes 884744 | tf_op jit(solution)/shard_map/ppermute | solution.py:30
  17.1 0.0 copy-done.1
  17.1 0.0 copy-done.4
  17.1 0.0 copy-start.2
  17.1 2.0 %copy-done.2 = bf16[768,2304]{1,0:T(8,128)(2,1)S(1)} copy-done((bf16[768,2304]{1,0:T(8,128)(2,1)S(1)}, bf16[768,2304]{1,0:T(8,128)(2,1)}, u32[]{:S(2)}) %copy-start.2) | copy-done | bytes 3538968
  19.1 0.0 copy-start.3
  19.1 3.3 %shard_map.68.inner_ref = bf16[384,768]{1,0:T(8,128)(2,1)S(1)} custom-call(bf16[16,64,768]{2,1,0:T(8,128)(2,1)S(1)} %copy-done.1, f32[8,128]{1,0:T(8,128)S(1)} %get-tuple-element.15.rows_ref, f32[6,128,128]{2,1,0:T(8,128)S(1)} %shard_map.67.bias_ref, bf16[768,2304]{1,0:T(8,128)(2,1)S(1)} %copy-done.2, bf16[768,768]{1,0:T(8,128)(2,1)S(1)} %copy-done.4), custom_call_target="tpu_custom_call" | custom-call | flops 1811939328 | bytes 1000000 | tf_op jit(solution)/shard_map/pallas_call | solution.py:40
  22.4 0.0 copy-done.3
  22.4 1.8 %shard_map.66.own_ref = bf16[384,2304]{1,0:T(8,128)(2,1)S(1)} custom-call(bf16[16,64,768]{2,1,0:T(8,128)(2,1)S(1)} %copy-done.1, bf16[768,2304]{1,0:T(8,128)(2,1)S(1)} %copy-done.3, f32[16,128]{1,0:T(8,128)S(1)} %get-tuple-element.16.order_ref.labels_ref), custom_call_target="tpu_custom_call" | custom-call | flops 1358954496 | bytes 1000000 | tf_op jit(solution)/shard_map/pallas_call | solution.py:40
  24.3 0.0 collective-permute-done.3.from_right_ref
  24.3 0.0 collective-permute-done.2.from_left_ref
  24.3 5.1 %shard_map.69 = (bf16[16,64,768]{2,1,0:T(8,128)(2,1)}, bf16[8,16,768]{2,1,0:T(8,128)(2,1)S(1)}) custom-call(bf16[16,64,768]{2,1,0:T(8,128)(2,1)S(1)} %copy-done.1, bf16[25,8,768]{2,1,0:T(8,128)(2,1)S(1)} %collective-permute-done.2.from_left_ref, bf16[24,8,768]{2,1,0:T(8,128)(2,1)S(1)} %collective-permute-done.3.from_right_ref, ...), custom_call_target="tpu_custom_call" | custom-call | flops 2415919104 | bytes 1000000 | tf_op jit(solution)/shard_map/pallas_call | solution.py:40
  29.4 0.0 collective-permute-done.halo_ref
  29.4 3.9 %shard_map.70 = bf16[16,64,768]{2,1,0:T(8,128)(2,1)} custom-call(bf16[16,64,768]{2,1,0:T(8,128)(2,1)S(1)} %copy-done.1, bf16[8,48,768]{2,1,0:T(8,128)(2,1)S(1)} %collective-permute-done.halo_ref, bf16[384,2304]{1,0:T(8,128)(2,1)S(1)} %shard_map.66.own_ref, f32[16,128]{1,0:T(8,128)S(1)} %get-tuple-element.16.order_ref.labels_ref, ...), custom_call_target="tpu_custom_call", output_to_operand_aliasing={{}: (8, {})} | custom-call | flops 1358954496 | bytes 1000000 | tf_op jit(solution)/shard_map/pallas_call | solution.py:40
  (2 shorter events, 0.1 us)
Async XLA Ops:
  0.0 1.4 %copy-start = (bf16[16,64,768]{2,1,0:T(8,128)(2,1)S(1)}, bf16[16,64,768]{2,1,0:T(8,128)(2,1)}, u32[]{:S(2)}) copy-start(bf16[16,64,768]{2,1,0:T(8,128)(2,1)} %tokens_ref.11) | copy-start | bytes 4718596
  1.4 0.7 %copy-start.6 = (s32[16,64]{1,0:T(8,128)S(1)}, s32[16,64]{1,0:T(8,128)}, u32[]{:S(2)}) copy-start(s32[16,64]{1,0:T(8,128)} %label_ref.1) | copy-start | bytes 12292
  2.1 10.0 %copy-start.7 = (f32[465,6]{0,1:T(8,128)S(1)}, f32[465,6]{0,1:T(8,128)}, u32[]{:S(2)}) copy-start(f32[465,6]{0,1:T(8,128)} %param.9) | copy-start | bytes 33484
  2.1 10.0 %copy-start.5 = (s32[128,128]{1,0:T(8,128)S(1)}, s32[128,128]{1,0:T(8,128)}, u32[]{:S(2)}) copy-start(s32[128,128]{1,0:T(8,128)} %index_ref.1) | copy-start | bytes 196612
  2.1 15.0 %copy-start.1 = (bf16[16,64,768]{2,1,0:T(8,128)(2,1)S(1)}, bf16[16,64,768]{2,1,0:T(8,128)(2,1)}, u32[]{:S(2)}) copy-start(bf16[16,64,768]{2,1,0:T(8,128)(2,1)} %tokens_ref.11) | copy-start | bytes 4718596
  2.1 15.0 %copy-start.4 = (bf16[768,768]{1,0:T(8,128)(2,1)S(1)}, bf16[768,768]{1,0:T(8,128)(2,1)}, u32[]{:S(2)}) copy-start(bf16[768,768]{1,0:T(8,128)(2,1)} %out_weight_ref.5) | copy-start | bytes 3538948
  2.7 9.3 %collective-permute-start.1 = (bf16[9,16,768]{2,1,0:T(8,128)(2,1)S(1)}, bf16[9,16,768]{2,1,0:T(8,128)(2,1)S(1)}, u32[]{:S(2)}, u32[]{:S(2)}) collective-permute-start(bf16[9,16,768]{2,1,0:T(8,128)(2,1)S(1)} %get-tuple-element.14), channel_id=1, source_target_pairs={{1,0},{0,1},{3,2},{2,3},{5,4},{4,5},{7,6},{6,7},{9,8},{8,9},{11,10... | collective-permute-start | bytes 663560 | tf_op jit(solution)/shard_map/ppermute | solution.py:30
  5.7 23.7 %collective-permute-start = (bf16[8,48,768]{2,1,0:T(8,128)(2,1)S(1)}, bf16[8,48,768]{2,1,0:T(8,128)(2,1)S(1)}, u32[]{:S(2)}, u32[]{:S(2)}) collective-permute-start(bf16[8,48,768]{2,1,0:T(8,128)(2,1)S(1)} %get-tuple-element.13), channel_id=1, source_target_pairs={{1,0},{0,1},{3,2},{2,3},{5,4},{4,5},{7,6},{6,7},{9,8},{8,9},{11,10... | collective-permute-start | bytes 1769480 | tf_op jit(solution)/shard_map/ppermute | solution.py:30
  12.0 12.2 %collective-permute-start.2 = (bf16[25,8,768]{2,1,0:T(8,128)(2,1)S(1)}, bf16[25,8,768]{2,1,0:T(8,128)(2,1)S(1)}, u32[]{:S(2)}, u32[]{:S(2)}) collective-permute-start(bf16[25,8,768]{2,1,0:T(8,128)(2,1)S(1)} %get-tuple-element.17), channel_id=1, source_target_pairs={{30,0},{0,2},{2,4},{4,6},{6,8},{8,10},{10,12},{12,14},{14,16},{16,... | collective-permute-start | bytes 921608 | tf_op jit(solution)/shard_map/ppermute | solution.py:30
  12.7 11.6 %collective-permute-start.3 = (bf16[24,8,768]{2,1,0:T(8,128)(2,1)S(1)}, bf16[24,8,768]{2,1,0:T(8,128)(2,1)S(1)}, u32[]{:S(2)}, u32[]{:S(2)}) collective-permute-start(bf16[24,8,768]{2,1,0:T(8,128)(2,1)S(1)} %get-tuple-element.18), channel_id=1, source_target_pairs={{2,0},{4,2},{6,4},{8,6},{10,8},{12,10},{14,12},{16,14},{18,16},{20... | collective-permute-start | bytes 884744 | tf_op jit(solution)/shard_map/ppermute | solution.py:30
  17.1 2.0 %copy-start.2 = (bf16[768,2304]{1,0:T(8,128)(2,1)S(1)}, bf16[768,2304]{1,0:T(8,128)(2,1)}, u32[]{:S(2)}) copy-start(bf16[768,2304]{1,0:T(8,128)(2,1)} %qkv_weight_ref.7) | copy-start | bytes 10616836
  19.1 3.3 %copy-start.3 = (bf16[768,2304]{1,0:T(8,128)(2,1)S(1)}, bf16[768,2304]{1,0:T(8,128)(2,1)}, u32[]{:S(2)}) copy-start(bf16[768,2304]{1,0:T(8,128)(2,1)} %qkv_weight_ref.7) | copy-start | bytes 10616836

commit v3 on v2

v3 whole, which is shorter than its diff:
```python
import functools

import jax
import jax.numpy as jnp
from jax import lax
from jax.experimental import pallas as pl
from jax.experimental.pallas import tpu as pltpu
from jax.sharding import PartitionSpec as P

HEADS = 6
HEAD = 128
WLAT = 8
WLON = 16
WIN = WLAT * WLON
HALF_LAT = WLAT // 2
HALF_LON = WLON // 2
LOG2E = 1.4426950408889634
SCALE = LOG2E / HEAD**0.5
EXCLUDED = -1e30
VMEM = pl.BlockSpec(memory_space=pltpu.VMEM)
HBM = pl.BlockSpec(memory_space=pltpu.HBM)
ANY = pl.BlockSpec(memory_space=pl.ANY)
F32 = jnp.float32
BF16 = jnp.bfloat16


def moved(block, axis, distance):
    count = lax.axis_size(axis)
    route = [((i - distance) % count, i) for i in range(count)]
    return lax.ppermute(block, axis, route)


def lat_exchange(message):
    if lax.axis_size("lat") == 2:
        return moved(message, "lat", 1)
    return jnp.concatenate([moved(message[:HALF_LAT], "lat", -1), moved(message[HALF_LAT:], "lat", 1)], axis=0)


def lon_exchange(even_odd, odd_even):
    count = lax.axis_size("lon")
    first = [(i, i ^ 1) for i in range(count)]
    second = [(i, (i + 1 if i % 2 else i - 1) % count) for i in range(count)]
    odd_even = lax.ppermute(odd_even, "lon", second)
    return lax.ppermute(even_odd, "lon", first), odd_even


def run(kernel, outs, operands, scratch=(), specs=None, out_specs=None, mib=4, flops=10**6):
    return pl.pallas_call(
        kernel,
        out_shape=outs,
        in_specs=specs or [VMEM] * len(operands),
        out_specs=out_specs or [VMEM] * len(outs),
        scratch_shapes=scratch,
        compiler_params=pltpu.CompilerParams(vmem_limit_bytes=mib * 2**20),
        cost_estimate=pl.CostEstimate(flops=flops, bytes_accessed=10**5, transcendentals=0),
    )(*operands)


def shape(*extent, dtype=BF16):
    return jax.ShapeDtypeStruct(extent, dtype)


def normalize(floats):
    floats = floats - jnp.mean(floats, axis=-1, keepdims=True)
    return floats * lax.rsqrt(jnp.mean(jnp.square(floats), axis=-1, keepdims=True) + 1e-05)


def label_rows(labels, strips):
    rows, columns = labels.shape
    labels = labels.astype(BF16)
    source = lax.broadcasted_iota(jnp.int32, (columns, WIN), 0)
    cell = lax.broadcasted_iota(jnp.int32, (columns, WIN), 1)
    at_row = lax.broadcasted_iota(jnp.int32, (rows, WIN), 0) % WLAT == lax.broadcasted_iota(jnp.int32, (rows, WIN), 1) // WLON
    place = lax.broadcasted_iota(jnp.int32, (rows // WLAT * strips, WIN), 0)
    result = jnp.zeros((rows // WLAT * strips, WIN), F32)
    for strip in range(strips):
        spread = jnp.dot(labels, (source == strip * WLON + cell % WLON).astype(BF16), preferred_element_type=F32)
        spread = jnp.where(at_row, spread, 0.0)
        for band in range(rows // WLAT):
            row = jnp.sum(spread[band * WLAT : (band + 1) * WLAT], axis=0, keepdims=True)
            result = jnp.where(place == band * strips + strip, row, result)
    return result


def message_kernel(tokens_ref, ends_ref, inner_ref, middle_ref, columns_ref):
    row_count = tokens_ref.shape[0]
    for row in range(row_count):
        floats = tokens_ref[row].astype(F32)
        columns = jnp.concatenate([floats[:HALF_LON], floats[-HALF_LON:]], axis=0).astype(BF16)
        inner = floats[HALF_LON:-HALF_LON].astype(BF16)
        columns_ref[row] = columns
        if HALF_LAT <= row < row_count - HALF_LAT:
            middle_ref[row - HALF_LAT] = inner
        else:
            at = row if row < HALF_LAT else row - row_count + WLAT
            ends_ref[at] = columns
            inner_ref[at] = inner


def column_kernel(strips, columns_ref, rows_ref, above_ref, even_odd_ref, odd_even_ref, labels_ref):
    row_count, _, feature = columns_ref.shape
    odd = lax.axis_index("lon") % 2 == 1
    for row in range(row_count):
        floats = columns_ref[row].astype(F32)
        left, right = floats[:HALF_LON], floats[HALF_LON:]
        even_odd_ref[row] = jnp.where(odd, left, right).astype(BF16)
        odd_even_ref[row] = jnp.where(odd, right, left).astype(BF16)
    labels = jnp.concatenate([label_rows(above_ref[above_ref.shape[0] - WLAT :, :], strips), rows_ref[...]], axis=0)
    labels = jnp.concatenate([labels, jnp.zeros((16 - labels.shape[0], WIN), F32)], axis=0)
    labels_ref[...] = labels
    filler = jnp.zeros((HALF_LON, feature - 2 * WIN), F32)
    message = jnp.concatenate([labels[:8], labels[8:], filler], axis=1).astype(BF16)
    even_odd_ref[row_count] = message
    odd_even_ref[row_count] = message


def corner_message_kernel(ends_ref, after_ref, even_odd_ref, odd_even_ref):
    odd = lax.axis_index("lon") % 2 == 1
    for row in range(WLAT):
        floats = ends_ref[row].astype(F32)
        left, right = floats[:HALF_LON], floats[HALF_LON:]
        even_odd_ref[row] = jnp.where(odd, left, right).astype(BF16)
        odd_even_ref[row] = jnp.where(odd, right, left).astype(BF16)


def halo_row(row, row_count):
    return row + HALF_LAT if row < HALF_LAT else row - row_count - HALF_LAT


def look_up(table_ref, index_ref, out_ref):
    entries = table_ref.shape[1]
    for row in range(0, WIN, 8):
        index = index_ref[row : row + 8, :]
        low, high = index & 127, index >> 7
        for head in range(HEADS):
            value = jnp.zeros((8, WIN), F32)
            for part in range(-(-entries // 128)):
                source = jnp.broadcast_to(table_ref[head : head + 1, part * 128 : part * 128 + 128], (8, 128))
                value = jnp.where(high == part, jnp.take_along_axis(source, low, axis=1), value)
            out_ref[head, row : row + 8, :] = value * LOG2E


def excluded(columns, row):
    return jnp.where(columns == row, 0.0, EXCLUDED)


def attention(entries):
    scores = []
    for queries, keys, _, bias, _ in entries:
        product = lax.dot_general(queries(), keys(), (((1,), (1,)), ((), ())), preferred_element_type=F32)
        scores.append(product * SCALE + bias())
    numerators = [jnp.exp2(score - jnp.max(score, axis=-1, keepdims=True)) for score in scores]
    for (_, _, values, _, store), numerator in zip(entries, numerators):
        total = jnp.sum(numerator, axis=-1, keepdims=True)
        summed = jnp.dot(numerator.astype(BF16), values(), preferred_element_type=F32)
        store((summed * (1.0 / total)).astype(BF16))


def project(source, weight_ref, first, count):
    return jnp.dot(source, weight_ref[:, first : first + count], preferred_element_type=F32).astype(BF16)


def out_project(attended, weight_ref):
    return jnp.dot(attended, weight_ref[...], preferred_element_type=F32).astype(BF16).astype(F32)


def lanes(head):
    return slice(head * HEAD, (head + 1) * HEAD)


def storer(ref, rows, head):
    def store(value):
        ref[rows, lanes(head)] = value

    return store


def inner_kernel(strips, middle_ref, label_ref, table_ref, index_ref, qkv_weight_ref, out_weight_ref,
                 out_ref, bias_ref, rows_ref, cells_ref, qkv_ref, attended_ref, wide_ref):
    feature = middle_ref.shape[-1]
    floats = []
    for strip in range(strips - 1):
        window = middle_ref[:, strip * WLON : (strip + 1) * WLON, :].astype(F32).reshape(WIN, feature)
        floats.append(window)
        cells_ref[strip * WIN : (strip + 1) * WIN, :] = normalize(window).astype(BF16)
    wide_ref[...] = jnp.zeros(wide_ref.shape, F32)
    wide_ref[: table_ref.shape[0], : table_ref.shape[1]] = table_ref[...]
    qkv_ref[...] = project(cells_ref[...], qkv_weight_ref, 0, 3 * feature)
    look_up(wide_ref, index_ref, bias_ref)
    labels = label_rows(label_ref[...], strips)
    rows_ref[...] = labels
    label_columns = labels.T
    entries = []
    for strip in range(strips - 1):
        mine = slice(strip * WIN, (strip + 1) * WIN)
        mask = excluded(label_columns[:, strip : strip + 1], labels[strip : strip + 1])
        for head in range(HEADS):
            entries.append(
                (
                    lambda mine=mine, head=head: qkv_ref[mine, lanes(head)],
                    lambda mine=mine, head=head: qkv_ref[mine, lanes(HEADS + head)],
                    lambda mine=mine, head=head: qkv_ref[mine, lanes(2 * HEADS + head)],
                    lambda mask=mask, head=head: bias_ref[head] + mask,
                    storer(attended_ref, mine, head),
                )
            )
    attention(entries)
    branch = out_project(attended_ref[...], out_weight_ref)
    for strip in range(strips - 1):
        mine = slice(strip * WIN, (strip + 1) * WIN)
        out_ref[mine, :] = (floats[strip] + branch[mine]).astype(BF16)


def rows_kernel(strips, inner_ref, qkv_weight_ref, after_ref, out_ref, cells_ref):
    feature = inner_ref.shape[-1]
    half = HALF_LAT * WLON
    for side in range(2):
        for strip in range(strips - 1):
            block = inner_ref[side * HALF_LAT : (side + 1) * HALF_LAT, strip * WLON : (strip + 1) * WLON, :]
            start = (side * (strips - 1) + strip) * half
            cells_ref[start : start + half, :] = normalize(block.astype(F32).reshape(half, feature)).astype(BF16)
    out_ref[...] = project(cells_ref[...], qkv_weight_ref, 0, 3 * feature)


def side_windows(bands, between):
    windows, start = [], 0
    for band in range(bands + 1):
        if (0 < band < bands) == between:
            count = HALF_LON * (WLAT if between else HALF_LAT)
            for side in range(2):
                windows.append((band, side, start, count))
                start += count
    return windows


def side_blocks(windows, bands, strips, own_of, halo_of, left_labels, labels, bias_ref, qkv_weight_ref, out_weight_ref,
                cells_ref, own_ref, queries_ref, keys_ref, attended_ref):
    feature = cells_ref.shape[-1]
    label_columns = left_labels.T, labels.T
    tokens_of = {}
    for at, (band, side, start, count) in enumerate(windows):
        own = [own_of(row, side) for row in range(band * WLAT, (band + 1) * WLAT)]
        halo = [halo_of(row, side) for row in range(band * WLAT, (band + 1) * WLAT)]
        mine = slice(HALF_LAT if band == 0 else 0, HALF_LAT if band == bands else WLAT)
        tokens_of[band, side] = own[mine]
        own = normalize(jnp.stack(own))
        halo = normalize(jnp.stack(halo))
        window = jnp.concatenate([own, halo] if side else [halo, own], axis=1)
        cells_ref[at * WIN : (at + 1) * WIN, :] = window.reshape(WIN, feature).astype(BF16)
        own_ref[start : start + count, :] = own[mine].reshape(count, feature).astype(BF16)
    queries_ref[...] = project(own_ref[...], qkv_weight_ref, 0, feature)
    keys_ref[...] = project(cells_ref[...], qkv_weight_ref, feature, 2 * feature)

    def own_rows(array, band, side):
        array = array.reshape(WLAT, WLON, WIN)
        array = array[HALF_LAT if band == 0 else 0 : HALF_LAT if band == bands else WLAT]
        array = array[:, :HALF_LON] if side else array[:, HALF_LON:]
        return array.reshape(-1, WIN)

    entries = []
    for at, (band, side, start, count) in enumerate(windows):
        mine, whole = slice(start, start + count), slice(at * WIN, (at + 1) * WIN)
        place = band * strips + strips - 1
        row = (labels if side else left_labels)[place : place + 1]
        mask = own_rows(excluded(label_columns[side][:, place : place + 1], row), band, side)
        for head in range(HEADS):
            entries.append(
                (
                    lambda mine=mine, head=head: queries_ref[mine, lanes(head)],
                    lambda whole=whole, head=head: keys_ref[whole, lanes(head)],
                    lambda whole=whole, head=head: keys_ref[whole, lanes(HEADS + head)],
                    lambda mask=mask, head=head, band=band, side=side: own_rows(bias_ref[head], band, side) + mask,
                    storer(attended_ref, mine, head),
                )
            )
    attention(entries)
    branch = out_project(attended_ref[...], out_weight_ref)
    blocks = {}
    for band, side, start, count in windows:
        for row, own in enumerate(tokens_of[band, side]):
            at = start + row * HALF_LON
            blocks[band, side, row] = own + branch[at : at + HALF_LON]
    return blocks


def swapped(even_odd_ref, odd_even_ref):
    odd = lax.axis_index("lon") % 2 == 1

    def row_of(row, side):
        first, second = even_odd_ref[row].astype(F32), odd_even_ref[row].astype(F32)
        return jnp.where(odd, second, first) if side else jnp.where(odd, first, second)

    return row_of


def half_of(floats, side):
    return floats[HALF_LON:] if side else floats[:HALF_LON]


def left_labels_of(received, row):
    message = received(row, 0)
    return jnp.concatenate([message[:, :WIN], message[:, WIN : 2 * WIN]], axis=0)


def between_kernel(strips, columns_ref, even_odd_ref, odd_even_ref, labels_ref, bias_ref, qkv_weight_ref, out_weight_ref, inner_ref,
                   after_ref, out_ref, left_ref, *scratch):
    row_count = columns_ref.shape[0]
    received = swapped(even_odd_ref, odd_even_ref)
    left_labels = left_labels_of(received, row_count)
    left_ref[...] = left_labels
    blocks = side_blocks(
        side_windows(row_count // WLAT, True), row_count // WLAT, strips,
        lambda row, side: half_of(columns_ref[row - HALF_LAT].astype(F32), side),
        lambda row, side: received(row - HALF_LAT, side),
        left_labels, labels_ref[...], bias_ref, qkv_weight_ref, out_weight_ref, *scratch,
    )
    for row in range(WLAT):
        middle = [inner_ref[strip * WIN + row * WLON : strip * WIN + (row + 1) * WLON, :].astype(F32) for strip in range(strips - 1)]
        out_ref[row] = jnp.concatenate([blocks[1, 0, row]] + middle + [blocks[1, 1, row]], axis=0).astype(BF16)


def corner_kernel(strips, columns_ref, even_odd_ref, odd_even_ref, corner_even_odd_ref, corner_odd_even_ref, ends_ref, labels_ref,
                  left_ref, bias_ref, qkv_weight_ref, out_weight_ref, corner_ref, *scratch):
    row_count = columns_ref.shape[0]
    bands = row_count // WLAT
    received = swapped(even_odd_ref, odd_even_ref)
    received_corner = swapped(corner_even_odd_ref, corner_odd_even_ref)

    def inside(row):
        return HALF_LAT <= row < row_count + HALF_LAT

    def own_of(row, side):
        floats = columns_ref[row - HALF_LAT] if inside(row) else ends_ref[halo_row(row, row_count)]
        return half_of(floats.astype(F32), side)

    def halo_of(row, side):
        return received(row - HALF_LAT, side) if inside(row) else received_corner(halo_row(row, row_count), side)

    blocks = side_blocks(
        side_windows(bands, False), bands, strips, own_of, halo_of,
        left_ref[...], labels_ref[...], bias_ref, qkv_weight_ref, out_weight_ref, *scratch,
    )
    for band, first in ((0, 0), (bands, HALF_LAT)):
        for row in range(HALF_LAT):
            corner_ref[first + row] = jnp.concatenate([blocks[band, 0, row], blocks[band, 1, row]], axis=0).astype(BF16)


def last_kernel(strips, inner_ref, halo_ref, own_ref, labels_ref, bias_ref, qkv_weight_ref, out_weight_ref, corner_ref, between_ref,
                out_ref, cells_ref, keys_ref, attended_ref, block_ref, sems):
    row_count, column_count, feature = out_ref.shape
    copies = [pltpu.make_async_copy(between_ref, out_ref.at[pl.ds(HALF_LAT, row_count - WLAT)], sems.at[2])]
    copies[0].start()
    bands = row_count // WLAT
    half = HALF_LAT * WLON
    places = [(side, strip) for side in range(2) for strip in range(strips - 1)]
    for at, (side, strip) in enumerate(places):
        block = halo_ref[HALF_LAT * (1 - side) : HALF_LAT * (2 - side), strip * WLON : (strip + 1) * WLON, :]
        cells_ref[at * half : (at + 1) * half, :] = normalize(block.astype(F32).reshape(half, feature)).astype(BF16)
    keys_ref[...] = project(cells_ref[...], qkv_weight_ref, feature, 2 * feature)
    labels = labels_ref[...]
    label_columns = labels.T
    entries = []
    for at, (side, strip) in enumerate(places):
        mine = slice(at * half, (at + 1) * half)
        rows = slice(0, half) if side else slice(half, WIN)
        place = side * bands * strips + strip
        mask = excluded(label_columns[rows, place : place + 1], labels[place : place + 1])

        def both(head, mine=mine, side=side):
            pair = own_ref[mine, lanes(HEADS + head)], keys_ref[mine, lanes(head)]
            return jnp.concatenate(pair if side else pair[::-1], axis=0)

        for head in range(HEADS):
            entries.append(
                (
                    lambda mine=mine, head=head: own_ref[mine, lanes(head)],
                    lambda head=head, both=both: both(head),
                    lambda head=head, both=both: both(HEADS + head),
                    lambda mask=mask, head=head, rows=rows: bias_ref[head, rows, :] + mask,
                    storer(attended_ref, mine, head),
                )
            )
    attention(entries)
    for side, first in enumerate((0, row_count - HALF_LAT)):
        cells = (strips - 1) * half
        branch = out_project(attended_ref[side * cells : (side + 1) * cells, :], out_weight_ref)
        for row in range(HALF_LAT):
            at = side * HALF_LAT + row
            corner = corner_ref[at].astype(F32)
            middle = [branch[strip * half + row * WLON : strip * half + (row + 1) * WLON] for strip in range(strips - 1)]
            middle = inner_ref[at].astype(F32) + jnp.concatenate(middle, axis=0)
            block_ref[at] = jnp.concatenate([corner[:HALF_LON], middle, corner[HALF_LON:]], axis=0).astype(BF16)
        source = block_ref.at[pl.ds(side * HALF_LAT, HALF_LAT)]
        copies.append(pltpu.make_async_copy(source, out_ref.at[pl.ds(first, HALF_LAT)], sems.at[side]))
        copies[-1].start()
    for copy in copies:
        copy.wait()


def shards(tokens, qkv_weight, out_weight, bias_table, position_index, region_label):
    row_count, column_count, feature = tokens.shape
    bands, strips = row_count // WLAT, column_count // WLON
    whole = shape(*tokens.shape)
    inner_columns = column_count - WLON
    dma = pltpu.SemaphoreType.DMA

    label_above = moved(region_label, "lat", 1)
    ends, inner_rows, middle, columns = run(
        message_kernel,
        [
            shape(WLAT, WLON, feature),
            shape(WLAT, inner_columns, feature),
            shape(row_count - WLAT, inner_columns, feature),
            shape(row_count, WLON, feature),
        ],
        [tokens],
        flops=5 * 10**9,
    )
    ends_received = lat_exchange(ends)
    rows_received = lat_exchange(inner_rows)

    inner_cells = (strips - 1) * WIN
    inner, bias, label_own = run(
        functools.partial(inner_kernel, strips),
        [shape(inner_cells, feature), shape(HEADS, WIN, WIN, dtype=F32), shape(bands * strips, WIN, dtype=F32)],
        [middle, region_label, bias_table.T, position_index, qkv_weight, out_weight],
        scratch=[pltpu.VMEM((inner_cells, width * feature), BF16) for width in (1, 3, 1)]
        + [pltpu.VMEM((8, -(-bias_table.shape[0] // 128) * 128), F32)],
        mib=12,
        flops=2 * 10**10,
    )
    message = shape(row_count + 1, HALF_LON, feature)
    *columns_sent, labels = run(
        functools.partial(column_kernel, strips), [message, message, shape(16, WIN, dtype=F32)], [columns, label_own, label_above]
    )
    columns_received = lon_exchange(*columns_sent)

    message = shape(WLAT, HALF_LON, feature)
    corners = run(corner_message_kernel, [message, message], [ends_received, columns_sent[0]], specs=[VMEM, ANY])
    corners_received = lon_exchange(*corners)
    row_cells = (strips - 1) * WIN
    (row_qkv,) = run(
        functools.partial(rows_kernel, strips),
        [shape(row_cells, 3 * feature)],
        [inner_rows, qkv_weight, corners[0]],
        specs=[VMEM, VMEM, ANY],
        scratch=[pltpu.VMEM((row_cells, feature), BF16)],
        mib=8,
    )

    def side_scratch(between):
        windows = side_windows(bands, between)
        cells, every = windows[-1][2] + windows[-1][3], len(windows) * WIN
        sizes = ((every, 1), (cells, 1), (cells, 1), (every, 2), (cells, 1))
        return cells, every, [pltpu.VMEM((count, width * feature), BF16) for count, width in sizes]

    cells, every, scratch = side_scratch(True)
    between, label_left = run(
        functools.partial(between_kernel, strips),
        [shape(row_count - WLAT, column_count, feature), shape(16, WIN, dtype=F32)],
        [columns, *columns_received, labels, bias, qkv_weight, out_weight, inner, row_qkv],
        specs=[VMEM] * 8 + [ANY],
        scratch=scratch,
        mib=12,
    )
    cells, every, scratch = side_scratch(False)
    (corner,) = run(
        functools.partial(corner_kernel, strips),
        [shape(WLAT, WLON, feature)],
        [columns, *columns_received, *corners_received, ends_received, labels, label_left, bias, qkv_weight, out_weight],
        scratch=scratch,
        mib=12,
    )
    (out,) = run(
        functools.partial(last_kernel, strips),
        [whole],
        [inner_rows, rows_received, row_qkv, labels, bias, qkv_weight, out_weight, corner, between],
        out_specs=[HBM],
        mib=12,
        scratch=[pltpu.VMEM((row_cells, width * feature), BF16) for width in (1, 2, 1)]
        + [pltpu.VMEM((WLAT, column_count, feature), BF16), dma((3,))],
    )
    return out


def solution(mesh):
    in_specs = (P("lat", "lon", None), P(), P(), P(), P(), P("lat", "lon"))
    out_specs = P("lat", "lon", None)
    return jax.shard_map(shards, mesh=mesh, in_specs=in_specs, out_specs=out_specs, check_vma=False)
```

time: 33.6 us -> 28.8 us (0.86)
  waiting for transfers between devices: 6.18 us -> 0.88 us
  starting transfers between devices: 7.63 us -> 11.9 us
  local copies, waits for them, and re-layouts: 4.13 us -> 1.43 us
  Pallas kernels: 15.3 us -> 14.3 us
    ppermute x0 -> x4, starting transfers between devices: none -> 6.85 us  [the longest x2 6.71 us: lon_exchange(): odd_even = lax.ppermute(odd_even, 'lon', second)]
    ppermute x4 -> x3, waiting for transfers between devices: 6.18 us -> 0.01 us  [moved(): return lax.ppermute(block, axis, route)]
    unnamed x16 -> x12, local copies, waits for them, and re-layouts: 4.12 us -> 1.43 us
    ppermute x4 -> x3, starting transfers between devices: 7.63 us -> 5.06 us  [moved(): return lax.ppermute(block, axis, route)]
    pallas_call x7 -> x8, Pallas kernels: 15.3 us -> 14.3 us  [run(): pl.pallas_call(kernel, out_shape=outs, in_specs=specs or [VMEM] * len(ope...]
    ppermute x0 -> x4, waiting for transfers between devices: none -> 0.87 us  [the longest x2 0.87 us: lon_exchange(): odd_even = lax.ppermute(odd_even, 'lon', second)]
  transfers between devices with their start and end apart: 4 -> 7, of which waited for: 1 -> 1; matrix products, arithmetic and copies ran while one was open for 0% -> 0% of each run, Pallas kernels for 32% -> 37%
where the time goes in v3:
time: 28.8 us; the launch traced here: 28.6 us
  Pallas kernels  14.3 us (50%)
  starting transfers between devices  11.9 us (41%)
  local copies, waits for them, and re-layouts  1.43 us (5%)
  waiting for transfers between devices  0.88 us (3%)
    pallas_call x8, Pallas kernels, run(): pl.pallas_call(kernel, out_shape=outs, in_specs=specs or [VMEM] * len(ope...  14.3 us
    ppermute x2, starting transfers between devices, lon_exchange(): odd_even = lax.ppermute(odd_even, 'lon', second)  6.71 us
    ppermute x3, starting transfers between devices, moved(): return lax.ppermute(block, axis, route)  5.06 us
    unnamed x12, local copies, waits for them, and re-layouts  1.43 us
    ppermute x2, waiting for transfers between devices, lon_exchange(): odd_even = lax.ppermute(odd_even, 'lon', second)  0.87 us
  transfers between devices with their start and end apart: 7, of which 1 were waited for; matrix products, arithmetic and copies ran while one was open for 0% of the time, Pallas kernels for 37%

profile of v3, /device:TPU:0, one launch (start us, length us, event | category | flops | bytes accessed | tf_op | source)
XLA Modules:
  0.0 28.6 jit_solution(15410723679424181835)
XLA Ops:
  0.0 0.0 copy-start
  0.0 0.0 copy-start.1
  0.0 3.0 %collective-permute-start.2 = (s32[16,64]{1,0:T(8,128)}, s32[16,64]{1,0:T(8,128)S(1)}, u32[]{:S(2)}, u32[]{:S(2)}) collective-permute-start(s32[16,64]{1,0:T(8,128)} %label_ref.1), channel_id=1, source_target_pairs={{1,0},{0,1},{3,2},{2,3},{5,4},{4,5},{7,6},{6,7},{9,8},{8,9},{11,10... | collective-permute-start | bytes 12296 | tf_op jit(solution)/shard_map/ppermute | solution.py:30
  3.0 0.0 copy-start.2
  3.0 1.4 %copy-done.2 = bf16[16,64,768]{2,1,0:T(8,128)(2,1)S(1)} copy-done((bf16[16,64,768]{2,1,0:T(8,128)(2,1)S(1)}, bf16[16,64,768]{2,1,0:T(8,128)(2,1)}, u32[]{:S(2)}) %copy-start.2) | copy-done | bytes 1572888
  4.4 0.0 copy-start.3
  4.4 0.0 copy-start.4
  4.4 0.0 copy-start.5
  4.4 0.1 shard_map.64
  4.5 0.2 collective-permute-start.1
  4.7 1.9 %collective-permute-start = (bf16[8,48,768]{2,1,0:T(8,128)(2,1)S(1)}, bf16[8,48,768]{2,1,0:T(8,128)(2,1)S(1)}, u32[]{:S(2)}, u32[]{:S(2)}) collective-permute-start(bf16[8,48,768]{2,1,0:T(8,128)(2,1)S(1)} %get-tuple-element.19.inner_ref), channel_id=1, source_target_pairs={{1,0},{0,1},{3,2},{2,3},{5,4},{4,5},{7,6},{6,7},{9,8},{8,9},{11,10... | collective-permute-start | bytes 1769480 | tf_op jit(solution)/shard_map/ppermute | solution.py:30
  6.6 0.0 copy-done
  6.6 0.0 copy-done.1
  6.6 0.0 copy-done.3
  6.6 0.0 copy-done.4
  6.6 0.0 copy-done.5
  6.6 3.3 %shard_map.65 = (bf16[384,768]{1,0:T(8,128)(2,1)S(1)}, f32[6,128,128]{2,1,0:T(8,128)S(1)}, f32[8,128]{1,0:T(8,128)S(1)}) custom-call(bf16[8,48,768]{2,1,0:T(8,128)(2,1)S(1)} %get-tuple-element.22.middle_ref, s32[16,64]{1,0:T(8,128)S(1)} %copy-done.5, f32[6,465]{1,0:T(8,128)S(1)} %bitcast.1, s32[128,128]{1,0:T(8,128)S(1)} %copy-done.3, ...), custom_call_target="tpu_custom_call" | custom-call | flops 20000000000 | bytes 100000 | tf_op jit(solution)/shard_map/pallas_call | solution.py:48
  10.0 0.0 collective-permute-done.2.above_ref
  10.0 0.2 shard_map.66
  10.2 0.1 collective-permute-start.3
  10.3 4.6 %collective-permute-start.4 = (bf16[17,8,768]{2,1,0:T(8,128)(2,1)S(1)}, bf16[17,8,768]{2,1,0:T(8,128)(2,1)S(1)}, u32[]{:S(2)}, u32[]{:S(2)}) collective-permute-start(bf16[17,8,768]{2,1,0:T(8,128)(2,1)S(1)} %get-tuple-element.28), channel_id=1, source_target_pairs={{0,30},{2,4},{4,2},{6,8},{8,6},{10,12},{12,10},{14,16},{16,14},{18... | collective-permute-start | bytes 626696 | tf_op jit(solution)/shard_map/ppermute | solution.py:43
  14.9 0.0 collective-permute-done.1.ends_ref
  14.9 0.1 shard_map.67
  15.0 0.1 collective-permute-start.5
  15.1 2.1 %collective-permute-start.6 = (bf16[8,8,768]{2,1,0:T(8,128)(2,1)S(1)}, bf16[8,8,768]{2,1,0:T(8,128)(2,1)S(1)}, u32[]{:S(2)}, u32[]{:S(2)}) collective-permute-start(bf16[8,8,768]{2,1,0:T(8,128)(2,1)S(1)} %get-tuple-element.29), channel_id=1, source_target_pairs={{0,30},{2,4},{4,2},{6,8},{8,6},{10,12},{12,10},{14,16},{16,14},{18... | collective-permute-start | bytes 294920 | tf_op jit(solution)/shard_map/ppermute | solution.py:43
  17.2 1.8 %shard_map.68.after_ref.own_ref = bf16[384,2304]{1,0:T(8,128)(2,1)S(1)} custom-call(bf16[8,48,768]{2,1,0:T(8,128)(2,1)S(1)} %get-tuple-element.19.inner_ref, bf16[768,2304]{1,0:T(8,128)(2,1)S(1)} %copy-done, bf16[8,8,768]{2,1,0:T(8,128)(2,1)S(1)} %get-tuple-element.25.after_ref), custom_call_target="tpu_custom_call" | custom-call | flops 1000000 | bytes 100000 | tf_op jit(solution)/shard_map/pallas_call | solution.py:48
  19.0 0.0 collective-permute-done.3.even_odd_ref
  19.0 0.0 collective-permute-done.4.odd_even_ref
  19.0 2.0 %shard_map.69 = (bf16[8,64,768]{2,1,0:T(8,128)(2,1)S(1)}, f32[16,128]{1,0:T(8,128)S(1)}) custom-call(bf16[16,16,768]{2,1,0:T(8,128)(2,1)S(1)} %get-tuple-element.21.columns_ref, bf16[17,8,768]{2,1,0:T(8,128)(2,1)S(1)} %collective-permute-done.3.even_odd_ref, bf16[17,8,768]{2,1,0:T(8,128)(2,1)S(1)} %collective-permute-done.4.odd_even_ref, ...), custom_call_target="tpu_custom_call" | custom-call | flops 1000000 | bytes 100000 | tf_op jit(solution)/shard_map/pallas_call | solution.py:48
  21.0 0.0 collective-permute-done.5.corner_even_odd_ref
  21.0 0.9 %collective-permute-done.6.corner_odd_even_ref = bf16[8,8,768]{2,1,0:T(8,128)(2,1)S(1)} collective-permute-done((bf16[8,8,768]{2,1,0:T(8,128)(2,1)S(1)}, bf16[8,8,768]{2,1,0:T(8,128)(2,1)S(1)}, u32[]{:S(2)}, u32[]{:S(2)}) %collective-permute-start.6) | collective-permute-done | bytes 98336 | tf_op jit(solution)/shard_map/ppermute | solution.py:43
  21.9 2.9 %shard_map.70.corner_ref = bf16[8,16,768]{2,1,0:T(8,128)(2,1)S(1)} custom-call(bf16[16,16,768]{2,1,0:T(8,128)(2,1)S(1)} %get-tuple-element.21.columns_ref, bf16[17,8,768]{2,1,0:T(8,128)(2,1)S(1)} %collective-permute-done.3.even_odd_ref, bf16[17,8,768]{2,1,0:T(8,128)(2,1)S(1)} %collective-permute-done.4.odd_even_ref, ...), custom_call_target="tpu_custom_call" | custom-call | flops 1000000 | bytes 100000 | tf_op jit(solution)/shard_map/pallas_call | solution.py:48
  24.8 0.0 collective-permute-done.halo_ref
  24.8 3.8 %shard_map.71 = bf16[16,64,768]{2,1,0:T(8,128)(2,1)} custom-call(bf16[8,48,768]{2,1,0:T(8,128)(2,1)S(1)} %get-tuple-element.19.inner_ref, bf16[8,48,768]{2,1,0:T(8,128)(2,1)S(1)} %collective-permute-done.halo_ref, bf16[384,2304]{1,0:T(8,128)(2,1)S(1)} %shard_map.68.after_ref.own_ref, f32[16,128]{1,0:T(8,128)S(1)} %get-tuple-element.26.labels_ref, ...), custom_call_target="tpu_custom_call" | custom-call | flops 1000000 | bytes 100000 | tf_op jit(solution)/shard_map/pallas_call | solution.py:48
Async XLA Ops:
  0.0 6.6 %copy-start = (bf16[768,2304]{1,0:T(8,128)(2,1)S(1)}, bf16[768,2304]{1,0:T(8,128)(2,1)}, u32[]{:S(2)}) copy-start(bf16[768,2304]{1,0:T(8,128)(2,1)} %qkv_weight_ref.9) | copy-start | bytes 10616836
  0.0 6.6 %copy-start.1 = (bf16[768,768]{1,0:T(8,128)(2,1)S(1)}, bf16[768,768]{1,0:T(8,128)(2,1)}, u32[]{:S(2)}) copy-start(bf16[768,768]{1,0:T(8,128)(2,1)} %out_weight_ref.7) | copy-start | bytes 3538948
  0.0 10.0 %collective-permute-start.2 = (s32[16,64]{1,0:T(8,128)}, s32[16,64]{1,0:T(8,128)S(1)}, u32[]{:S(2)}, u32[]{:S(2)}) collective-permute-start(s32[16,64]{1,0:T(8,128)} %label_ref.1), channel_id=1, source_target_pairs={{1,0},{0,1},{3,2},{2,3},{5,4},{4,5},{7,6},{6,7},{9,8},{8,9},{11,10... | collective-permute-start | bytes 12296 | tf_op jit(solution)/shard_map/ppermute | solution.py:30
  3.0 1.4 %copy-start.2 = (bf16[16,64,768]{2,1,0:T(8,128)(2,1)S(1)}, bf16[16,64,768]{2,1,0:T(8,128)(2,1)}, u32[]{:S(2)}) copy-start(bf16[16,64,768]{2,1,0:T(8,128)(2,1)} %tokens_ref.1) | copy-start | bytes 4718596
  4.4 2.2 %copy-start.3 = (s32[128,128]{1,0:T(8,128)S(1)}, s32[128,128]{1,0:T(8,128)}, u32[]{:S(2)}) copy-start(s32[128,128]{1,0:T(8,128)} %index_ref.1) | copy-start | bytes 196612
  4.4 2.2 %copy-start.4 = (f32[465,6]{0,1:T(8,128)S(1)}, f32[465,6]{0,1:T(8,128)}, u32[]{:S(2)}) copy-start(f32[465,6]{0,1:T(8,128)} %param.9) | copy-start | bytes 33484
  4.4 2.2 %copy-start.5 = (s32[16,64]{1,0:T(8,128)S(1)}, s32[16,64]{1,0:T(8,128)}, u32[]{:S(2)}) copy-start(s32[16,64]{1,0:T(8,128)} %label_ref.1) | copy-start | bytes 12292
  4.5 10.4 %collective-permute-start.1 = (bf16[8,16,768]{2,1,0:T(8,128)(2,1)S(1)}, bf16[8,16,768]{2,1,0:T(8,128)(2,1)S(1)}, u32[]{:S(2)}, u32[]{:S(2)}) collective-permute-start(bf16[8,16,768]{2,1,0:T(8,128)(2,1)S(1)} %get-tuple-element.20), channel_id=1, source_target_pairs={{1,0},{0,1},{3,2},{2,3},{5,4},{4,5},{7,6},{6,7},{9,8},{8,9},{11,10... | collective-permute-start | bytes 589832 | tf_op jit(solution)/shard_map/ppermute | solution.py:30
  4.7 20.1 %collective-permute-start = (bf16[8,48,768]{2,1,0:T(8,128)(2,1)S(1)}, bf16[8,48,768]{2,1,0:T(8,128)(2,1)S(1)}, u32[]{:S(2)}, u32[]{:S(2)}) collective-permute-start(bf16[8,48,768]{2,1,0:T(8,128)(2,1)S(1)} %get-tuple-element.19.inner_ref), channel_id=1, source_target_pairs={{1,0},{0,1},{3,2},{2,3},{5,4},{4,5},{7,6},{6,7},{9,8},{8,9},{11,10... | collective-permute-start | bytes 1769480 | tf_op jit(solution)/shard_map/ppermute | solution.py:30
  10.2 8.8 %collective-permute-start.3 = (bf16[17,8,768]{2,1,0:T(8,128)(2,1)S(1)}, bf16[17,8,768]{2,1,0:T(8,128)(2,1)S(1)}, u32[]{:S(2)}, u32[]{:S(2)}) collective-permute-start(bf16[17,8,768]{2,1,0:T(8,128)(2,1)S(1)} %get-tuple-element.24.after_ref), channel_id=1, source_target_pairs={{0,2},{2,0},{4,6},{6,4},{8,10},{10,8},{12,14},{14,12},{16,18},{18,... | collective-permute-start | bytes 626696 | tf_op jit(solution)/shard_map/ppermute | solution.py:44
  10.3 8.7 %collective-permute-start.4 = (bf16[17,8,768]{2,1,0:T(8,128)(2,1)S(1)}, bf16[17,8,768]{2,1,0:T(8,128)(2,1)S(1)}, u32[]{:S(2)}, u32[]{:S(2)}) collective-permute-start(bf16[17,8,768]{2,1,0:T(8,128)(2,1)S(1)} %get-tuple-element.28), channel_id=1, source_target_pairs={{0,30},{2,4},{4,2},{6,8},{8,6},{10,12},{12,10},{14,16},{16,14},{18... | collective-permute-start | bytes 626696 | tf_op jit(solution)/shard_map/ppermute | solution.py:43
  15.0 6.0 %collective-permute-start.5 = (bf16[8,8,768]{2,1,0:T(8,128)(2,1)S(1)}, bf16[8,8,768]{2,1,0:T(8,128)(2,1)S(1)}, u32[]{:S(2)}, u32[]{:S(2)}) collective-permute-start(bf16[8,8,768]{2,1,0:T(8,128)(2,1)S(1)} %get-tuple-element.25.after_ref), channel_id=1, source_target_pairs={{0,2},{2,0},{4,6},{6,4},{8,10},{10,8},{12,14},{14,12},{16,18},{18,... | collective-permute-start | bytes 294920 | tf_op jit(solution)/shard_map/ppermute | solution.py:44
  15.1 6.8 %collective-permute-start.6 = (bf16[8,8,768]{2,1,0:T(8,128)(2,1)S(1)}, bf16[8,8,768]{2,1,0:T(8,128)(2,1)S(1)}, u32[]{:S(2)}, u32[]{:S(2)}) collective-permute-start(bf16[8,8,768]{2,1,0:T(8,128)(2,1)S(1)} %get-tuple-element.29), channel_id=1, source_target_pairs={{0,30},{2,4},{4,2},{6,8},{8,6},{10,12},{12,10},{14,16},{16,14},{18... | collective-permute-start | bytes 294920 | tf_op jit(solution)/shard_map/ppermute | solution.py:43

commit v4 on v3

--- a/solution.py
+++ b/solution.py
@@ -30,18 +30,18 @@
     return lax.ppermute(block, axis, route)
 
 
-def lat_exchange(message):
+def lat_exchange(message, cut):
     if lax.axis_size("lat") == 2:
         return moved(message, "lat", 1)
-    return jnp.concatenate([moved(message[:HALF_LAT], "lat", -1), moved(message[HALF_LAT:], "lat", 1)], axis=0)
-
-
-def lon_exchange(even_odd, odd_even):
+    return jnp.concatenate([moved(message[:cut], "lat", -1), moved(message[cut:], "lat", 1)], axis=0)
+
+
+def lon_exchange(odd_even, even_odd):
     count = lax.axis_size("lon")
     first = [(i, i ^ 1) for i in range(count)]
     second = [(i, (i + 1 if i % 2 else i - 1) % count) for i in range(count)]
-    odd_even = lax.ppermute(odd_even, "lon", second)
-    return lax.ppermute(even_odd, "lon", first), odd_even
+    even_odd = lax.ppermute(even_odd, "lon", first)
+    return lax.ppermute(odd_even, "lon", second), even_odd
 
 
 def run(kernel, outs, operands, scratch=(), specs=None, out_specs=None, mib=4, flops=10**6):
@@ -82,22 +82,32 @@
     return result
 
 
-def message_kernel(tokens_ref, ends_ref, inner_ref, middle_ref, columns_ref):
-    row_count = tokens_ref.shape[0]
+def label_kernel(strips, label_ref, rows_ref):
+    rows_ref[...] = label_rows(label_ref[...], strips)
+
+
+def label_message(rows, feature):
+    rows = jnp.concatenate([rows, jnp.zeros((HALF_LON - rows.shape[0], WIN), F32)], axis=0) if rows.shape[0] < HALF_LON else rows
+    return jnp.concatenate([rows, jnp.zeros((HALF_LON, feature - WIN), F32)], axis=1).astype(BF16)
+
+
+def message_kernel(tokens_ref, rows_ref, ends_ref, inner_ref, middle_ref, columns_ref):
+    row_count, _, feature = tokens_ref.shape
     for row in range(row_count):
         floats = tokens_ref[row].astype(F32)
-        columns = jnp.concatenate([floats[:HALF_LON], floats[-HALF_LON:]], axis=0).astype(BF16)
+        columns_ref[row] = jnp.concatenate([floats[:HALF_LON], floats[-HALF_LON:]], axis=0).astype(BF16)
         inner = floats[HALF_LON:-HALF_LON].astype(BF16)
-        columns_ref[row] = columns
         if HALF_LAT <= row < row_count - HALF_LAT:
             middle_ref[row - HALF_LAT] = inner
         else:
             at = row if row < HALF_LAT else row - row_count + WLAT
-            ends_ref[at] = columns
+            ends_ref[2 * at] = floats[:HALF_LON].astype(BF16)
+            ends_ref[2 * at + 1] = floats[-HALF_LON:].astype(BF16)
             inner_ref[at] = inner
-
-
-def column_kernel(strips, columns_ref, rows_ref, above_ref, even_odd_ref, odd_even_ref, labels_ref):
+    ends_ref[2 * WLAT] = label_message(rows_ref[...], feature)
+
+
+def column_kernel(columns_ref, rows_ref, even_odd_ref, odd_even_ref):
     row_count, _, feature = columns_ref.shape
     odd = lax.axis_index("lon") % 2 == 1
     for row in range(row_count):
@@ -105,22 +115,23 @@
         left, right = floats[:HALF_LON], floats[HALF_LON:]
         even_odd_ref[row] = jnp.where(odd, left, right).astype(BF16)
         odd_even_ref[row] = jnp.where(odd, right, left).astype(BF16)
-    labels = jnp.concatenate([label_rows(above_ref[above_ref.shape[0] - WLAT :, :], strips), rows_ref[...]], axis=0)
-    labels = jnp.concatenate([labels, jnp.zeros((16 - labels.shape[0], WIN), F32)], axis=0)
-    labels_ref[...] = labels
-    filler = jnp.zeros((HALF_LON, feature - 2 * WIN), F32)
-    message = jnp.concatenate([labels[:8], labels[8:], filler], axis=1).astype(BF16)
+    message = label_message(rows_ref[...], feature)
     even_odd_ref[row_count] = message
     odd_even_ref[row_count] = message
 
 
-def corner_message_kernel(ends_ref, after_ref, even_odd_ref, odd_even_ref):
+def corner_message_kernel(strips, ends_ref, rows_ref, after_ref, even_odd_ref, odd_even_ref, labels_ref):
     odd = lax.axis_index("lon") % 2 == 1
     for row in range(WLAT):
-        floats = ends_ref[row].astype(F32)
-        left, right = floats[:HALF_LON], floats[HALF_LON:]
+        left, right = ends_ref[2 * row].astype(F32), ends_ref[2 * row + 1].astype(F32)
         even_odd_ref[row] = jnp.where(odd, left, right).astype(BF16)
         odd_even_ref[row] = jnp.where(odd, right, left).astype(BF16)
+    own = rows_ref[...]
+    above = ends_ref[2 * WLAT].astype(F32)[own.shape[0] - strips : own.shape[0], :WIN]
+    labels_ref[...] = jnp.concatenate([above, own, jnp.zeros((16 - strips - own.shape[0], WIN), F32)], axis=0)
+    message = label_message(above, ends_ref.shape[-1])
+    even_odd_ref[WLAT] = message
+    odd_even_ref[WLAT] = message
 
 
 def halo_row(row, row_count):
@@ -175,8 +186,8 @@
     return store
 
 
-def inner_kernel(strips, middle_ref, label_ref, table_ref, index_ref, qkv_weight_ref, out_weight_ref,
-                 out_ref, bias_ref, rows_ref, cells_ref, qkv_ref, attended_ref, wide_ref):
+def inner_kernel(strips, middle_ref, rows_ref, table_ref, index_ref, qkv_weight_ref, out_weight_ref,
+                 after_ref, out_ref, bias_ref, cells_ref, qkv_ref, attended_ref, wide_ref):
     feature = middle_ref.shape[-1]
     floats = []
     for strip in range(strips - 1):
@@ -187,8 +198,7 @@
     wide_ref[: table_ref.shape[0], : table_ref.shape[1]] = table_ref[...]
     qkv_ref[...] = project(cells_ref[...], qkv_weight_ref, 0, 3 * feature)
     look_up(wide_ref, index_ref, bias_ref)
-    labels = label_rows(label_ref[...], strips)
-    rows_ref[...] = labels
+    labels = rows_ref[...]
     label_columns = labels.T
     entries = []
     for strip in range(strips - 1):
@@ -283,7 +293,7 @@
     return blocks
 
 
-def swapped(even_odd_ref, odd_even_ref):
+def swapped(odd_even_ref, even_odd_ref):
     odd = lax.axis_index("lon") % 2 == 1
 
     def row_of(row, side):
@@ -297,17 +307,15 @@
     return floats[HALF_LON:] if side else floats[:HALF_LON]
 
 
-def left_labels_of(received, row):
-    message = received(row, 0)
-    return jnp.concatenate([message[:, :WIN], message[:, WIN : 2 * WIN]], axis=0)
-
-
-def between_kernel(strips, columns_ref, even_odd_ref, odd_even_ref, labels_ref, bias_ref, qkv_weight_ref, out_weight_ref, inner_ref,
-                   after_ref, out_ref, left_ref, *scratch):
+def left_labels_of(above, own):
+    return jnp.concatenate([above, own, jnp.zeros((16 - above.shape[0] - own.shape[0], WIN), F32)], axis=0)
+
+
+def between_kernel(strips, columns_ref, odd_even_ref, even_odd_ref, labels_ref, bias_ref, qkv_weight_ref, out_weight_ref, inner_ref,
+                   after_ref, out_ref, *scratch):
     row_count = columns_ref.shape[0]
-    received = swapped(even_odd_ref, odd_even_ref)
-    left_labels = left_labels_of(received, row_count)
-    left_ref[...] = left_labels
+    received = swapped(odd_even_ref, even_odd_ref)
+    left_labels = left_labels_of(jnp.zeros((strips, WIN), F32), received(row_count, 0)[:, :WIN])
     blocks = side_blocks(
         side_windows(row_count // WLAT, True), row_count // WLAT, strips,
         lambda row, side: half_of(columns_ref[row - HALF_LAT].astype(F32), side),
@@ -319,26 +327,28 @@
         out_ref[row] = jnp.concatenate([blocks[1, 0, row]] + middle + [blocks[1, 1, row]], axis=0).astype(BF16)
 
 
-def corner_kernel(strips, columns_ref, even_odd_ref, odd_even_ref, corner_even_odd_ref, corner_odd_even_ref, ends_ref, labels_ref,
-                  left_ref, bias_ref, qkv_weight_ref, out_weight_ref, corner_ref, *scratch):
+def corner_kernel(strips, columns_ref, odd_even_ref, even_odd_ref, corner_odd_even_ref, corner_even_odd_ref, ends_ref, labels_ref,
+                  bias_ref, qkv_weight_ref, out_weight_ref, corner_ref, *scratch):
     row_count = columns_ref.shape[0]
     bands = row_count // WLAT
-    received = swapped(even_odd_ref, odd_even_ref)
-    received_corner = swapped(corner_even_odd_ref, corner_odd_even_ref)
+    received = swapped(odd_even_ref, even_odd_ref)
+    received_corner = swapped(corner_odd_even_ref, corner_even_odd_ref)
+    left_labels = left_labels_of(received_corner(WLAT, 0)[:strips, :WIN], received(row_count, 0)[:, :WIN])
 
     def inside(row):
         return HALF_LAT <= row < row_count + HALF_LAT
 
     def own_of(row, side):
-        floats = columns_ref[row - HALF_LAT] if inside(row) else ends_ref[halo_row(row, row_count)]
-        return half_of(floats.astype(F32), side)
+        if inside(row):
+            return half_of(columns_ref[row - HALF_LAT].astype(F32), side)
+        return ends_ref[2 * halo_row(row, row_count) + side].astype(F32)
 
     def halo_of(row, side):
         return received(row - HALF_LAT, side) if inside(row) else received_corner(halo_row(row, row_count), side)
 
     blocks = side_blocks(
         side_windows(bands, False), bands, strips, own_of, halo_of,
-        left_ref[...], labels_ref[...], bias_ref, qkv_weight_ref, out_weight_ref, *scratch,
+        left_labels, labels_ref[...], bias_ref, qkv_weight_ref, out_weight_ref, *scratch,
     )
     for band, first in ((0, 0), (bands, HALF_LAT)):
         for row in range(HALF_LAT):
@@ -348,7 +358,7 @@
 def last_kernel(strips, inner_ref, halo_ref, own_ref, labels_ref, bias_ref, qkv_weight_ref, out_weight_ref, corner_ref, between_ref,
                 out_ref, cells_ref, keys_ref, attended_ref, block_ref, sems):
     row_count, column_count, feature = out_ref.shape
-    copies = [pltpu.make_async_copy(between_ref, out_ref.at[pl.ds(HALF_LAT, row_count - WLAT)], sems.at[2])]
+    copies = [pltpu.make_async_copy(between_ref, out_ref.at[pl.ds(HALF_LAT, row_count - WLAT)], sems.at[WLAT])]
     copies[0].start()
     bands = row_count // WLAT
     half = HALF_LAT * WLON
@@ -390,9 +400,8 @@
             middle = [branch[strip * half + row * WLON : strip * half + (row + 1) * WLON] for strip in range(strips - 1)]
             middle = inner_ref[at].astype(F32) + jnp.concatenate(middle, axis=0)
             block_ref[at] = jnp.concatenate([corner[:HALF_LON], middle, corner[HALF_LON:]], axis=0).astype(BF16)
-        source = block_ref.at[pl.ds(side * HALF_LAT, HALF_LAT)]
-        copies.append(pltpu.make_async_copy(source, out_ref.at[pl.ds(first, HALF_LAT)], sems.at[side]))
-        copies[-1].start()
+            copies.append(pltpu.make_async_copy(block_ref.at[at], out_ref.at[first + row], sems.at[at]))
+            copies[-1].start()
     for copy in copies:
         copy.wait()
 
@@ -404,40 +413,45 @@
     inner_columns = column_count - WLON
     dma = pltpu.SemaphoreType.DMA
 
-    label_above = moved(region_label, "lat", 1)
+    (label_own,) = run(
+        functools.partial(label_kernel, strips), [shape(bands * strips, WIN, dtype=F32)], [region_label], flops=5 * 10**9
+    )
     ends, inner_rows, middle, columns = run(
         message_kernel,
         [
-            shape(WLAT, WLON, feature),
+            shape(2 * WLAT + 1, HALF_LON, feature),
             shape(WLAT, inner_columns, feature),
             shape(row_count - WLAT, inner_columns, feature),
             shape(row_count, WLON, feature),
         ],
-        [tokens],
+        [tokens, label_own],
         flops=5 * 10**9,
     )
-    ends_received = lat_exchange(ends)
-    rows_received = lat_exchange(inner_rows)
+    ends_received = lat_exchange(ends, 2 * HALF_LAT)
+    rows_received = lat_exchange(inner_rows, HALF_LAT)
+    message = shape(row_count + 1, HALF_LON, feature)
+    columns_sent = run(column_kernel, [message, message], [columns, label_own], flops=2 * 10**10)
+    columns_received = lon_exchange(*columns_sent[::-1])
 
     inner_cells = (strips - 1) * WIN
-    inner, bias, label_own = run(
+    inner, bias = run(
         functools.partial(inner_kernel, strips),
-        [shape(inner_cells, feature), shape(HEADS, WIN, WIN, dtype=F32), shape(bands * strips, WIN, dtype=F32)],
-        [middle, region_label, bias_table.T, position_index, qkv_weight, out_weight],
+        [shape(inner_cells, feature), shape(HEADS, WIN, WIN, dtype=F32)],
+        [middle, label_own, bias_table.T, position_index, qkv_weight, out_weight, columns_sent[0]],
+        specs=[VMEM] * 6 + [ANY],
         scratch=[pltpu.VMEM((inner_cells, width * feature), BF16) for width in (1, 3, 1)]
         + [pltpu.VMEM((8, -(-bias_table.shape[0] // 128) * 128), F32)],
         mib=12,
-        flops=2 * 10**10,
-    )
-    message = shape(row_count + 1, HALF_LON, feature)
-    *columns_sent, labels = run(
-        functools.partial(column_kernel, strips), [message, message, shape(16, WIN, dtype=F32)], [columns, label_own, label_above]
-    )
-    columns_received = lon_exchange(*columns_sent)
-
-    message = shape(WLAT, HALF_LON, feature)
-    corners = run(corner_message_kernel, [message, message], [ends_received, columns_sent[0]], specs=[VMEM, ANY])
-    corners_received = lon_exchange(*corners)
+        flops=5 * 10**9,
+    )
+    message = shape(WLAT + 1, HALF_LON, feature)
+    *corners, labels = run(
+        functools.partial(corner_message_kernel, strips),
+        [message, message, shape(16, WIN, dtype=F32)],
+        [ends_received, label_own, inner],
+        specs=[VMEM, VMEM, ANY],
+    )
+    corners_received = lon_exchange(*corners[::-1])
     row_cells = (strips - 1) * WIN
     (row_qkv,) = run(
         functools.partial(rows_kernel, strips),
@@ -455,9 +469,9 @@
         return cells, every, [pltpu.VMEM((count, width * feature), BF16) for count, width in sizes]
 
     cells, every, scratch = side_scratch(True)
-    between, label_left = run(
+    (between,) = run(
         functools.partial(between_kernel, strips),
-        [shape(row_count - WLAT, column_count, feature), shape(16, WIN, dtype=F32)],
+        [shape(row_count - WLAT, column_count, feature)],
         [columns, *columns_received, labels, bias, qkv_weight, out_weight, inner, row_qkv],
         specs=[VMEM] * 8 + [ANY],
         scratch=scratch,
@@ -467,7 +481,7 @@
     (corner,) = run(
         functools.partial(corner_kernel, strips),
         [shape(WLAT, WLON, feature)],
-        [columns, *columns_received, *corners_received, ends_received, labels, label_left, bias, qkv_weight, out_weight],
+        [columns, *columns_received, *corners_received, ends_received, labels, bias, qkv_weight, out_weight],
         scratch=scratch,
         mib=12,
     )
@@ -478,7 +492,7 @@
         out_specs=[HBM],
         mib=12,
         scratch=[pltpu.VMEM((row_cells, width * feature), BF16) for width in (1, 2, 1)]
-        + [pltpu.VMEM((WLAT, column_count, feature), BF16), dma((3,))],
+        + [pltpu.VMEM((WLAT, column_count, feature), BF16), dma((WLAT + 1,))],
     )
     return out
 

time: 28.8 us -> 26.4 us (0.917)
  starting transfers between devices: 11.9 us -> 9.2 us
  waiting for transfers between devices: 0.88 us -> 1.6 us
  Pallas kernels: 14.3 us -> 14 us
    ppermute x3 -> x2, starting transfers between devices: 5.06 us -> 3.11 us  [moved(): return lax.ppermute(block, axis, route)]
    ppermute x4, starting transfers between devices: 6.85 us -> 6.09 us  [the longest x2 6.09 us: lon_exchange(): return (lax.ppermute(odd_even, 'lon', second), even_odd)]
    ppermute x3 -> x2, waiting for transfers between devices: 0.01 us -> 0.61 us  [moved(): return lax.ppermute(block, axis, route)]
    pallas_call x8 -> x9, Pallas kernels: 14.3 us -> 14 us  [run(): pl.pallas_call(kernel, out_shape=outs, in_specs=specs or [VMEM] * len(ope...]
  transfers between devices with their start and end apart: 7 -> 6, of which waited for: 1 -> 2; matrix products, arithmetic and copies ran while one was open for 0% -> 0% of each run, Pallas kernels for 37% -> 38%
where the time goes in v4:
time: 26.4 us; the launch traced here: 26.2 us
  Pallas kernels  14 us (53%)
  starting transfers between devices  9.2 us (35%)
  waiting for transfers between devices  1.6 us (6%)
  local copies, waits for them, and re-layouts  1.3 us (5%)
    pallas_call x9, Pallas kernels, run(): pl.pallas_call(kernel, out_shape=outs, in_specs=specs or [VMEM] * len(ope...  14 us
    ppermute x2, starting transfers between devices, lon_exchange(): return (lax.ppermute(odd_even, 'lon', second), even_odd)  6.09 us
    ppermute x2, starting transfers between devices, moved(): return lax.ppermute(block, axis, route)  3.11 us
    unnamed x12, local copies, waits for them, and re-layouts  1.3 us
    ppermute x2, waiting for transfers between devices, lon_exchange(): return (lax.ppermute(odd_even, 'lon', second), even_odd)  0.98 us
    ppermute x2, waiting for transfers between devices, moved(): return lax.ppermute(block, axis, route)  0.61 us
  transfers between devices with their start and end apart: 6, of which 2 were waited for; matrix products, arithmetic and copies ran while one was open for 0% of the time, Pallas kernels for 38%

profile of v4, /device:TPU:0, one launch (start us, length us, event | category | flops | bytes accessed | tf_op | source)
XLA Modules:
  0.0 26.2 jit_solution(2856751929946633042)
XLA Ops:
  0.0 0.0 copy-start.2
  0.0 0.0 copy-start.5
  0.0 0.8 %copy-done.5 = s32[16,64]{1,0:T(8,128)S(1)} copy-done((s32[16,64]{1,0:T(8,128)S(1)}, s32[16,64]{1,0:T(8,128)}, u32[]{:S(2)}) %copy-start.5) | copy-done | bytes 4120
  0.8 0.1 shard_map.64.rows_ref
  1.0 0.5 %copy-done.2 = bf16[16,64,768]{2,1,0:T(8,128)(2,1)S(1)} copy-done((bf16[16,64,768]{2,1,0:T(8,128)(2,1)S(1)}, bf16[16,64,768]{2,1,0:T(8,128)(2,1)}, u32[]{:S(2)}) %copy-start.2) | copy-done | bytes 1572888
  1.4 0.1 shard_map.65
  1.5 3.0 %collective-permute-start.1 = (bf16[17,8,768]{2,1,0:T(8,128)(2,1)S(1)}, bf16[17,8,768]{2,1,0:T(8,128)(2,1)S(1)}, u32[]{:S(2)}, u32[]{:S(2)}) collective-permute-start(bf16[17,8,768]{2,1,0:T(8,128)(2,1)S(1)} %get-tuple-element.17), channel_id=1, source_target_pairs={{1,0},{0,1},{3,2},{2,3},{5,4},{4,5},{7,6},{6,7},{9,8},{8,9},{11,10... | collective-permute-start | bytes 626696 | tf_op jit(solution)/shard_map/ppermute | solution.py:30
  4.6 0.1 collective-permute-start
  4.7 0.0 copy-start
  4.7 0.0 copy-start.1
  4.7 0.0 copy-start.3
  4.7 0.0 copy-start.4
  4.7 0.1 shard_map.66
  4.8 3.9 %collective-permute-start.2 = (bf16[17,8,768]{2,1,0:T(8,128)(2,1)S(1)}, bf16[17,8,768]{2,1,0:T(8,128)(2,1)S(1)}, u32[]{:S(2)}, u32[]{:S(2)}) collective-permute-start(bf16[17,8,768]{2,1,0:T(8,128)(2,1)S(1)} %get-tuple-element.25), channel_id=1, source_target_pairs={{0,30},{2,4},{4,2},{6,8},{8,6},{10,12},{12,10},{14,16},{16,14},{18... | collective-permute-start | bytes 626696 | tf_op jit(solution)/shard_map/ppermute | solution.py:44
  8.7 0.0 collective-permute-start.3
  8.7 0.0 copy-done
  8.7 0.0 copy-done.1
  8.7 0.0 copy-done.3
  8.7 0.0 copy-done.4
  8.7 3.2 %shard_map.67 = (bf16[384,768]{1,0:T(8,128)(2,1)S(1)}, f32[6,128,128]{2,1,0:T(8,128)S(1)}) custom-call(bf16[8,48,768]{2,1,0:T(8,128)(2,1)S(1)} %get-tuple-element.18.middle_ref, f32[8,128]{1,0:T(8,128)S(1)} %shard_map.64.rows_ref, f32[6,465]{1,0:T(8,128)S(1)} %bitcast.1, s32[128,128]{1,0:T(8,128)S(1)} %copy-done.3, bf16[768,2304]{1,0:T(8,128)(2,1)S(1)} %copy-done, ...), custom_call_target="tpu_custom_call" | custom-call | flops 5000000000 | bytes 100000 | tf_op jit(solution)/shard_map/pallas_call | solution.py:48
  11.9 0.0 collective-permute-done.1.ends_ref
  11.9 0.1 shard_map.68
  12.0 2.2 %collective-permute-start.4 = (bf16[9,8,768]{2,1,0:T(8,128)(2,1)S(1)}, bf16[9,8,768]{2,1,0:T(8,128)(2,1)S(1)}, u32[]{:S(2)}, u32[]{:S(2)}) collective-permute-start(bf16[9,8,768]{2,1,0:T(8,128)(2,1)S(1)} %get-tuple-element.26), channel_id=1, source_target_pairs={{0,30},{2,4},{4,2},{6,8},{8,6},{10,12},{12,10},{14,16},{16,14},{18... | collective-permute-start | bytes 331784 | tf_op jit(solution)/shard_map/ppermute | solution.py:44
  14.2 0.0 collective-permute-start.5
  14.2 1.8 %shard_map.69.after_ref.own_ref = bf16[384,2304]{1,0:T(8,128)(2,1)S(1)} custom-call(bf16[8,48,768]{2,1,0:T(8,128)(2,1)S(1)} %get-tuple-element.16.inner_ref, bf16[768,2304]{1,0:T(8,128)(2,1)S(1)} %copy-done, bf16[9,8,768]{2,1,0:T(8,128)(2,1)S(1)} %get-tuple-element.22.after_ref), custom_call_target="tpu_custom_call" | custom-call | flops 1000000 | bytes 100000 | tf_op jit(solution)/shard_map/pallas_call | solution.py:48
  16.0 0.0 collective-permute-done.2.odd_even_ref
  16.0 0.0 collective-permute-done.3.even_odd_ref
  16.0 1.9 %shard_map.71.between_ref = bf16[8,64,768]{2,1,0:T(8,128)(2,1)S(1)} custom-call(bf16[16,16,768]{2,1,0:T(8,128)(2,1)S(1)} %get-tuple-element.19.columns_ref, bf16[17,8,768]{2,1,0:T(8,128)(2,1)S(1)} %collective-permute-done.2.odd_even_ref, bf16[17,8,768]{2,1,0:T(8,128)(2,1)S(1)} %collective-permute-done.3.even_odd_ref, ...), custom_call_target="tpu_custom_call" | custom-call | flops 1000000 | bytes 100000 | tf_op jit(solution)/shard_map/pallas_call | solution.py:48
  17.9 1.0 %collective-permute-done.4.corner_odd_even_ref = bf16[9,8,768]{2,1,0:T(8,128)(2,1)S(1)} collective-permute-done((bf16[9,8,768]{2,1,0:T(8,128)(2,1)S(1)}, bf16[9,8,768]{2,1,0:T(8,128)(2,1)S(1)}, u32[]{:S(2)}, u32[]{:S(2)}) %collective-permute-start.4) | collective-permute-done | bytes 110624 | tf_op jit(solution)/shard_map/ppermute | solution.py:44
  18.9 0.0 collective-permute-done.5.corner_even_odd_ref
  18.9 2.9 %shard_map.70.corner_ref = bf16[8,16,768]{2,1,0:T(8,128)(2,1)S(1)} custom-call(bf16[16,16,768]{2,1,0:T(8,128)(2,1)S(1)} %get-tuple-element.19.columns_ref, bf16[17,8,768]{2,1,0:T(8,128)(2,1)S(1)} %collective-permute-done.2.odd_even_ref, bf16[17,8,768]{2,1,0:T(8,128)(2,1)S(1)} %collective-permute-done.3.even_odd_ref, ...), custom_call_target="tpu_custom_call" | custom-call | flops 1000000 | bytes 100000 | tf_op jit(solution)/shard_map/pallas_call | solution.py:48
  21.8 0.6 %collective-permute-done.halo_ref = bf16[8,48,768]{2,1,0:T(8,128)(2,1)S(1)} collective-permute-done((bf16[8,48,768]{2,1,0:T(8,128)(2,1)S(1)}, bf16[8,48,768]{2,1,0:T(8,128)(2,1)S(1)}, u32[]{:S(2)}, u32[]{:S(2)}) %collective-permute-start) | collective-permute-done | bytes 589856 | tf_op jit(solution)/shard_map/ppermute | solution.py:30
  22.4 3.9 %shard_map.72 = bf16[16,64,768]{2,1,0:T(8,128)(2,1)} custom-call(bf16[8,48,768]{2,1,0:T(8,128)(2,1)S(1)} %get-tuple-element.16.inner_ref, bf16[8,48,768]{2,1,0:T(8,128)(2,1)S(1)} %collective-permute-done.halo_ref, bf16[384,2304]{1,0:T(8,128)(2,1)S(1)} %shard_map.69.after_ref.own_ref, f32[16,128]{1,0:T(8,128)S(1)} %get-tuple-element.23.labels_ref, ...), custom_call_target="tpu_custom_call" | custom-call | flops 1000000 | bytes 100000 | tf_op jit(solution)/shard_map/pallas_call | solution.py:48
Async XLA Ops:
  0.0 1.4 %copy-start.2 = (bf16[16,64,768]{2,1,0:T(8,128)(2,1)S(1)}, bf16[16,64,768]{2,1,0:T(8,128)(2,1)}, u32[]{:S(2)}) copy-start(bf16[16,64,768]{2,1,0:T(8,128)(2,1)} %tokens_ref.1) | copy-start | bytes 4718596
  0.0 0.8 %copy-start.5 = (s32[16,64]{1,0:T(8,128)S(1)}, s32[16,64]{1,0:T(8,128)}, u32[]{:S(2)}) copy-start(s32[16,64]{1,0:T(8,128)} %label_ref.1) | copy-start | bytes 12292
  1.5 10.4 %collective-permute-start.1 = (bf16[17,8,768]{2,1,0:T(8,128)(2,1)S(1)}, bf16[17,8,768]{2,1,0:T(8,128)(2,1)S(1)}, u32[]{:S(2)}, u32[]{:S(2)}) collective-permute-start(bf16[17,8,768]{2,1,0:T(8,128)(2,1)S(1)} %get-tuple-element.17), channel_id=1, source_target_pairs={{1,0},{0,1},{3,2},{2,3},{5,4},{4,5},{7,6},{6,7},{9,8},{8,9},{11,10... | collective-permute-start | bytes 626696 | tf_op jit(solution)/shard_map/ppermute | solution.py:30
  4.6 17.8 %collective-permute-start = (bf16[8,48,768]{2,1,0:T(8,128)(2,1)S(1)}, bf16[8,48,768]{2,1,0:T(8,128)(2,1)S(1)}, u32[]{:S(2)}, u32[]{:S(2)}) collective-permute-start(bf16[8,48,768]{2,1,0:T(8,128)(2,1)S(1)} %get-tuple-element.16.inner_ref), channel_id=1, source_target_pairs={{1,0},{0,1},{3,2},{2,3},{5,4},{4,5},{7,6},{6,7},{9,8},{8,9},{11,10... | collective-permute-start | bytes 1769480 | tf_op jit(solution)/shard_map/ppermute | solution.py:30
  4.7 4.0 %copy-start = (bf16[768,2304]{1,0:T(8,128)(2,1)S(1)}, bf16[768,2304]{1,0:T(8,128)(2,1)}, u32[]{:S(2)}) copy-start(bf16[768,2304]{1,0:T(8,128)(2,1)} %qkv_weight_ref.9) | copy-start | bytes 10616836
  4.7 4.0 %copy-start.1 = (bf16[768,768]{1,0:T(8,128)(2,1)S(1)}, bf16[768,768]{1,0:T(8,128)(2,1)}, u32[]{:S(2)}) copy-start(bf16[768,768]{1,0:T(8,128)(2,1)} %out_weight_ref.7) | copy-start | bytes 3538948
  4.7 4.0 %copy-start.3 = (s32[128,128]{1,0:T(8,128)S(1)}, s32[128,128]{1,0:T(8,128)}, u32[]{:S(2)}) copy-start(s32[128,128]{1,0:T(8,128)} %index_ref.1) | copy-start | bytes 196612
  4.7 4.0 %copy-start.4 = (f32[465,6]{0,1:T(8,128)S(1)}, f32[465,6]{0,1:T(8,128)}, u32[]{:S(2)}) copy-start(f32[465,6]{0,1:T(8,128)} %param.9) | copy-start | bytes 33484
  4.8 11.2 %collective-permute-start.2 = (bf16[17,8,768]{2,1,0:T(8,128)(2,1)S(1)}, bf16[17,8,768]{2,1,0:T(8,128)(2,1)S(1)}, u32[]{:S(2)}, u32[]{:S(2)}) collective-permute-start(bf16[17,8,768]{2,1,0:T(8,128)(2,1)S(1)} %get-tuple-element.25), channel_id=1, source_target_pairs={{0,30},{2,4},{4,2},{6,8},{8,6},{10,12},{12,10},{14,16},{16,14},{18... | collective-permute-start | bytes 626696 | tf_op jit(solution)/shard_map/ppermute | solution.py:44
  8.7 7.3 %collective-permute-start.3 = (bf16[17,8,768]{2,1,0:T(8,128)(2,1)S(1)}, bf16[17,8,768]{2,1,0:T(8,128)(2,1)S(1)}, u32[]{:S(2)}, u32[]{:S(2)}) collective-permute-start(bf16[17,8,768]{2,1,0:T(8,128)(2,1)S(1)} %get-tuple-element.20.after_ref), channel_id=1, source_target_pairs={{0,2},{2,0},{4,6},{6,4},{8,10},{10,8},{12,14},{14,12},{16,18},{18,... | collective-permute-start | bytes 626696 | tf_op jit(solution)/shard_map/ppermute | solution.py:43
  12.0 6.9 %collective-permute-start.4 = (bf16[9,8,768]{2,1,0:T(8,128)(2,1)S(1)}, bf16[9,8,768]{2,1,0:T(8,128)(2,1)S(1)}, u32[]{:S(2)}, u32[]{:S(2)}) collective-permute-start(bf16[9,8,768]{2,1,0:T(8,128)(2,1)S(1)} %get-tuple-element.26), channel_id=1, source_target_pairs={{0,30},{2,4},{4,2},{6,8},{8,6},{10,12},{12,10},{14,16},{16,14},{18... | collective-permute-start | bytes 331784 | tf_op jit(solution)/shard_map/ppermute | solution.py:44
  14.2 4.8 %collective-permute-start.5 = (bf16[9,8,768]{2,1,0:T(8,128)(2,1)S(1)}, bf16[9,8,768]{2,1,0:T(8,128)(2,1)S(1)}, u32[]{:S(2)}, u32[]{:S(2)}) collective-permute-start(bf16[9,8,768]{2,1,0:T(8,128)(2,1)S(1)} %get-tuple-element.22.after_ref), channel_id=1, source_target_pairs={{0,2},{2,0},{4,6},{6,4},{8,10},{10,8},{12,14},{14,12},{16,18},{18,... | collective-permute-start | bytes 331784 | tf_op jit(solution)/shard_map/ppermute | solution.py:43

commit v5 on v4

--- a/solution.py
+++ b/solution.py
@@ -86,9 +86,25 @@
     rows_ref[...] = label_rows(label_ref[...], strips)
 
 
-def label_message(rows, feature):
-    rows = jnp.concatenate([rows, jnp.zeros((HALF_LON - rows.shape[0], WIN), F32)], axis=0) if rows.shape[0] < HALF_LON else rows
-    return jnp.concatenate([rows, jnp.zeros((HALF_LON, feature - WIN), F32)], axis=1).astype(BF16)
+def put_cells(message_ref, row, cells):
+    groups = cells.shape[1] // WIN
+    for group in range(groups):
+        message_ref[row * groups + group] = cells[:, group * WIN : (group + 1) * WIN].astype(BF16)
+
+
+def cells_of(message_ref, row):
+    groups = HEADS * HEAD // WIN
+    return jnp.concatenate([message_ref[row * groups + group].astype(F32) for group in range(groups)], axis=1)
+
+
+def put_labels(message_ref, rows):
+    if rows.shape[0] < HALF_LON:
+        rows = jnp.concatenate([rows, jnp.zeros((HALF_LON - rows.shape[0], WIN), F32)], axis=0)
+    message_ref[message_ref.shape[0] - 1] = rows.astype(BF16)
+
+
+def labels_of(message_ref):
+    return message_ref[message_ref.shape[0] - 1].astype(F32)
 
 
 def message_kernel(tokens_ref, rows_ref, ends_ref, inner_ref, middle_ref, columns_ref):
@@ -101,37 +117,34 @@
             middle_ref[row - HALF_LAT] = inner
         else:
             at = row if row < HALF_LAT else row - row_count + WLAT
-            ends_ref[2 * at] = floats[:HALF_LON].astype(BF16)
-            ends_ref[2 * at + 1] = floats[-HALF_LON:].astype(BF16)
+            put_cells(ends_ref, 2 * at, floats[:HALF_LON])
+            put_cells(ends_ref, 2 * at + 1, floats[-HALF_LON:])
             inner_ref[at] = inner
-    ends_ref[2 * WLAT] = label_message(rows_ref[...], feature)
+    put_labels(ends_ref, rows_ref[...])
 
 
 def column_kernel(columns_ref, rows_ref, even_odd_ref, odd_even_ref):
-    row_count, _, feature = columns_ref.shape
     odd = lax.axis_index("lon") % 2 == 1
-    for row in range(row_count):
+    for row in range(columns_ref.shape[0]):
         floats = columns_ref[row].astype(F32)
         left, right = floats[:HALF_LON], floats[HALF_LON:]
-        even_odd_ref[row] = jnp.where(odd, left, right).astype(BF16)
-        odd_even_ref[row] = jnp.where(odd, right, left).astype(BF16)
-    message = label_message(rows_ref[...], feature)
-    even_odd_ref[row_count] = message
-    odd_even_ref[row_count] = message
+        put_cells(even_odd_ref, row, jnp.where(odd, left, right))
+        put_cells(odd_even_ref, row, jnp.where(odd, right, left))
+    put_labels(even_odd_ref, rows_ref[...])
+    put_labels(odd_even_ref, rows_ref[...])
 
 
 def corner_message_kernel(strips, ends_ref, rows_ref, after_ref, even_odd_ref, odd_even_ref, labels_ref):
     odd = lax.axis_index("lon") % 2 == 1
     for row in range(WLAT):
-        left, right = ends_ref[2 * row].astype(F32), ends_ref[2 * row + 1].astype(F32)
-        even_odd_ref[row] = jnp.where(odd, left, right).astype(BF16)
-        odd_even_ref[row] = jnp.where(odd, right, left).astype(BF16)
+        left, right = cells_of(ends_ref, 2 * row), cells_of(ends_ref, 2 * row + 1)
+        put_cells(even_odd_ref, row, jnp.where(odd, left, right))
+        put_cells(odd_even_ref, row, jnp.where(odd, right, left))
     own = rows_ref[...]
-    above = ends_ref[2 * WLAT].astype(F32)[own.shape[0] - strips : own.shape[0], :WIN]
+    above = labels_of(ends_ref)[own.shape[0] - strips : own.shape[0]]
     labels_ref[...] = jnp.concatenate([above, own, jnp.zeros((16 - strips - own.shape[0], WIN), F32)], axis=0)
-    message = label_message(above, ends_ref.shape[-1])
-    even_odd_ref[WLAT] = message
-    odd_even_ref[WLAT] = message
+    put_labels(even_odd_ref, above)
+    put_labels(odd_even_ref, above)
 
 
 def halo_row(row, row_count):
@@ -297,10 +310,10 @@
     odd = lax.axis_index("lon") % 2 == 1
 
     def row_of(row, side):
-        first, second = even_odd_ref[row].astype(F32), odd_even_ref[row].astype(F32)
+        first, second = cells_of(even_odd_ref, row), cells_of(odd_even_ref, row)
         return jnp.where(odd, second, first) if side else jnp.where(odd, first, second)
 
-    return row_of
+    return row_of, jnp.where(odd, labels_of(even_odd_ref), labels_of(odd_even_ref))
 
 
 def half_of(floats, side):
@@ -314,8 +327,8 @@
 def between_kernel(strips, columns_ref, odd_even_ref, even_odd_ref, labels_ref, bias_ref, qkv_weight_ref, out_weight_ref, inner_ref,
                    after_ref, out_ref, *scratch):
     row_count = columns_ref.shape[0]
-    received = swapped(odd_even_ref, even_odd_ref)
-    left_labels = left_labels_of(jnp.zeros((strips, WIN), F32), received(row_count, 0)[:, :WIN])
+    received, own_labels = swapped(odd_even_ref, even_odd_ref)
+    left_labels = left_labels_of(jnp.zeros((strips, WIN), F32), own_labels)
     blocks = side_blocks(
         side_windows(row_count // WLAT, True), row_count // WLAT, strips,
         lambda row, side: half_of(columns_ref[row - HALF_LAT].astype(F32), side),
@@ -331,9 +344,9 @@
                   bias_ref, qkv_weight_ref, out_weight_ref, corner_ref, *scratch):
     row_count = columns_ref.shape[0]
     bands = row_count // WLAT
-    received = swapped(odd_even_ref, even_odd_ref)
-    received_corner = swapped(corner_odd_even_ref, corner_even_odd_ref)
-    left_labels = left_labels_of(received_corner(WLAT, 0)[:strips, :WIN], received(row_count, 0)[:, :WIN])
+    received, own_labels = swapped(odd_even_ref, even_odd_ref)
+    received_corner, above_labels = swapped(corner_odd_even_ref, corner_even_odd_ref)
+    left_labels = left_labels_of(above_labels[:strips], own_labels)
 
     def inside(row):
         return HALF_LAT <= row < row_count + HALF_LAT
@@ -341,7 +354,7 @@
     def own_of(row, side):
         if inside(row):
             return half_of(columns_ref[row - HALF_LAT].astype(F32), side)
-        return ends_ref[2 * halo_row(row, row_count) + side].astype(F32)
+        return cells_of(ends_ref, 2 * halo_row(row, row_count) + side)
 
     def halo_of(row, side):
         return received(row - HALF_LAT, side) if inside(row) else received_corner(halo_row(row, row_count), side)
@@ -411,6 +424,7 @@
     bands, strips = row_count // WLAT, column_count // WLON
     whole = shape(*tokens.shape)
     inner_columns = column_count - WLON
+    blocks = feature // WIN
     dma = pltpu.SemaphoreType.DMA
 
     (label_own,) = run(
@@ -419,7 +433,7 @@
     ends, inner_rows, middle, columns = run(
         message_kernel,
         [
-            shape(2 * WLAT + 1, HALF_LON, feature),
+            shape(2 * WLAT * blocks + 1, HALF_LON, WIN),
             shape(WLAT, inner_columns, feature),
             shape(row_count - WLAT, inner_columns, feature),
             shape(row_count, WLON, feature),
@@ -427,9 +441,9 @@
         [tokens, label_own],
         flops=5 * 10**9,
     )
-    ends_received = lat_exchange(ends, 2 * HALF_LAT)
+    ends_received = lat_exchange(ends, 2 * HALF_LAT * blocks)
     rows_received = lat_exchange(inner_rows, HALF_LAT)
-    message = shape(row_count + 1, HALF_LON, feature)
+    message = shape(row_count * blocks + 1, HALF_LON, WIN)
     columns_sent = run(column_kernel, [message, message], [columns, label_own], flops=2 * 10**10)
     columns_received = lon_exchange(*columns_sent[::-1])
 
@@ -444,7 +458,7 @@
         mib=12,
         flops=5 * 10**9,
     )
-    message = shape(WLAT + 1, HALF_LON, feature)
+    message = shape(WLAT * blocks + 1, HALF_LON, WIN)
     *corners, labels = run(
         functools.partial(corner_message_kernel, strips),
         [message, message, shape(16, WIN, dtype=F32)],

time: 26.4 us -> 26.2 us (level)
  no operation moved by 1% of the time
where the time goes in v5:
time: 26.2 us; the launch traced here: 26 us
  Pallas kernels  14 us (53%)
  starting transfers between devices  9.2 us (35%)
  waiting for transfers between devices  1.39 us (5%)
  local copies, waits for them, and re-layouts  1.3 us (5%)
    pallas_call x9, Pallas kernels, run(): pl.pallas_call(kernel, out_shape=outs, in_specs=specs or [VMEM] * len(ope...  14 us
    ppermute x2, starting transfers between devices, lon_exchange(): return (lax.ppermute(odd_even, 'lon', second), even_odd)  6.09 us
    ppermute x2, starting transfers between devices, moved(): return lax.ppermute(block, axis, route)  3.11 us
    unnamed x12, local copies, waits for them, and re-layouts  1.3 us
    ppermute x2, waiting for transfers between devices, lon_exchange(): return (lax.ppermute(odd_even, 'lon', second), even_odd)  0.87 us
  transfers between devices with their start and end apart: 6, of which 2 were waited for; matrix products, arithmetic and copies ran while one was open for 0% of the time, Pallas kernels for 38%

profile of v5, /device:TPU:0, one launch (start us, length us, event | category | flops | bytes accessed | tf_op | source)
XLA Modules:
  0.0 26.0 jit_solution(4120803940109026794)
XLA Ops:
  0.0 0.0 copy-start.2
  0.0 0.0 copy-start.5
  0.0 0.8 %copy-done.5 = s32[16,64]{1,0:T(8,128)S(1)} copy-done((s32[16,64]{1,0:T(8,128)S(1)}, s32[16,64]{1,0:T(8,128)}, u32[]{:S(2)}) %copy-start.5) | copy-done | bytes 4120
  0.8 0.1 shard_map.64.rows_ref
  1.0 0.5 %copy-done.2 = bf16[16,64,768]{2,1,0:T(8,128)(2,1)S(1)} copy-done((bf16[16,64,768]{2,1,0:T(8,128)(2,1)S(1)}, bf16[16,64,768]{2,1,0:T(8,128)(2,1)}, u32[]{:S(2)}) %copy-start.2) | copy-done | bytes 1572888
  1.4 0.1 shard_map.65
  1.6 3.0 %collective-permute-start.1 = (bf16[97,8,128]{2,1,0:T(8,128)(2,1)S(1)}, bf16[97,8,128]{2,1,0:T(8,128)(2,1)S(1)}, u32[]{:S(2)}, u32[]{:S(2)}) collective-permute-start(bf16[97,8,128]{2,1,0:T(8,128)(2,1)S(1)} %get-tuple-element.17), channel_id=1, source_target_pairs={{1,0},{0,1},{3,2},{2,3},{5,4},{4,5},{7,6},{6,7},{9,8},{8,9},{11,10... | collective-permute-start | bytes 595976 | tf_op jit(solution)/shard_map/ppermute | solution.py:30
  4.6 0.1 collective-permute-start
  4.7 0.0 copy-start
  4.7 0.0 copy-start.1
  4.7 0.0 copy-start.3
  4.7 0.0 copy-start.4
  4.7 0.1 shard_map.66
  4.8 3.9 %collective-permute-start.2 = (bf16[97,8,128]{2,1,0:T(8,128)(2,1)S(1)}, bf16[97,8,128]{2,1,0:T(8,128)(2,1)S(1)}, u32[]{:S(2)}, u32[]{:S(2)}) collective-permute-start(bf16[97,8,128]{2,1,0:T(8,128)(2,1)S(1)} %get-tuple-element.25), channel_id=1, source_target_pairs={{0,30},{2,4},{4,2},{6,8},{8,6},{10,12},{12,10},{14,16},{16,14},{18... | collective-permute-start | bytes 595976 | tf_op jit(solution)/shard_map/ppermute | solution.py:44
  8.7 0.0 collective-permute-start.3
  8.7 0.0 copy-done
  8.7 0.0 copy-done.1
  8.7 0.0 copy-done.3
  8.7 0.0 copy-done.4
  8.7 3.2 %shard_map.67 = (bf16[384,768]{1,0:T(8,128)(2,1)S(1)}, f32[6,128,128]{2,1,0:T(8,128)S(1)}) custom-call(bf16[8,48,768]{2,1,0:T(8,128)(2,1)S(1)} %get-tuple-element.18.middle_ref, f32[8,128]{1,0:T(8,128)S(1)} %shard_map.64.rows_ref, f32[6,465]{1,0:T(8,128)S(1)} %bitcast.1, s32[128,128]{1,0:T(8,128)S(1)} %copy-done.3, bf16[768,2304]{1,0:T(8,128)(2,1)S(1)} %copy-done, ...), custom_call_target="tpu_custom_call" | custom-call | flops 5000000000 | bytes 100000 | tf_op jit(solution)/shard_map/pallas_call | solution.py:48
  11.9 0.0 collective-permute-done.1.ends_ref
  11.9 0.1 shard_map.68
  12.0 2.2 %collective-permute-start.4 = (bf16[49,8,128]{2,1,0:T(8,128)(2,1)S(1)}, bf16[49,8,128]{2,1,0:T(8,128)(2,1)S(1)}, u32[]{:S(2)}, u32[]{:S(2)}) collective-permute-start(bf16[49,8,128]{2,1,0:T(8,128)(2,1)S(1)} %get-tuple-element.26), channel_id=1, source_target_pairs={{0,30},{2,4},{4,2},{6,8},{8,6},{10,12},{12,10},{14,16},{16,14},{18... | collective-permute-start | bytes 301064 | tf_op jit(solution)/shard_map/ppermute | solution.py:44
  14.2 0.0 collective-permute-start.5
  14.2 1.8 %shard_map.69.after_ref.own_ref = bf16[384,2304]{1,0:T(8,128)(2,1)S(1)} custom-call(bf16[8,48,768]{2,1,0:T(8,128)(2,1)S(1)} %get-tuple-element.16.inner_ref, bf16[768,2304]{1,0:T(8,128)(2,1)S(1)} %copy-done, bf16[49,8,128]{2,1,0:T(8,128)(2,1)S(1)} %get-tuple-element.22.after_ref), custom_call_target="tpu_custom_call" | custom-call | flops 1000000 | bytes 100000 | tf_op jit(solution)/shard_map/pallas_call | solution.py:48
  16.0 0.0 collective-permute-done.2.odd_even_ref
  16.0 0.0 collective-permute-done.3.even_odd_ref
  16.0 1.9 %shard_map.71.between_ref = bf16[8,64,768]{2,1,0:T(8,128)(2,1)S(1)} custom-call(bf16[16,16,768]{2,1,0:T(8,128)(2,1)S(1)} %get-tuple-element.19.columns_ref, bf16[97,8,128]{2,1,0:T(8,128)(2,1)S(1)} %collective-permute-done.2.odd_even_ref, bf16[97,8,128]{2,1,0:T(8,128)(2,1)S(1)} %collective-permute-done.3.even_odd_ref, ...), custom_call_target="tpu_custom_call" | custom-call | flops 1000000 | bytes 100000 | tf_op jit(solution)/shard_map/pallas_call | solution.py:48
  18.0 0.9 %collective-permute-done.4.corner_odd_even_ref = bf16[49,8,128]{2,1,0:T(8,128)(2,1)S(1)} collective-permute-done((bf16[49,8,128]{2,1,0:T(8,128)(2,1)S(1)}, bf16[49,8,128]{2,1,0:T(8,128)(2,1)S(1)}, u32[]{:S(2)}, u32[]{:S(2)}) %collective-permute-start.4) | collective-permute-done | bytes 100384 | tf_op jit(solution)/shard_map/ppermute | solution.py:44
  18.8 0.0 collective-permute-done.5.corner_even_odd_ref
  18.8 2.8 %shard_map.70.corner_ref = bf16[8,16,768]{2,1,0:T(8,128)(2,1)S(1)} custom-call(bf16[16,16,768]{2,1,0:T(8,128)(2,1)S(1)} %get-tuple-element.19.columns_ref, bf16[97,8,128]{2,1,0:T(8,128)(2,1)S(1)} %collective-permute-done.2.odd_even_ref, bf16[97,8,128]{2,1,0:T(8,128)(2,1)S(1)} %collective-permute-done.3.even_odd_ref, ...), custom_call_target="tpu_custom_call" | custom-call | flops 1000000 | bytes 100000 | tf_op jit(solution)/shard_map/pallas_call | solution.py:48
  21.7 0.5 %collective-permute-done.halo_ref = bf16[8,48,768]{2,1,0:T(8,128)(2,1)S(1)} collective-permute-done((bf16[8,48,768]{2,1,0:T(8,128)(2,1)S(1)}, bf16[8,48,768]{2,1,0:T(8,128)(2,1)S(1)}, u32[]{:S(2)}, u32[]{:S(2)}) %collective-permute-start) | collective-permute-done | bytes 589856 | tf_op jit(solution)/shard_map/ppermute | solution.py:30
  22.2 3.9 %shard_map.72 = bf16[16,64,768]{2,1,0:T(8,128)(2,1)} custom-call(bf16[8,48,768]{2,1,0:T(8,128)(2,1)S(1)} %get-tuple-element.16.inner_ref, bf16[8,48,768]{2,1,0:T(8,128)(2,1)S(1)} %collective-permute-done.halo_ref, bf16[384,2304]{1,0:T(8,128)(2,1)S(1)} %shard_map.69.after_ref.own_ref, f32[16,128]{1,0:T(8,128)S(1)} %get-tuple-element.23.labels_ref, ...), custom_call_target="tpu_custom_call" | custom-call | flops 1000000 | bytes 100000 | tf_op jit(solution)/shard_map/pallas_call | solution.py:48
Async XLA Ops:
  0.0 1.4 %copy-start.2 = (bf16[16,64,768]{2,1,0:T(8,128)(2,1)S(1)}, bf16[16,64,768]{2,1,0:T(8,128)(2,1)}, u32[]{:S(2)}) copy-start(bf16[16,64,768]{2,1,0:T(8,128)(2,1)} %tokens_ref.1) | copy-start | bytes 4718596
  0.0 0.8 %copy-start.5 = (s32[16,64]{1,0:T(8,128)S(1)}, s32[16,64]{1,0:T(8,128)}, u32[]{:S(2)}) copy-start(s32[16,64]{1,0:T(8,128)} %label_ref.1) | copy-start | bytes 12292
  1.6 10.4 %collective-permute-start.1 = (bf16[97,8,128]{2,1,0:T(8,128)(2,1)S(1)}, bf16[97,8,128]{2,1,0:T(8,128)(2,1)S(1)}, u32[]{:S(2)}, u32[]{:S(2)}) collective-permute-start(bf16[97,8,128]{2,1,0:T(8,128)(2,1)S(1)} %get-tuple-element.17), channel_id=1, source_target_pairs={{1,0},{0,1},{3,2},{2,3},{5,4},{4,5},{7,6},{6,7},{9,8},{8,9},{11,10... | collective-permute-start | bytes 595976 | tf_op jit(solution)/shard_map/ppermute | solution.py:30
  4.6 17.6 %collective-permute-start = (bf16[8,48,768]{2,1,0:T(8,128)(2,1)S(1)}, bf16[8,48,768]{2,1,0:T(8,128)(2,1)S(1)}, u32[]{:S(2)}, u32[]{:S(2)}) collective-permute-start(bf16[8,48,768]{2,1,0:T(8,128)(2,1)S(1)} %get-tuple-element.16.inner_ref), channel_id=1, source_target_pairs={{1,0},{0,1},{3,2},{2,3},{5,4},{4,5},{7,6},{6,7},{9,8},{8,9},{11,10... | collective-permute-start | bytes 1769480 | tf_op jit(solution)/shard_map/ppermute | solution.py:30
  4.7 4.0 %copy-start = (bf16[768,2304]{1,0:T(8,128)(2,1)S(1)}, bf16[768,2304]{1,0:T(8,128)(2,1)}, u32[]{:S(2)}) copy-start(bf16[768,2304]{1,0:T(8,128)(2,1)} %qkv_weight_ref.9) | copy-start | bytes 10616836
  4.7 4.0 %copy-start.1 = (bf16[768,768]{1,0:T(8,128)(2,1)S(1)}, bf16[768,768]{1,0:T(8,128)(2,1)}, u32[]{:S(2)}) copy-start(bf16[768,768]{1,0:T(8,128)(2,1)} %out_weight_ref.7) | copy-start | bytes 3538948
  4.7 4.0 %copy-start.3 = (s32[128,128]{1,0:T(8,128)S(1)}, s32[128,128]{1,0:T(8,128)}, u32[]{:S(2)}) copy-start(s32[128,128]{1,0:T(8,128)} %index_ref.1) | copy-start | bytes 196612
  4.7 4.0 %copy-start.4 = (f32[465,6]{0,1:T(8,128)S(1)}, f32[465,6]{0,1:T(8,128)}, u32[]{:S(2)}) copy-start(f32[465,6]{0,1:T(8,128)} %param.9) | copy-start | bytes 33484
  4.8 11.2 %collective-permute-start.2 = (bf16[97,8,128]{2,1,0:T(8,128)(2,1)S(1)}, bf16[97,8,128]{2,1,0:T(8,128)(2,1)S(1)}, u32[]{:S(2)}, u32[]{:S(2)}) collective-permute-start(bf16[97,8,128]{2,1,0:T(8,128)(2,1)S(1)} %get-tuple-element.25), channel_id=1, source_target_pairs={{0,30},{2,4},{4,2},{6,8},{8,6},{10,12},{12,10},{14,16},{16,14},{18... | collective-permute-start | bytes 595976 | tf_op jit(solution)/shard_map/ppermute | solution.py:44
  8.7 7.3 %collective-permute-start.3 = (bf16[97,8,128]{2,1,0:T(8,128)(2,1)S(1)}, bf16[97,8,128]{2,1,0:T(8,128)(2,1)S(1)}, u32[]{:S(2)}, u32[]{:S(2)}) collective-permute-start(bf16[97,8,128]{2,1,0:T(8,128)(2,1)S(1)} %get-tuple-element.20.after_ref), channel_id=1, source_target_pairs={{0,2},{2,0},{4,6},{6,4},{8,10},{10,8},{12,14},{14,12},{16,18},{18,... | collective-permute-start | bytes 595976 | tf_op jit(solution)/shard_map/ppermute | solution.py:43
  12.0 6.8 %collective-permute-start.4 = (bf16[49,8,128]{2,1,0:T(8,128)(2,1)S(1)}, bf16[49,8,128]{2,1,0:T(8,128)(2,1)S(1)}, u32[]{:S(2)}, u32[]{:S(2)}) collective-permute-start(bf16[49,8,128]{2,1,0:T(8,128)(2,1)S(1)} %get-tuple-element.26), channel_id=1, source_target_pairs={{0,30},{2,4},{4,2},{6,8},{8,6},{10,12},{12,10},{14,16},{16,14},{18... | collective-permute-start | bytes 301064 | tf_op jit(solution)/shard_map/ppermute | solution.py:44
  14.2 4.6 %collective-permute-start.5 = (bf16[49,8,128]{2,1,0:T(8,128)(2,1)S(1)}, bf16[49,8,128]{2,1,0:T(8,128)(2,1)S(1)}, u32[]{:S(2)}, u32[]{:S(2)}) collective-permute-start(bf16[49,8,128]{2,1,0:T(8,128)(2,1)S(1)} %get-tuple-element.22.after_ref), channel_id=1, source_target_pairs={{0,2},{2,0},{4,6},{6,4},{8,10},{10,8},{12,14},{14,12},{16,18},{18,... | collective-permute-start | bytes 301064 | tf_op jit(solution)/shard_map/ppermute | solution.py:43

commit v6 on v5

--- a/solution.py
+++ b/solution.py
@@ -121,6 +121,11 @@
             put_cells(ends_ref, 2 * at + 1, floats[-HALF_LON:])
             inner_ref[at] = inner
     put_labels(ends_ref, rows_ref[...])
+
+
+def normalize_kernel(inner_ref, normed_ref):
+    for row in range(inner_ref.shape[0]):
+        normed_ref[row] = normalize(inner_ref[row].astype(F32)).astype(BF16)
 
 
 def column_kernel(columns_ref, rows_ref, even_odd_ref, odd_even_ref):
@@ -241,7 +246,7 @@
         for strip in range(strips - 1):
             block = inner_ref[side * HALF_LAT : (side + 1) * HALF_LAT, strip * WLON : (strip + 1) * WLON, :]
             start = (side * (strips - 1) + strip) * half
-            cells_ref[start : start + half, :] = normalize(block.astype(F32).reshape(half, feature)).astype(BF16)
+            cells_ref[start : start + half, :] = block.astype(F32).reshape(half, feature).astype(BF16)
     out_ref[...] = project(cells_ref[...], qkv_weight_ref, 0, 3 * feature)
 
 
@@ -378,7 +383,7 @@
     places = [(side, strip) for side in range(2) for strip in range(strips - 1)]
     for at, (side, strip) in enumerate(places):
         block = halo_ref[HALF_LAT * (1 - side) : HALF_LAT * (2 - side), strip * WLON : (strip + 1) * WLON, :]
-        cells_ref[at * half : (at + 1) * half, :] = normalize(block.astype(F32).reshape(half, feature)).astype(BF16)
+        cells_ref[at * half : (at + 1) * half, :] = block.astype(F32).reshape(half, feature).astype(BF16)
     keys_ref[...] = project(cells_ref[...], qkv_weight_ref, feature, 2 * feature)
     labels = labels_ref[...]
     label_columns = labels.T
@@ -442,7 +447,8 @@
         flops=5 * 10**9,
     )
     ends_received = lat_exchange(ends, 2 * HALF_LAT * blocks)
-    rows_received = lat_exchange(inner_rows, HALF_LAT)
+    (normed_rows,) = run(normalize_kernel, [shape(WLAT, inner_columns, feature)], [inner_rows])
+    rows_received = lat_exchange(normed_rows, HALF_LAT)
     message = shape(row_count * blocks + 1, HALF_LON, WIN)
     columns_sent = run(column_kernel, [message, message], [columns, label_own], flops=2 * 10**10)
     columns_received = lon_exchange(*columns_sent[::-1])
@@ -470,7 +476,7 @@
     (row_qkv,) = run(
         functools.partial(rows_kernel, strips),
         [shape(row_cells, 3 * feature)],
-        [inner_rows, qkv_weight, corners[0]],
+        [normed_rows, qkv_weight, corners[0]],
         specs=[VMEM, VMEM, ANY],
         scratch=[pltpu.VMEM((row_cells, feature), BF16)],
         mib=8,

time: 26.2 us -> 25.9 us (0.989)
    ppermute x2, waiting for transfers between devices: 0.51 us -> 0.09 us  [moved(): return lax.ppermute(block, axis, route)]
    pallas_call x9 -> x10, Pallas kernels: 14 us -> 13.8 us  [run(): pl.pallas_call(kernel, out_shape=outs, in_specs=specs or [VMEM] * len(ope...]
  transfers between devices with their start and end apart: 6 -> 6, of which waited for: 2 -> 2; matrix products, arithmetic and copies ran while one was open for 0% -> 0% of each run, Pallas kernels for 38% -> 39%
where the time goes in v6:
time: 25.9 us; the launch traced here: 25.7 us
  Pallas kernels  13.8 us (53%)
  starting transfers between devices  9.23 us (36%)
  local copies, waits for them, and re-layouts  1.31 us (5%)
  waiting for transfers between devices  1.21 us (5%)
    pallas_call x10, Pallas kernels, run(): pl.pallas_call(kernel, out_shape=outs, in_specs=specs or [VMEM] * len(ope...  13.8 us
    ppermute x2, starting transfers between devices, lon_exchange(): return (lax.ppermute(odd_even, 'lon', second), even_odd)  6.11 us
    ppermute x2, starting transfers between devices, moved(): return lax.ppermute(block, axis, route)  3.12 us
    unnamed x12, local copies, waits for them, and re-layouts  1.31 us
    ppermute x2, waiting for transfers between devices, lon_exchange(): return (lax.ppermute(odd_even, 'lon', second), even_odd)  1.12 us
  transfers between devices with their start and end apart: 6, of which 2 were waited for; matrix products, arithmetic and copies ran while one was open for 0% of the time, Pallas kernels for 39%

profile of v6, /device:TPU:0, one launch (start us, length us, event | category | flops | bytes accessed | tf_op | source)
XLA Modules:
  0.0 25.7 jit_solution(6179435284587270564)
XLA Ops:
  0.0 0.0 copy-start.2
  0.0 0.0 copy-start.5
  0.0 0.8 %copy-done.5 = s32[16,64]{1,0:T(8,128)S(1)} copy-done((s32[16,64]{1,0:T(8,128)S(1)}, s32[16,64]{1,0:T(8,128)}, u32[]{:S(2)}) %copy-start.5) | copy-done | bytes 4120
  0.8 0.1 shard_map.64.rows_ref
  1.0 0.5 %copy-done.2 = bf16[16,64,768]{2,1,0:T(8,128)(2,1)S(1)} copy-done((bf16[16,64,768]{2,1,0:T(8,128)(2,1)S(1)}, bf16[16,64,768]{2,1,0:T(8,128)(2,1)}, u32[]{:S(2)}) %copy-start.2) | copy-done | bytes 1572888
  1.4 0.1 shard_map.65
  1.6 3.0 %collective-permute-start.1 = (bf16[97,8,128]{2,1,0:T(8,128)(2,1)S(1)}, bf16[97,8,128]{2,1,0:T(8,128)(2,1)S(1)}, u32[]{:S(2)}, u32[]{:S(2)}) collective-permute-start(bf16[97,8,128]{2,1,0:T(8,128)(2,1)S(1)} %get-tuple-element.17), channel_id=1, source_target_pairs={{1,0},{0,1},{3,2},{2,3},{5,4},{4,5},{7,6},{6,7},{9,8},{8,9},{11,10... | collective-permute-start | bytes 595976 | tf_op jit(solution)/shard_map/ppermute | solution.py:30
  4.6 0.4 %shard_map.66.inner_ref = bf16[8,48,768]{2,1,0:T(8,128)(2,1)S(1)} custom-call(bf16[8,48,768]{2,1,0:T(8,128)(2,1)S(1)} %get-tuple-element.16.inner_ref), custom_call_target="tpu_custom_call" | custom-call | flops 1000000 | bytes 100000 | tf_op jit(solution)/shard_map/pallas_call | solution.py:48
  4.9 0.1 collective-permute-start
  5.0 0.0 copy-start
  5.0 0.0 copy-start.1
  5.0 0.0 copy-start.3
  5.1 0.0 copy-start.4
  5.1 0.1 shard_map.67
  5.2 3.9 %collective-permute-start.2 = (bf16[97,8,128]{2,1,0:T(8,128)(2,1)S(1)}, bf16[97,8,128]{2,1,0:T(8,128)(2,1)S(1)}, u32[]{:S(2)}, u32[]{:S(2)}) collective-permute-start(bf16[97,8,128]{2,1,0:T(8,128)(2,1)S(1)} %get-tuple-element.25), channel_id=1, source_target_pairs={{0,30},{2,4},{4,2},{6,8},{8,6},{10,12},{12,10},{14,16},{16,14},{18... | collective-permute-start | bytes 595976 | tf_op jit(solution)/shard_map/ppermute | solution.py:44
  9.1 0.0 collective-permute-start.3
  9.1 0.0 copy-done
  9.1 0.0 copy-done.1
  9.1 0.0 copy-done.3
  9.1 0.0 copy-done.4
  9.1 3.2 %shard_map.68 = (bf16[384,768]{1,0:T(8,128)(2,1)S(1)}, f32[6,128,128]{2,1,0:T(8,128)S(1)}) custom-call(bf16[8,48,768]{2,1,0:T(8,128)(2,1)S(1)} %get-tuple-element.18.middle_ref, f32[8,128]{1,0:T(8,128)S(1)} %shard_map.64.rows_ref, f32[6,465]{1,0:T(8,128)S(1)} %bitcast.1, s32[128,128]{1,0:T(8,128)S(1)} %copy-done.3, bf16[768,2304]{1,0:T(8,128)(2,1)S(1)} %copy-done, ...), custom_call_target="tpu_custom_call" | custom-call | flops 5000000000 | bytes 100000 | tf_op jit(solution)/shard_map/pallas_call | solution.py:48
  12.3 0.0 collective-permute-done.1.ends_ref
  12.3 0.1 shard_map.69
  12.4 2.2 %collective-permute-start.4 = (bf16[49,8,128]{2,1,0:T(8,128)(2,1)S(1)}, bf16[49,8,128]{2,1,0:T(8,128)(2,1)S(1)}, u32[]{:S(2)}, u32[]{:S(2)}) collective-permute-start(bf16[49,8,128]{2,1,0:T(8,128)(2,1)S(1)} %get-tuple-element.26), channel_id=1, source_target_pairs={{0,30},{2,4},{4,2},{6,8},{8,6},{10,12},{12,10},{14,16},{16,14},{18... | collective-permute-start | bytes 301064 | tf_op jit(solution)/shard_map/ppermute | solution.py:44
  14.6 0.0 collective-permute-start.5
  14.6 1.5 %shard_map.70.after_ref.own_ref = bf16[384,2304]{1,0:T(8,128)(2,1)S(1)} custom-call(bf16[8,48,768]{2,1,0:T(8,128)(2,1)S(1)} %shard_map.66.inner_ref, bf16[768,2304]{1,0:T(8,128)(2,1)S(1)} %copy-done, bf16[49,8,128]{2,1,0:T(8,128)(2,1)S(1)} %get-tuple-element.22.after_ref), custom_call_target="tpu_custom_call" | custom-call | flops 1000000 | bytes 100000 | tf_op jit(solution)/shard_map/pallas_call | solution.py:48
  16.2 0.0 collective-permute-done.2.odd_even_ref
  16.2 0.0 collective-permute-done.3.even_odd_ref
  16.2 1.9 %shard_map.72.between_ref = bf16[8,64,768]{2,1,0:T(8,128)(2,1)S(1)} custom-call(bf16[16,16,768]{2,1,0:T(8,128)(2,1)S(1)} %get-tuple-element.19.columns_ref, bf16[97,8,128]{2,1,0:T(8,128)(2,1)S(1)} %collective-permute-done.2.odd_even_ref, bf16[97,8,128]{2,1,0:T(8,128)(2,1)S(1)} %collective-permute-done.3.even_odd_ref, ...), custom_call_target="tpu_custom_call" | custom-call | flops 1000000 | bytes 100000 | tf_op jit(solution)/shard_map/pallas_call | solution.py:48
  18.1 1.1 %collective-permute-done.4.corner_odd_even_ref = bf16[49,8,128]{2,1,0:T(8,128)(2,1)S(1)} collective-permute-done((bf16[49,8,128]{2,1,0:T(8,128)(2,1)S(1)}, bf16[49,8,128]{2,1,0:T(8,128)(2,1)S(1)}, u32[]{:S(2)}, u32[]{:S(2)}) %collective-permute-start.4) | collective-permute-done | bytes 100384 | tf_op jit(solution)/shard_map/ppermute | solution.py:44
  19.2 0.0 collective-permute-done.5.corner_even_odd_ref
  19.2 2.8 %shard_map.71.corner_ref = bf16[8,16,768]{2,1,0:T(8,128)(2,1)S(1)} custom-call(bf16[16,16,768]{2,1,0:T(8,128)(2,1)S(1)} %get-tuple-element.19.columns_ref, bf16[97,8,128]{2,1,0:T(8,128)(2,1)S(1)} %collective-permute-done.2.odd_even_ref, bf16[97,8,128]{2,1,0:T(8,128)(2,1)S(1)} %collective-permute-done.3.even_odd_ref, ...), custom_call_target="tpu_custom_call" | custom-call | flops 1000000 | bytes 100000 | tf_op jit(solution)/shard_map/pallas_call | solution.py:48
  22.1 0.1 collective-permute-done.halo_ref
  22.2 3.6 %shard_map.73 = bf16[16,64,768]{2,1,0:T(8,128)(2,1)} custom-call(bf16[8,48,768]{2,1,0:T(8,128)(2,1)S(1)} %get-tuple-element.16.inner_ref, bf16[8,48,768]{2,1,0:T(8,128)(2,1)S(1)} %collective-permute-done.halo_ref, bf16[384,2304]{1,0:T(8,128)(2,1)S(1)} %shard_map.70.after_ref.own_ref, f32[16,128]{1,0:T(8,128)S(1)} %get-tuple-element.23.labels_ref, ...), custom_call_target="tpu_custom_call" | custom-call | flops 1000000 | bytes 100000 | tf_op jit(solution)/shard_map/pallas_call | solution.py:48
Async XLA Ops:
  0.0 1.4 %copy-start.2 = (bf16[16,64,768]{2,1,0:T(8,128)(2,1)S(1)}, bf16[16,64,768]{2,1,0:T(8,128)(2,1)}, u32[]{:S(2)}) copy-start(bf16[16,64,768]{2,1,0:T(8,128)(2,1)} %tokens_ref.1) | copy-start | bytes 4718596
  0.0 0.8 %copy-start.5 = (s32[16,64]{1,0:T(8,128)S(1)}, s32[16,64]{1,0:T(8,128)}, u32[]{:S(2)}) copy-start(s32[16,64]{1,0:T(8,128)} %label_ref.1) | copy-start | bytes 12292
  1.6 10.8 %collective-permute-start.1 = (bf16[97,8,128]{2,1,0:T(8,128)(2,1)S(1)}, bf16[97,8,128]{2,1,0:T(8,128)(2,1)S(1)}, u32[]{:S(2)}, u32[]{:S(2)}) collective-permute-start(bf16[97,8,128]{2,1,0:T(8,128)(2,1)S(1)} %get-tuple-element.17), channel_id=1, source_target_pairs={{1,0},{0,1},{3,2},{2,3},{5,4},{4,5},{7,6},{6,7},{9,8},{8,9},{11,10... | collective-permute-start | bytes 595976 | tf_op jit(solution)/shard_map/ppermute | solution.py:30
  4.9 17.2 %collective-permute-start = (bf16[8,48,768]{2,1,0:T(8,128)(2,1)S(1)}, bf16[8,48,768]{2,1,0:T(8,128)(2,1)S(1)}, u32[]{:S(2)}, u32[]{:S(2)}) collective-permute-start(bf16[8,48,768]{2,1,0:T(8,128)(2,1)S(1)} %shard_map.66.inner_ref), channel_id=1, source_target_pairs={{1,0},{0,1},{3,2},{2,3},{5,4},{4,5},{7,6},{6,7},{9,8},{8,9},{11,10... | collective-permute-start | bytes 1769480 | tf_op jit(solution)/shard_map/ppermute | solution.py:30
  5.0 4.1 %copy-start = (bf16[768,2304]{1,0:T(8,128)(2,1)S(1)}, bf16[768,2304]{1,0:T(8,128)(2,1)}, u32[]{:S(2)}) copy-start(bf16[768,2304]{1,0:T(8,128)(2,1)} %qkv_weight_ref.9) | copy-start | bytes 10616836
  5.0 4.1 %copy-start.1 = (bf16[768,768]{1,0:T(8,128)(2,1)S(1)}, bf16[768,768]{1,0:T(8,128)(2,1)}, u32[]{:S(2)}) copy-start(bf16[768,768]{1,0:T(8,128)(2,1)} %out_weight_ref.7) | copy-start | bytes 3538948
  5.0 4.1 %copy-start.3 = (s32[128,128]{1,0:T(8,128)S(1)}, s32[128,128]{1,0:T(8,128)}, u32[]{:S(2)}) copy-start(s32[128,128]{1,0:T(8,128)} %index_ref.1) | copy-start | bytes 196612
  5.1 4.1 %copy-start.4 = (f32[465,6]{0,1:T(8,128)S(1)}, f32[465,6]{0,1:T(8,128)}, u32[]{:S(2)}) copy-start(f32[465,6]{0,1:T(8,128)} %param.9) | copy-start | bytes 33484
  5.2 11.0 %collective-permute-start.2 = (bf16[97,8,128]{2,1,0:T(8,128)(2,1)S(1)}, bf16[97,8,128]{2,1,0:T(8,128)(2,1)S(1)}, u32[]{:S(2)}, u32[]{:S(2)}) collective-permute-start(bf16[97,8,128]{2,1,0:T(8,128)(2,1)S(1)} %get-tuple-element.25), channel_id=1, source_target_pairs={{0,30},{2,4},{4,2},{6,8},{8,6},{10,12},{12,10},{14,16},{16,14},{18... | collective-permute-start | bytes 595976 | tf_op jit(solution)/shard_map/ppermute | solution.py:44
  9.1 7.1 %collective-permute-start.3 = (bf16[97,8,128]{2,1,0:T(8,128)(2,1)S(1)}, bf16[97,8,128]{2,1,0:T(8,128)(2,1)S(1)}, u32[]{:S(2)}, u32[]{:S(2)}) collective-permute-start(bf16[97,8,128]{2,1,0:T(8,128)(2,1)S(1)} %get-tuple-element.20.after_ref), channel_id=1, source_target_pairs={{0,2},{2,0},{4,6},{6,4},{8,10},{10,8},{12,14},{14,12},{16,18},{18,... | collective-permute-start | bytes 595976 | tf_op jit(solution)/shard_map/ppermute | solution.py:43
  12.4 6.8 %collective-permute-start.4 = (bf16[49,8,128]{2,1,0:T(8,128)(2,1)S(1)}, bf16[49,8,128]{2,1,0:T(8,128)(2,1)S(1)}, u32[]{:S(2)}, u32[]{:S(2)}) collective-permute-start(bf16[49,8,128]{2,1,0:T(8,128)(2,1)S(1)} %get-tuple-element.26), channel_id=1, source_target_pairs={{0,30},{2,4},{4,2},{6,8},{8,6},{10,12},{12,10},{14,16},{16,14},{18... | collective-permute-start | bytes 301064 | tf_op jit(solution)/shard_map/ppermute | solution.py:44
  14.6 4.6 %collective-permute-start.5 = (bf16[49,8,128]{2,1,0:T(8,128)(2,1)S(1)}, bf16[49,8,128]{2,1,0:T(8,128)(2,1)S(1)}, u32[]{:S(2)}, u32[]{:S(2)}) collective-permute-start(bf16[49,8,128]{2,1,0:T(8,128)(2,1)S(1)} %get-tuple-element.22.after_ref), channel_id=1, source_target_pairs={{0,2},{2,0},{4,6},{6,4},{8,10},{10,8},{12,14},{14,12},{16,18},{18,... | collective-permute-start | bytes 301064 | tf_op jit(solution)/shard_map/ppermute | solution.py:43

commit v7 on v6

--- a/solution.py
+++ b/solution.py
@@ -250,34 +250,8 @@
     out_ref[...] = project(cells_ref[...], qkv_weight_ref, 0, 3 * feature)
 
 
-def side_windows(bands, between):
-    windows, start = [], 0
-    for band in range(bands + 1):
-        if (0 < band < bands) == between:
-            count = HALF_LON * (WLAT if between else HALF_LAT)
-            for side in range(2):
-                windows.append((band, side, start, count))
-                start += count
-    return windows
-
-
-def side_blocks(windows, bands, strips, own_of, halo_of, left_labels, labels, bias_ref, qkv_weight_ref, out_weight_ref,
-                cells_ref, own_ref, queries_ref, keys_ref, attended_ref):
-    feature = cells_ref.shape[-1]
+def side_attention(windows, bands, strips, queries_of, keys_of, left_labels, labels, bias_ref, attended_ref):
     label_columns = left_labels.T, labels.T
-    tokens_of = {}
-    for at, (band, side, start, count) in enumerate(windows):
-        own = [own_of(row, side) for row in range(band * WLAT, (band + 1) * WLAT)]
-        halo = [halo_of(row, side) for row in range(band * WLAT, (band + 1) * WLAT)]
-        mine = slice(HALF_LAT if band == 0 else 0, HALF_LAT if band == bands else WLAT)
-        tokens_of[band, side] = own[mine]
-        own = normalize(jnp.stack(own))
-        halo = normalize(jnp.stack(halo))
-        window = jnp.concatenate([own, halo] if side else [halo, own], axis=1)
-        cells_ref[at * WIN : (at + 1) * WIN, :] = window.reshape(WIN, feature).astype(BF16)
-        own_ref[start : start + count, :] = own[mine].reshape(count, feature).astype(BF16)
-    queries_ref[...] = project(own_ref[...], qkv_weight_ref, 0, feature)
-    keys_ref[...] = project(cells_ref[...], qkv_weight_ref, feature, 2 * feature)
 
     def own_rows(array, band, side):
         array = array.reshape(WLAT, WLON, WIN)
@@ -287,28 +261,21 @@
 
     entries = []
     for at, (band, side, start, count) in enumerate(windows):
-        mine, whole = slice(start, start + count), slice(at * WIN, (at + 1) * WIN)
+        mine = slice(start, start + count)
         place = band * strips + strips - 1
         row = (labels if side else left_labels)[place : place + 1]
         mask = own_rows(excluded(label_columns[side][:, place : place + 1], row), band, side)
         for head in range(HEADS):
             entries.append(
                 (
-                    lambda mine=mine, head=head: queries_ref[mine, lanes(head)],
-                    lambda whole=whole, head=head: keys_ref[whole, lanes(head)],
-                    lambda whole=whole, head=head: keys_ref[whole, lanes(HEADS + head)],
+                    lambda mine=mine, head=head: queries_of(mine, lanes(head)),
+                    lambda at=at, head=head: keys_of(at, lanes(head)),
+                    lambda at=at, head=head: keys_of(at, lanes(HEADS + head)),
                     lambda mask=mask, head=head, band=band, side=side: own_rows(bias_ref[head], band, side) + mask,
                     storer(attended_ref, mine, head),
                 )
             )
     attention(entries)
-    branch = out_project(attended_ref[...], out_weight_ref)
-    blocks = {}
-    for band, side, start, count in windows:
-        for row, own in enumerate(tokens_of[band, side]):
-            at = start + row * HALF_LON
-            blocks[band, side, row] = own + branch[at : at + HALF_LON]
-    return blocks
 
 
 def swapped(odd_even_ref, even_odd_ref):
@@ -329,48 +296,92 @@
     return jnp.concatenate([above, own, jnp.zeros((16 - above.shape[0] - own.shape[0], WIN), F32)], axis=0)
 
 
+def between_windows():
+    return [(1, side, side * WLAT * HALF_LON, WLAT * HALF_LON) for side in range(2)]
+
+
+def corner_windows(bands):
+    count = HALF_LAT * HALF_LON
+    return [(band, side, at * count, count) for at, (band, side) in enumerate((b, s) for b in (0, bands) for s in range(2))]
+
+
 def between_kernel(strips, columns_ref, odd_even_ref, even_odd_ref, labels_ref, bias_ref, qkv_weight_ref, out_weight_ref, inner_ref,
-                   after_ref, out_ref, *scratch):
-    row_count = columns_ref.shape[0]
+                   after_ref, out_ref, corner_queries_ref, corner_keys_ref, cells_ref, own_ref, queries_ref, keys_ref, attended_ref):
+    row_count, _, feature = columns_ref.shape
+    bands = row_count // WLAT
     received, own_labels = swapped(odd_even_ref, even_odd_ref)
     left_labels = left_labels_of(jnp.zeros((strips, WIN), F32), own_labels)
-    blocks = side_blocks(
-        side_windows(row_count // WLAT, True), row_count // WLAT, strips,
-        lambda row, side: half_of(columns_ref[row - HALF_LAT].astype(F32), side),
-        lambda row, side: received(row - HALF_LAT, side),
-        left_labels, labels_ref[...], bias_ref, qkv_weight_ref, out_weight_ref, *scratch,
-    )
+    windows = between_windows()
+    half = HALF_LAT * WLON
+    tokens_of = {}
+
+    def put(first, rows, side, key_start, query_start):
+        own = jnp.stack([half_of(columns_ref[row].astype(F32), side) for row in range(first, first + rows)])
+        halo = normalize(jnp.stack([received(row, side) for row in range(first, first + rows)]))
+        normed = normalize(own)
+        cells = jnp.concatenate([normed, halo] if side else [halo, normed], axis=1)
+        cells_ref[key_start : key_start + rows * WLON, :] = cells.reshape(rows * WLON, feature).astype(BF16)
+        own_ref[query_start : query_start + rows * HALF_LON, :] = normed.reshape(rows * HALF_LON, feature).astype(BF16)
+        return own
+
+    for at, (band, side, start, count) in enumerate(windows):
+        tokens_of[side] = put(HALF_LAT, WLAT, side, at * WIN, start)
+    ends = corner_windows(bands)
+    for at, (band, side, start, count) in enumerate(ends):
+        put(row_count - HALF_LAT if band else 0, HALF_LAT, side, len(windows) * WIN + at * half, WLAT * WLON + start)
+    queries_ref[...] = project(own_ref[...], qkv_weight_ref, 0, feature)
+    keys_ref[...] = project(cells_ref[...], qkv_weight_ref, feature, 2 * feature)
+    corner_queries_ref[...] = queries_ref[WLAT * WLON :, :]
+    corner_keys_ref[...] = keys_ref[len(windows) * WIN :, :]
+    side_attention(
+        windows, bands, strips,
+        lambda mine, columns: queries_ref[mine, columns],
+        lambda at, columns: keys_ref[at * WIN : (at + 1) * WIN, columns],
+        left_labels, labels_ref[...], bias_ref, attended_ref,
+    )
+    branch = out_project(attended_ref[...], out_weight_ref)
     for row in range(WLAT):
         middle = [inner_ref[strip * WIN + row * WLON : strip * WIN + (row + 1) * WLON, :].astype(F32) for strip in range(strips - 1)]
-        out_ref[row] = jnp.concatenate([blocks[1, 0, row]] + middle + [blocks[1, 1, row]], axis=0).astype(BF16)
-
-
-def corner_kernel(strips, columns_ref, odd_even_ref, even_odd_ref, corner_odd_even_ref, corner_even_odd_ref, ends_ref, labels_ref,
-                  bias_ref, qkv_weight_ref, out_weight_ref, corner_ref, *scratch):
-    row_count = columns_ref.shape[0]
+        ends = []
+        for side, (_, _, start, _) in enumerate(windows):
+            at = start + row * HALF_LON
+            ends.append(tokens_of[side][row] + branch[at : at + HALF_LON])
+        out_ref[row] = jnp.concatenate([ends[0]] + middle + [ends[1]], axis=0).astype(BF16)
+
+
+def corner_kernel(strips, columns_ref, odd_even_ref, even_odd_ref, corner_odd_even_ref, corner_even_odd_ref, ends_ref, labels_ref, queries_ref, own_ref,
+                  bias_ref, qkv_weight_ref, out_weight_ref, corner_ref, cells_ref, keys_ref, attended_ref):
+    row_count, _, feature = columns_ref.shape
     bands = row_count // WLAT
-    received, own_labels = swapped(odd_even_ref, even_odd_ref)
-    received_corner, above_labels = swapped(corner_odd_even_ref, corner_even_odd_ref)
+    half = HALF_LAT * WLON
+    _, own_labels = swapped(odd_even_ref, even_odd_ref)
+    received, above_labels = swapped(corner_odd_even_ref, corner_even_odd_ref)
     left_labels = left_labels_of(above_labels[:strips], own_labels)
-
-    def inside(row):
-        return HALF_LAT <= row < row_count + HALF_LAT
-
-    def own_of(row, side):
-        if inside(row):
-            return half_of(columns_ref[row - HALF_LAT].astype(F32), side)
-        return cells_of(ends_ref, 2 * halo_row(row, row_count) + side)
-
-    def halo_of(row, side):
-        return received(row - HALF_LAT, side) if inside(row) else received_corner(halo_row(row, row_count), side)
-
-    blocks = side_blocks(
-        side_windows(bands, False), bands, strips, own_of, halo_of,
-        left_labels, labels_ref[...], bias_ref, qkv_weight_ref, out_weight_ref, *scratch,
-    )
-    for band, first in ((0, 0), (bands, HALF_LAT)):
+    windows = corner_windows(bands)
+    for at, (band, side, start, count) in enumerate(windows):
+        rows = range(0 if band else HALF_LAT, HALF_LAT if band else WLAT)
+        near = normalize(jnp.stack([cells_of(ends_ref, 2 * row + side) for row in rows]))
+        far = normalize(jnp.stack([received(row, side) for row in rows]))
+        cells = jnp.concatenate([near, far] if side else [far, near], axis=1)
+        cells_ref[at * half : (at + 1) * half, :] = cells.reshape(half, feature).astype(BF16)
+    keys_ref[...] = project(cells_ref[...], qkv_weight_ref, feature, 2 * feature)
+
+    def keys_of(at, columns):
+        mine = slice(at * half, (at + 1) * half)
+        pair = own_ref[mine, columns], keys_ref[mine, columns]
+        return jnp.concatenate(pair if windows[at][0] else pair[::-1], axis=0)
+
+    side_attention(
+        windows, bands, strips, lambda mine, columns: queries_ref[mine, columns], keys_of,
+        left_labels, labels_ref[...], bias_ref, attended_ref,
+    )
+    branch = out_project(attended_ref[...], out_weight_ref)
+    for end in range(2):
         for row in range(HALF_LAT):
-            corner_ref[first + row] = jnp.concatenate([blocks[band, 0, row], blocks[band, 1, row]], axis=0).astype(BF16)
+            cells = columns_ref[row_count - HALF_LAT + row if end else row].astype(F32)
+            starts = [windows[2 * end + side][2] + row * HALF_LON for side in range(2)]
+            added = jnp.concatenate([branch[start : start + HALF_LON] for start in starts], axis=0)
+            corner_ref[end * HALF_LAT + row] = (cells + added).astype(BF16)
 
 
 def last_kernel(strips, inner_ref, halo_ref, own_ref, labels_ref, bias_ref, qkv_weight_ref, out_weight_ref, corner_ref, between_ref,
@@ -482,27 +493,22 @@
         mib=8,
     )
 
-    def side_scratch(between):
-        windows = side_windows(bands, between)
-        cells, every = windows[-1][2] + windows[-1][3], len(windows) * WIN
-        sizes = ((every, 1), (cells, 1), (cells, 1), (every, 2), (cells, 1))
-        return cells, every, [pltpu.VMEM((count, width * feature), BF16) for count, width in sizes]
-
-    cells, every, scratch = side_scratch(True)
-    (between,) = run(
+    side_cells, corner_cells = WLAT * WLON, 2 * HALF_LAT * WLON
+    every = 4 * WIN
+    between, corner_queries, corner_keys = run(
         functools.partial(between_kernel, strips),
-        [shape(row_count - WLAT, column_count, feature)],
+        [shape(row_count - WLAT, column_count, feature), shape(corner_cells, feature), shape(2 * WIN, 2 * feature)],
         [columns, *columns_received, labels, bias, qkv_weight, out_weight, inner, row_qkv],
         specs=[VMEM] * 8 + [ANY],
-        scratch=scratch,
+        scratch=[pltpu.VMEM((count, width * feature), BF16) for count, width in
+                 ((every, 1), (side_cells + corner_cells, 1), (side_cells + corner_cells, 1), (every, 2), (side_cells, 1))],
         mib=12,
     )
-    cells, every, scratch = side_scratch(False)
     (corner,) = run(
         functools.partial(corner_kernel, strips),
         [shape(WLAT, WLON, feature)],
-        [columns, *columns_received, *corners_received, ends_received, labels, bias, qkv_weight, out_weight],
-        scratch=scratch,
+        [columns, *columns_received, *corners_received, ends_received, labels, corner_queries, corner_keys, bias, qkv_weight, out_weight],
+        scratch=[pltpu.VMEM((count, width * feature), BF16) for count, width in ((2 * WIN, 1), (2 * WIN, 2), (corner_cells, 1))],
         mib=12,
     )
     (out,) = run(

time: 25.9 us -> 25.9 us (level)
    ppermute x2, waiting for transfers between devices: 0.09 us -> 0.96 us  [moved(): return lax.ppermute(block, axis, route)]
    ppermute x2, waiting for transfers between devices: 1.12 us -> 0.28 us  [lon_exchange(): return (lax.ppermute(odd_even, 'lon', second), even_odd)]
where the time goes in v7:
time: 25.9 us; the launch traced here: 25.7 us
  Pallas kernels  13.8 us (53%)
  starting transfers between devices  9.24 us (36%)
  local copies, waits for them, and re-layouts  1.31 us (5%)
  waiting for transfers between devices  1.24 us (5%)
    pallas_call x10, Pallas kernels, run(): pl.pallas_call(kernel, out_shape=outs, in_specs=specs or [VMEM] * len(ope...  13.8 us
    ppermute x2, starting transfers between devices, lon_exchange(): return (lax.ppermute(odd_even, 'lon', second), even_odd)  6.12 us
    ppermute x2, starting transfers between devices, moved(): return lax.ppermute(block, axis, route)  3.12 us
    unnamed x12, local copies, waits for them, and re-layouts  1.31 us
    ppermute x2, waiting for transfers between devices, moved(): return lax.ppermute(block, axis, route)  0.96 us
  transfers between devices with their start and end apart: 6, of which 2 were waited for; matrix products, arithmetic and copies ran while one was open for 0% of the time, Pallas kernels for 39%

profile of v7, /device:TPU:0, one launch (start us, length us, event | category | flops | bytes accessed | tf_op | source)
XLA Modules:
  0.0 25.7 jit_solution(18088103765230149779)
XLA Ops:
  0.0 0.0 copy-start.2
  0.0 0.0 copy-start.5
  0.0 0.8 %copy-done.5 = s32[16,64]{1,0:T(8,128)S(1)} copy-done((s32[16,64]{1,0:T(8,128)S(1)}, s32[16,64]{1,0:T(8,128)}, u32[]{:S(2)}) %copy-start.5) | copy-done | bytes 4120
  0.8 0.1 shard_map.64.rows_ref
  1.0 0.5 %copy-done.2 = bf16[16,64,768]{2,1,0:T(8,128)(2,1)S(1)} copy-done((bf16[16,64,768]{2,1,0:T(8,128)(2,1)S(1)}, bf16[16,64,768]{2,1,0:T(8,128)(2,1)}, u32[]{:S(2)}) %copy-start.2) | copy-done | bytes 1572888
  1.4 0.1 shard_map.65
  1.6 3.0 %collective-permute-start.1 = (bf16[97,8,128]{2,1,0:T(8,128)(2,1)S(1)}, bf16[97,8,128]{2,1,0:T(8,128)(2,1)S(1)}, u32[]{:S(2)}, u32[]{:S(2)}) collective-permute-start(bf16[97,8,128]{2,1,0:T(8,128)(2,1)S(1)} %get-tuple-element.20), channel_id=1, source_target_pairs={{1,0},{0,1},{3,2},{2,3},{5,4},{4,5},{7,6},{6,7},{9,8},{8,9},{11,10... | collective-permute-start | bytes 595976 | tf_op jit(solution)/shard_map/ppermute | solution.py:30
  4.6 0.4 %shard_map.66.inner_ref = bf16[8,48,768]{2,1,0:T(8,128)(2,1)S(1)} custom-call(bf16[8,48,768]{2,1,0:T(8,128)(2,1)S(1)} %get-tuple-element.19.inner_ref), custom_call_target="tpu_custom_call" | custom-call | flops 1000000 | bytes 100000 | tf_op jit(solution)/shard_map/pallas_call | solution.py:48
  4.9 0.1 collective-permute-start
  5.0 0.0 copy-start
  5.0 0.0 copy-start.1
  5.0 0.0 copy-start.3
  5.1 0.0 copy-start.4
  5.1 0.1 shard_map.67
  5.2 3.9 %collective-permute-start.2 = (bf16[97,8,128]{2,1,0:T(8,128)(2,1)S(1)}, bf16[97,8,128]{2,1,0:T(8,128)(2,1)S(1)}, u32[]{:S(2)}, u32[]{:S(2)}) collective-permute-start(bf16[97,8,128]{2,1,0:T(8,128)(2,1)S(1)} %get-tuple-element.28), channel_id=1, source_target_pairs={{0,30},{2,4},{4,2},{6,8},{8,6},{10,12},{12,10},{14,16},{16,14},{18... | collective-permute-start | bytes 595976 | tf_op jit(solution)/shard_map/ppermute | solution.py:44
  9.1 0.0 collective-permute-start.3
  9.1 0.0 copy-done
  9.1 0.0 copy-done.1
  9.1 0.0 copy-done.3
  9.1 0.0 copy-done.4
  9.1 3.2 %shard_map.68 = (bf16[384,768]{1,0:T(8,128)(2,1)S(1)}, f32[6,128,128]{2,1,0:T(8,128)S(1)}) custom-call(bf16[8,48,768]{2,1,0:T(8,128)(2,1)S(1)} %get-tuple-element.21.middle_ref, f32[8,128]{1,0:T(8,128)S(1)} %shard_map.64.rows_ref, f32[6,465]{1,0:T(8,128)S(1)} %bitcast.1, s32[128,128]{1,0:T(8,128)S(1)} %copy-done.3, bf16[768,2304]{1,0:T(8,128)(2,1)S(1)} %copy-done, ...), custom_call_target="tpu_custom_call" | custom-call | flops 5000000000 | bytes 100000 | tf_op jit(solution)/shard_map/pallas_call | solution.py:48
  12.3 0.0 collective-permute-done.1.ends_ref
  12.3 0.1 shard_map.69
  12.4 2.2 %collective-permute-start.4 = (bf16[49,8,128]{2,1,0:T(8,128)(2,1)S(1)}, bf16[49,8,128]{2,1,0:T(8,128)(2,1)S(1)}, u32[]{:S(2)}, u32[]{:S(2)}) collective-permute-start(bf16[49,8,128]{2,1,0:T(8,128)(2,1)S(1)} %get-tuple-element.29), channel_id=1, source_target_pairs={{0,30},{2,4},{4,2},{6,8},{8,6},{10,12},{12,10},{14,16},{16,14},{18... | collective-permute-start | bytes 301064 | tf_op jit(solution)/shard_map/ppermute | solution.py:44
  14.6 0.0 collective-permute-start.5
  14.6 1.5 %shard_map.70.after_ref.own_ref = bf16[384,2304]{1,0:T(8,128)(2,1)S(1)} custom-call(bf16[8,48,768]{2,1,0:T(8,128)(2,1)S(1)} %shard_map.66.inner_ref, bf16[768,2304]{1,0:T(8,128)(2,1)S(1)} %copy-done, bf16[49,8,128]{2,1,0:T(8,128)(2,1)S(1)} %get-tuple-element.25.after_ref), custom_call_target="tpu_custom_call" | custom-call | flops 1000000 | bytes 100000 | tf_op jit(solution)/shard_map/pallas_call | solution.py:48
  16.1 0.0 collective-permute-done.2.odd_even_ref
  16.2 0.0 collective-permute-done.3.even_odd_ref
  16.2 2.8 %shard_map.71 = (bf16[8,64,768]{2,1,0:T(8,128)(2,1)S(1)}, bf16[128,768]{1,0:T(8,128)(2,1)S(1)}, bf16[256,1536]{1,0:T(8,128)(2,1)S(1)}) custom-call(bf16[16,16,768]{2,1,0:T(8,128)(2,1)S(1)} %get-tuple-element.22.columns_ref, bf16[97,8,128]{2,1,0:T(8,128)(2,1)S(1)} %collective-permute-done.2.odd_even_ref, ...), custom_call_target="tpu_custom_call" | custom-call | flops 1000000 | bytes 100000 | tf_op jit(solution)/shard_map/pallas_call | solution.py:48
  19.0 0.3 %collective-permute-done.4.corner_odd_even_ref = bf16[49,8,128]{2,1,0:T(8,128)(2,1)S(1)} collective-permute-done((bf16[49,8,128]{2,1,0:T(8,128)(2,1)S(1)}, bf16[49,8,128]{2,1,0:T(8,128)(2,1)S(1)}, u32[]{:S(2)}, u32[]{:S(2)}) %collective-permute-start.4) | collective-permute-done | bytes 100384 | tf_op jit(solution)/shard_map/ppermute | solution.py:44
  19.2 0.0 collective-permute-done.5.corner_even_odd_ref
  19.2 2.0 %shard_map.72.corner_ref = bf16[8,16,768]{2,1,0:T(8,128)(2,1)S(1)} custom-call(bf16[16,16,768]{2,1,0:T(8,128)(2,1)S(1)} %get-tuple-element.22.columns_ref, bf16[97,8,128]{2,1,0:T(8,128)(2,1)S(1)} %collective-permute-done.2.odd_even_ref, bf16[97,8,128]{2,1,0:T(8,128)(2,1)S(1)} %collective-permute-done.3.even_odd_ref, ...), custom_call_target="tpu_custom_call" | custom-call | flops 1000000 | bytes 100000 | tf_op jit(solution)/shard_map/pallas_call | solution.py:48
  21.2 1.0 %collective-permute-done.halo_ref = bf16[8,48,768]{2,1,0:T(8,128)(2,1)S(1)} collective-permute-done((bf16[8,48,768]{2,1,0:T(8,128)(2,1)S(1)}, bf16[8,48,768]{2,1,0:T(8,128)(2,1)S(1)}, u32[]{:S(2)}, u32[]{:S(2)}) %collective-permute-start) | collective-permute-done | bytes 589856 | tf_op jit(solution)/shard_map/ppermute | solution.py:30
  22.2 3.5 %shard_map.73 = bf16[16,64,768]{2,1,0:T(8,128)(2,1)} custom-call(bf16[8,48,768]{2,1,0:T(8,128)(2,1)S(1)} %get-tuple-element.19.inner_ref, bf16[8,48,768]{2,1,0:T(8,128)(2,1)S(1)} %collective-permute-done.halo_ref, bf16[384,2304]{1,0:T(8,128)(2,1)S(1)} %shard_map.70.after_ref.own_ref, f32[16,128]{1,0:T(8,128)S(1)} %get-tuple-element.26.labels_ref, ...), custom_call_target="tpu_custom_call" | custom-call | flops 1000000 | bytes 100000 | tf_op jit(solution)/shard_map/pallas_call | solution.py:48
Async XLA Ops:
  0.0 1.4 %copy-start.2 = (bf16[16,64,768]{2,1,0:T(8,128)(2,1)S(1)}, bf16[16,64,768]{2,1,0:T(8,128)(2,1)}, u32[]{:S(2)}) copy-start(bf16[16,64,768]{2,1,0:T(8,128)(2,1)} %tokens_ref.1) | copy-start | bytes 4718596
  0.0 0.8 %copy-start.5 = (s32[16,64]{1,0:T(8,128)S(1)}, s32[16,64]{1,0:T(8,128)}, u32[]{:S(2)}) copy-start(s32[16,64]{1,0:T(8,128)} %label_ref.1) | copy-start | bytes 12292
  1.6 10.8 %collective-permute-start.1 = (bf16[97,8,128]{2,1,0:T(8,128)(2,1)S(1)}, bf16[97,8,128]{2,1,0:T(8,128)(2,1)S(1)}, u32[]{:S(2)}, u32[]{:S(2)}) collective-permute-start(bf16[97,8,128]{2,1,0:T(8,128)(2,1)S(1)} %get-tuple-element.20), channel_id=1, source_target_pairs={{1,0},{0,1},{3,2},{2,3},{5,4},{4,5},{7,6},{6,7},{9,8},{8,9},{11,10... | collective-permute-start | bytes 595976 | tf_op jit(solution)/shard_map/ppermute | solution.py:30
  4.9 17.2 %collective-permute-start = (bf16[8,48,768]{2,1,0:T(8,128)(2,1)S(1)}, bf16[8,48,768]{2,1,0:T(8,128)(2,1)S(1)}, u32[]{:S(2)}, u32[]{:S(2)}) collective-permute-start(bf16[8,48,768]{2,1,0:T(8,128)(2,1)S(1)} %shard_map.66.inner_ref), channel_id=1, source_target_pairs={{1,0},{0,1},{3,2},{2,3},{5,4},{4,5},{7,6},{6,7},{9,8},{8,9},{11,10... | collective-permute-start | bytes 1769480 | tf_op jit(solution)/shard_map/ppermute | solution.py:30
  5.0 4.1 %copy-start = (bf16[768,2304]{1,0:T(8,128)(2,1)S(1)}, bf16[768,2304]{1,0:T(8,128)(2,1)}, u32[]{:S(2)}) copy-start(bf16[768,2304]{1,0:T(8,128)(2,1)} %qkv_weight_ref.9) | copy-start | bytes 10616836
  5.0 4.1 %copy-start.1 = (bf16[768,768]{1,0:T(8,128)(2,1)S(1)}, bf16[768,768]{1,0:T(8,128)(2,1)}, u32[]{:S(2)}) copy-start(bf16[768,768]{1,0:T(8,128)(2,1)} %out_weight_ref.7) | copy-start | bytes 3538948
  5.0 4.1 %copy-start.3 = (s32[128,128]{1,0:T(8,128)S(1)}, s32[128,128]{1,0:T(8,128)}, u32[]{:S(2)}) copy-start(s32[128,128]{1,0:T(8,128)} %index_ref.1) | copy-start | bytes 196612
  5.1 4.1 %copy-start.4 = (f32[465,6]{0,1:T(8,128)S(1)}, f32[465,6]{0,1:T(8,128)}, u32[]{:S(2)}) copy-start(f32[465,6]{0,1:T(8,128)} %param.9) | copy-start | bytes 33484
  5.2 11.0 %collective-permute-start.2 = (bf16[97,8,128]{2,1,0:T(8,128)(2,1)S(1)}, bf16[97,8,128]{2,1,0:T(8,128)(2,1)S(1)}, u32[]{:S(2)}, u32[]{:S(2)}) collective-permute-start(bf16[97,8,128]{2,1,0:T(8,128)(2,1)S(1)} %get-tuple-element.28), channel_id=1, source_target_pairs={{0,30},{2,4},{4,2},{6,8},{8,6},{10,12},{12,10},{14,16},{16,14},{18... | collective-permute-start | bytes 595976 | tf_op jit(solution)/shard_map/ppermute | solution.py:44
  9.1 7.1 %collective-permute-start.3 = (bf16[97,8,128]{2,1,0:T(8,128)(2,1)S(1)}, bf16[97,8,128]{2,1,0:T(8,128)(2,1)S(1)}, u32[]{:S(2)}, u32[]{:S(2)}) collective-permute-start(bf16[97,8,128]{2,1,0:T(8,128)(2,1)S(1)} %get-tuple-element.23.after_ref), channel_id=1, source_target_pairs={{0,2},{2,0},{4,6},{6,4},{8,10},{10,8},{12,14},{14,12},{16,18},{18,... | collective-permute-start | bytes 595976 | tf_op jit(solution)/shard_map/ppermute | solution.py:43
  12.4 6.8 %collective-permute-start.4 = (bf16[49,8,128]{2,1,0:T(8,128)(2,1)S(1)}, bf16[49,8,128]{2,1,0:T(8,128)(2,1)S(1)}, u32[]{:S(2)}, u32[]{:S(2)}) collective-permute-start(bf16[49,8,128]{2,1,0:T(8,128)(2,1)S(1)} %get-tuple-element.29), channel_id=1, source_target_pairs={{0,30},{2,4},{4,2},{6,8},{8,6},{10,12},{12,10},{14,16},{16,14},{18... | collective-permute-start | bytes 301064 | tf_op jit(solution)/shard_map/ppermute | solution.py:44
  14.6 4.6 %collective-permute-start.5 = (bf16[49,8,128]{2,1,0:T(8,128)(2,1)S(1)}, bf16[49,8,128]{2,1,0:T(8,128)(2,1)S(1)}, u32[]{:S(2)}, u32[]{:S(2)}) collective-permute-start(bf16[49,8,128]{2,1,0:T(8,128)(2,1)S(1)} %get-tuple-element.25.after_ref), channel_id=1, source_target_pairs={{0,2},{2,0},{4,6},{6,4},{8,10},{10,8},{12,14},{14,12},{16,18},{18,... | collective-permute-start | bytes 301064 | tf_op jit(solution)/shard_map/ppermute | solution.py:43

commit v8 on v7

--- a/solution.py
+++ b/solution.py
@@ -107,25 +107,27 @@
     return message_ref[message_ref.shape[0] - 1].astype(F32)
 
 
-def message_kernel(tokens_ref, rows_ref, ends_ref, inner_ref, middle_ref, columns_ref):
-    row_count, _, feature = tokens_ref.shape
+def message_kernel(tokens_ref, rows_ref, ends_ref):
+    row_count = tokens_ref.shape[0]
+    for at in range(WLAT):
+        row = at if at < HALF_LAT else row_count - WLAT + at
+        put_cells(ends_ref, 2 * at, tokens_ref[row, :WLON, :].astype(F32)[:HALF_LON])
+        put_cells(ends_ref, 2 * at + 1, tokens_ref[row, tokens_ref.shape[1] - WLON :, :].astype(F32)[HALF_LON:])
+    put_labels(ends_ref, rows_ref[...])
+
+
+def split_kernel(tokens_ref, after_ref, normed_ref, inner_ref, middle_ref, columns_ref):
+    row_count = tokens_ref.shape[0]
     for row in range(row_count):
         floats = tokens_ref[row].astype(F32)
         columns_ref[row] = jnp.concatenate([floats[:HALF_LON], floats[-HALF_LON:]], axis=0).astype(BF16)
-        inner = floats[HALF_LON:-HALF_LON].astype(BF16)
+        inner = floats[HALF_LON:-HALF_LON]
         if HALF_LAT <= row < row_count - HALF_LAT:
-            middle_ref[row - HALF_LAT] = inner
+            middle_ref[row - HALF_LAT] = inner.astype(BF16)
         else:
             at = row if row < HALF_LAT else row - row_count + WLAT
-            put_cells(ends_ref, 2 * at, floats[:HALF_LON])
-            put_cells(ends_ref, 2 * at + 1, floats[-HALF_LON:])
-            inner_ref[at] = inner
-    put_labels(ends_ref, rows_ref[...])
-
-
-def normalize_kernel(inner_ref, normed_ref):
-    for row in range(inner_ref.shape[0]):
-        normed_ref[row] = normalize(inner_ref[row].astype(F32)).astype(BF16)
+            inner_ref[at] = inner.astype(BF16)
+            normed_ref[at] = normalize(inner).astype(BF16)
 
 
 def column_kernel(columns_ref, rows_ref, even_odd_ref, odd_even_ref):
@@ -446,19 +448,19 @@
     (label_own,) = run(
         functools.partial(label_kernel, strips), [shape(bands * strips, WIN, dtype=F32)], [region_label], flops=5 * 10**9
     )
-    ends, inner_rows, middle, columns = run(
-        message_kernel,
+    (ends,) = run(message_kernel, [shape(2 * WLAT * blocks + 1, HALF_LON, WIN)], [tokens, label_own], flops=5 * 10**9)
+    ends_received = lat_exchange(ends, 2 * HALF_LAT * blocks)
+    normed_rows, inner_rows, middle, columns = run(
+        split_kernel,
         [
-            shape(2 * WLAT * blocks + 1, HALF_LON, WIN),
+            shape(WLAT, inner_columns, feature),
             shape(WLAT, inner_columns, feature),
             shape(row_count - WLAT, inner_columns, feature),
             shape(row_count, WLON, feature),
         ],
-        [tokens, label_own],
-        flops=5 * 10**9,
-    )
-    ends_received = lat_exchange(ends, 2 * HALF_LAT * blocks)
-    (normed_rows,) = run(normalize_kernel, [shape(WLAT, inner_columns, feature)], [inner_rows])
+        [tokens, ends],
+        specs=[VMEM, ANY],
+    )
     rows_received = lat_exchange(normed_rows, HALF_LAT)
     message = shape(row_count * blocks + 1, HALF_LON, WIN)
     columns_sent = run(column_kernel, [message, message], [columns, label_own], flops=2 * 10**10)

time: 25.9 us -> 25.8 us (level)
  no operation moved by 1% of the time
where the time goes in v8:
time: 25.8 us; the launch traced here: 25.6 us
  Pallas kernels  13.8 us (53%)
  starting transfers between devices  9.23 us (36%)
  local copies, waits for them, and re-layouts  1.31 us (5%)
  waiting for transfers between devices  1.14 us (4%)
    pallas_call x10, Pallas kernels, run(): pl.pallas_call(kernel, out_shape=outs, in_specs=specs or [VMEM] * len(ope...  13.8 us
    ppermute x2, starting transfers between devices, lon_exchange(): return (lax.ppermute(odd_even, 'lon', second), even_odd)  6.11 us
    ppermute x2, starting transfers between devices, moved(): return lax.ppermute(block, axis, route)  3.12 us
    unnamed x12, local copies, waits for them, and re-layouts  1.31 us
    ppermute x2, waiting for transfers between devices, moved(): return lax.ppermute(block, axis, route)  0.87 us
  transfers between devices with their start and end apart: 6, of which 2 were waited for; matrix products, arithmetic and copies ran while one was open for 0% of the time, Pallas kernels for 39%

profile of v8, /device:TPU:0, one launch (start us, length us, event | category | flops | bytes accessed | tf_op | source)
XLA Modules:
  0.0 25.6 jit_solution(16479306300238145186)
XLA Ops:
  0.0 0.0 copy-start.2
  0.0 0.0 copy-start.5
  0.0 0.8 %copy-done.5 = s32[16,64]{1,0:T(8,128)S(1)} copy-done((s32[16,64]{1,0:T(8,128)S(1)}, s32[16,64]{1,0:T(8,128)}, u32[]{:S(2)}) %copy-start.5) | copy-done | bytes 4120
  0.8 0.1 shard_map.64.rows_ref
  1.0 0.5 %copy-done.2 = bf16[16,64,768]{2,1,0:T(8,128)(2,1)S(1)} copy-done((bf16[16,64,768]{2,1,0:T(8,128)(2,1)S(1)}, bf16[16,64,768]{2,1,0:T(8,128)(2,1)}, u32[]{:S(2)}) %copy-start.2) | copy-done | bytes 1572888
  1.5 3.0 %collective-permute-start.1 = (bf16[97,8,128]{2,1,0:T(8,128)(2,1)S(1)}, bf16[97,8,128]{2,1,0:T(8,128)(2,1)S(1)}, u32[]{:S(2)}, u32[]{:S(2)}) collective-permute-start(bf16[97,8,128]{2,1,0:T(8,128)(2,1)S(1)} %shard_map.65.after_ref), channel_id=1, source_target_pairs={{1,0},{0,1},{3,2},{2,3},{5,4},{4,5},{7,6},{6,7},{9,8},{8,9},{11,10... | collective-permute-start | bytes 595976 | tf_op jit(solution)/shard_map/ppermute | solution.py:30
  4.5 0.4 %shard_map.66 = (bf16[8,48,768]{2,1,0:T(8,128)(2,1)S(1)}, bf16[8,48,768]{2,1,0:T(8,128)(2,1)S(1)}, bf16[8,48,768]{2,1,0:T(8,128)(2,1)S(1)}, bf16[16,16,768]{2,1,0:T(8,128)(2,1)S(1)}) custom-call(bf16[16,64,768]{2,1,0:T(8,128)(2,1)S(1)} %copy-done.2, bf16[97,8,128]{2,1,0:T(8,128)(2,1)S(1)} %shard_map.65.after_ref), custom_call_target="tpu_custom_call" | custom-call | flops 1000000 | bytes 100000 | tf_op jit(solution)/shard_map/pallas_call | solution.py:48
  4.9 0.1 collective-permute-start
  5.0 0.0 copy-start
  5.0 0.0 copy-start.1
  5.0 0.0 copy-start.3
  5.1 0.0 copy-start.4
  5.1 0.1 shard_map.67
  5.2 3.9 %collective-permute-start.2 = (bf16[97,8,128]{2,1,0:T(8,128)(2,1)S(1)}, bf16[97,8,128]{2,1,0:T(8,128)(2,1)S(1)}, u32[]{:S(2)}, u32[]{:S(2)}) collective-permute-start(bf16[97,8,128]{2,1,0:T(8,128)(2,1)S(1)} %get-tuple-element.28), channel_id=1, source_target_pairs={{0,30},{2,4},{4,2},{6,8},{8,6},{10,12},{12,10},{14,16},{16,14},{18... | collective-permute-start | bytes 595976 | tf_op jit(solution)/shard_map/ppermute | solution.py:44
  9.1 0.0 collective-permute-start.3
  9.1 0.0 copy-done
  9.1 0.0 copy-done.1
  9.1 0.0 copy-done.3
  9.1 0.0 copy-done.4
  9.1 3.2 %shard_map.68 = (bf16[384,768]{1,0:T(8,128)(2,1)S(1)}, f32[6,128,128]{2,1,0:T(8,128)S(1)}) custom-call(bf16[8,48,768]{2,1,0:T(8,128)(2,1)S(1)} %get-tuple-element.21.middle_ref, f32[8,128]{1,0:T(8,128)S(1)} %shard_map.64.rows_ref, f32[6,465]{1,0:T(8,128)S(1)} %bitcast.1, s32[128,128]{1,0:T(8,128)S(1)} %copy-done.3, bf16[768,2304]{1,0:T(8,128)(2,1)S(1)} %copy-done, ...), custom_call_target="tpu_custom_call" | custom-call | flops 5000000000 | bytes 100000 | tf_op jit(solution)/shard_map/pallas_call | solution.py:48
  12.3 0.0 collective-permute-done.1.ends_ref
  12.3 0.1 shard_map.69
  12.4 2.2 %collective-permute-start.4 = (bf16[49,8,128]{2,1,0:T(8,128)(2,1)S(1)}, bf16[49,8,128]{2,1,0:T(8,128)(2,1)S(1)}, u32[]{:S(2)}, u32[]{:S(2)}) collective-permute-start(bf16[49,8,128]{2,1,0:T(8,128)(2,1)S(1)} %get-tuple-element.29), channel_id=1, source_target_pairs={{0,30},{2,4},{4,2},{6,8},{8,6},{10,12},{12,10},{14,16},{16,14},{18... | collective-permute-start | bytes 301064 | tf_op jit(solution)/shard_map/ppermute | solution.py:44
  14.6 0.0 collective-permute-start.5
  14.6 1.6 %shard_map.70.after_ref.own_ref = bf16[384,2304]{1,0:T(8,128)(2,1)S(1)} custom-call(bf16[8,48,768]{2,1,0:T(8,128)(2,1)S(1)} %get-tuple-element.20.inner_ref, bf16[768,2304]{1,0:T(8,128)(2,1)S(1)} %copy-done, bf16[49,8,128]{2,1,0:T(8,128)(2,1)S(1)} %get-tuple-element.25.after_ref), custom_call_target="tpu_custom_call" | custom-call | flops 1000000 | bytes 100000 | tf_op jit(solution)/shard_map/pallas_call | solution.py:48
  16.1 0.0 collective-permute-done.2.odd_even_ref
  16.2 0.0 collective-permute-done.3.even_odd_ref
  16.2 2.8 %shard_map.71 = (bf16[8,64,768]{2,1,0:T(8,128)(2,1)S(1)}, bf16[128,768]{1,0:T(8,128)(2,1)S(1)}, bf16[256,1536]{1,0:T(8,128)(2,1)S(1)}) custom-call(bf16[16,16,768]{2,1,0:T(8,128)(2,1)S(1)} %get-tuple-element.22.columns_ref, bf16[97,8,128]{2,1,0:T(8,128)(2,1)S(1)} %collective-permute-done.2.odd_even_ref, ...), custom_call_target="tpu_custom_call" | custom-call | flops 1000000 | bytes 100000 | tf_op jit(solution)/shard_map/pallas_call | solution.py:48
  19.0 0.3 %collective-permute-done.4.corner_odd_even_ref = bf16[49,8,128]{2,1,0:T(8,128)(2,1)S(1)} collective-permute-done((bf16[49,8,128]{2,1,0:T(8,128)(2,1)S(1)}, bf16[49,8,128]{2,1,0:T(8,128)(2,1)S(1)}, u32[]{:S(2)}, u32[]{:S(2)}) %collective-permute-start.4) | collective-permute-done | bytes 100384 | tf_op jit(solution)/shard_map/ppermute | solution.py:44
  19.2 0.0 collective-permute-done.5.corner_even_odd_ref
  19.2 2.0 %shard_map.72.corner_ref = bf16[8,16,768]{2,1,0:T(8,128)(2,1)S(1)} custom-call(bf16[16,16,768]{2,1,0:T(8,128)(2,1)S(1)} %get-tuple-element.22.columns_ref, bf16[97,8,128]{2,1,0:T(8,128)(2,1)S(1)} %collective-permute-done.2.odd_even_ref, bf16[97,8,128]{2,1,0:T(8,128)(2,1)S(1)} %collective-permute-done.3.even_odd_ref, ...), custom_call_target="tpu_custom_call" | custom-call | flops 1000000 | bytes 100000 | tf_op jit(solution)/shard_map/pallas_call | solution.py:48
  21.2 0.9 %collective-permute-done.halo_ref = bf16[8,48,768]{2,1,0:T(8,128)(2,1)S(1)} collective-permute-done((bf16[8,48,768]{2,1,0:T(8,128)(2,1)S(1)}, bf16[8,48,768]{2,1,0:T(8,128)(2,1)S(1)}, u32[]{:S(2)}, u32[]{:S(2)}) %collective-permute-start) | collective-permute-done | bytes 589856 | tf_op jit(solution)/shard_map/ppermute | solution.py:30
  22.1 3.5 %shard_map.73 = bf16[16,64,768]{2,1,0:T(8,128)(2,1)} custom-call(bf16[8,48,768]{2,1,0:T(8,128)(2,1)S(1)} %get-tuple-element.19.inner_ref, bf16[8,48,768]{2,1,0:T(8,128)(2,1)S(1)} %collective-permute-done.halo_ref, bf16[384,2304]{1,0:T(8,128)(2,1)S(1)} %shard_map.70.after_ref.own_ref, f32[16,128]{1,0:T(8,128)S(1)} %get-tuple-element.26.labels_ref, ...), custom_call_target="tpu_custom_call" | custom-call | flops 1000000 | bytes 100000 | tf_op jit(solution)/shard_map/pallas_call | solution.py:48
  (1 shorter events, 0.0 us)
Async XLA Ops:
  0.0 1.4 %copy-start.2 = (bf16[16,64,768]{2,1,0:T(8,128)(2,1)S(1)}, bf16[16,64,768]{2,1,0:T(8,128)(2,1)}, u32[]{:S(2)}) copy-start(bf16[16,64,768]{2,1,0:T(8,128)(2,1)} %tokens_ref.3) | copy-start | bytes 4718596
  0.0 0.8 %copy-start.5 = (s32[16,64]{1,0:T(8,128)S(1)}, s32[16,64]{1,0:T(8,128)}, u32[]{:S(2)}) copy-start(s32[16,64]{1,0:T(8,128)} %label_ref.1) | copy-start | bytes 12292
  1.5 10.9 %collective-permute-start.1 = (bf16[97,8,128]{2,1,0:T(8,128)(2,1)S(1)}, bf16[97,8,128]{2,1,0:T(8,128)(2,1)S(1)}, u32[]{:S(2)}, u32[]{:S(2)}) collective-permute-start(bf16[97,8,128]{2,1,0:T(8,128)(2,1)S(1)} %shard_map.65.after_ref), channel_id=1, source_target_pairs={{1,0},{0,1},{3,2},{2,3},{5,4},{4,5},{7,6},{6,7},{9,8},{8,9},{11,10... | collective-permute-start | bytes 595976 | tf_op jit(solution)/shard_map/ppermute | solution.py:30
  4.9 17.1 %collective-permute-start = (bf16[8,48,768]{2,1,0:T(8,128)(2,1)S(1)}, bf16[8,48,768]{2,1,0:T(8,128)(2,1)S(1)}, u32[]{:S(2)}, u32[]{:S(2)}) collective-permute-start(bf16[8,48,768]{2,1,0:T(8,128)(2,1)S(1)} %get-tuple-element.20.inner_ref), channel_id=1, source_target_pairs={{1,0},{0,1},{3,2},{2,3},{5,4},{4,5},{7,6},{6,7},{9,8},{8,9},{11,10... | collective-permute-start | bytes 1769480 | tf_op jit(solution)/shard_map/ppermute | solution.py:30
  5.0 4.1 %copy-start = (bf16[768,2304]{1,0:T(8,128)(2,1)S(1)}, bf16[768,2304]{1,0:T(8,128)(2,1)}, u32[]{:S(2)}) copy-start(bf16[768,2304]{1,0:T(8,128)(2,1)} %qkv_weight_ref.9) | copy-start | bytes 10616836
  5.0 4.1 %copy-start.1 = (bf16[768,768]{1,0:T(8,128)(2,1)S(1)}, bf16[768,768]{1,0:T(8,128)(2,1)}, u32[]{:S(2)}) copy-start(bf16[768,768]{1,0:T(8,128)(2,1)} %out_weight_ref.7) | copy-start | bytes 3538948
  5.0 4.1 %copy-start.3 = (s32[128,128]{1,0:T(8,128)S(1)}, s32[128,128]{1,0:T(8,128)}, u32[]{:S(2)}) copy-start(s32[128,128]{1,0:T(8,128)} %index_ref.1) | copy-start | bytes 196612
  5.1 4.1 %copy-start.4 = (f32[465,6]{0,1:T(8,128)S(1)}, f32[465,6]{0,1:T(8,128)}, u32[]{:S(2)}) copy-start(f32[465,6]{0,1:T(8,128)} %param.9) | copy-start | bytes 33484
  5.2 11.0 %collective-permute-start.2 = (bf16[97,8,128]{2,1,0:T(8,128)(2,1)S(1)}, bf16[97,8,128]{2,1,0:T(8,128)(2,1)S(1)}, u32[]{:S(2)}, u32[]{:S(2)}) collective-permute-start(bf16[97,8,128]{2,1,0:T(8,128)(2,1)S(1)} %get-tuple-element.28), channel_id=1, source_target_pairs={{0,30},{2,4},{4,2},{6,8},{8,6},{10,12},{12,10},{14,16},{16,14},{18... | collective-permute-start | bytes 595976 | tf_op jit(solution)/shard_map/ppermute | solution.py:44
  9.1 7.1 %collective-permute-start.3 = (bf16[97,8,128]{2,1,0:T(8,128)(2,1)S(1)}, bf16[97,8,128]{2,1,0:T(8,128)(2,1)S(1)}, u32[]{:S(2)}, u32[]{:S(2)}) collective-permute-start(bf16[97,8,128]{2,1,0:T(8,128)(2,1)S(1)} %get-tuple-element.23.after_ref), channel_id=1, source_target_pairs={{0,2},{2,0},{4,6},{6,4},{8,10},{10,8},{12,14},{14,12},{16,18},{18,... | collective-permute-start | bytes 595976 | tf_op jit(solution)/shard_map/ppermute | solution.py:43
  12.4 6.8 %collective-permute-start.4 = (bf16[49,8,128]{2,1,0:T(8,128)(2,1)S(1)}, bf16[49,8,128]{2,1,0:T(8,128)(2,1)S(1)}, u32[]{:S(2)}, u32[]{:S(2)}) collective-permute-start(bf16[49,8,128]{2,1,0:T(8,128)(2,1)S(1)} %get-tuple-element.29), channel_id=1, source_target_pairs={{0,30},{2,4},{4,2},{6,8},{8,6},{10,12},{12,10},{14,16},{16,14},{18... | collective-permute-start | bytes 301064 | tf_op jit(solution)/shard_map/ppermute | solution.py:44
  14.6 4.6 %collective-permute-start.5 = (bf16[49,8,128]{2,1,0:T(8,128)(2,1)S(1)}, bf16[49,8,128]{2,1,0:T(8,128)(2,1)S(1)}, u32[]{:S(2)}, u32[]{:S(2)}) collective-permute-start(bf16[49,8,128]{2,1,0:T(8,128)(2,1)S(1)} %get-tuple-element.25.after_ref), channel_id=1, source_target_pairs={{0,2},{2,0},{4,6},{6,4},{8,10},{10,8},{12,14},{14,12},{16,18},{18,... | collective-permute-start | bytes 301064 | tf_op jit(solution)/shard_map/ppermute | solution.py:43

commit v9 on v8

--- a/solution.py
+++ b/solution.py
@@ -182,9 +182,10 @@
         scores.append(product * SCALE + bias())
     numerators = [jnp.exp2(score - jnp.max(score, axis=-1, keepdims=True)) for score in scores]
     for (_, _, values, _, store), numerator in zip(entries, numerators):
-        total = jnp.sum(numerator, axis=-1, keepdims=True)
-        summed = jnp.dot(numerator.astype(BF16), values(), preferred_element_type=F32)
-        store((summed * (1.0 / total)).astype(BF16))
+        value = values()
+        both = jnp.concatenate([value, jnp.ones_like(value)], axis=1)
+        both = jnp.dot(numerator.astype(BF16), both, preferred_element_type=F32)
+        store((both[:, :HEAD] * (1.0 / both[:, HEAD:])).astype(BF16))
 
 
 def project(source, weight_ref, first, count):

time: 25.8 us -> 25.8 us (level)
  Pallas kernels: 13.8 us -> 14.1 us
    pallas_call x10, Pallas kernels: 13.8 us -> 14.1 us  [run(): pl.pallas_call(kernel, out_shape=outs, in_specs=specs or [VMEM] * len(ope...]
  transfers between devices with their start and end apart: 6 -> 6, of which waited for: 2 -> 2; matrix products, arithmetic and copies ran while one was open for 0% -> 0% of each run, Pallas kernels for 39% -> 40%
where the time goes in v9:
time: 25.8 us; the launch traced here: 25.6 us
  Pallas kernels  14.1 us (55%)
  starting transfers between devices  9.22 us (36%)
  local copies, waits for them, and re-layouts  1.31 us (5%)
  waiting for transfers between devices  0.9 us (3%)
    pallas_call x10, Pallas kernels, run(): pl.pallas_call(kernel, out_shape=outs, in_specs=specs or [VMEM] * len(ope...  14.1 us
    ppermute x2, starting transfers between devices, lon_exchange(): return (lax.ppermute(odd_even, 'lon', second), even_odd)  6.1 us
    ppermute x2, starting transfers between devices, moved(): return lax.ppermute(block, axis, route)  3.12 us
    unnamed x12, local copies, waits for them, and re-layouts  1.31 us
    ppermute x2, waiting for transfers between devices, moved(): return lax.ppermute(block, axis, route)  0.68 us
  transfers between devices with their start and end apart: 6, of which 2 were waited for; matrix products, arithmetic and copies ran while one was open for 0% of the time, Pallas kernels for 40%

profile of v9, /device:TPU:0, one launch (start us, length us, event | category | flops | bytes accessed | tf_op | source)
XLA Modules:
  0.0 25.6 jit_solution(14606009869093855669)
XLA Ops:
  0.0 0.0 copy-start.2
  0.0 0.0 copy-start.5
  0.0 0.8 %copy-done.5 = s32[16,64]{1,0:T(8,128)S(1)} copy-done((s32[16,64]{1,0:T(8,128)S(1)}, s32[16,64]{1,0:T(8,128)}, u32[]{:S(2)}) %copy-start.5) | copy-done | bytes 4120
  0.8 0.1 shard_map.64.rows_ref
  1.0 0.5 %copy-done.2 = bf16[16,64,768]{2,1,0:T(8,128)(2,1)S(1)} copy-done((bf16[16,64,768]{2,1,0:T(8,128)(2,1)S(1)}, bf16[16,64,768]{2,1,0:T(8,128)(2,1)}, u32[]{:S(2)}) %copy-start.2) | copy-done | bytes 1572888
  1.5 3.0 %collective-permute-start.1 = (bf16[97,8,128]{2,1,0:T(8,128)(2,1)S(1)}, bf16[97,8,128]{2,1,0:T(8,128)(2,1)S(1)}, u32[]{:S(2)}, u32[]{:S(2)}) collective-permute-start(bf16[97,8,128]{2,1,0:T(8,128)(2,1)S(1)} %shard_map.65.after_ref), channel_id=1, source_target_pairs={{1,0},{0,1},{3,2},{2,3},{5,4},{4,5},{7,6},{6,7},{9,8},{8,9},{11,10... | collective-permute-start | bytes 595976 | tf_op jit(solution)/shard_map/ppermute | solution.py:30
  4.5 0.4 %shard_map.66 = (bf16[8,48,768]{2,1,0:T(8,128)(2,1)S(1)}, bf16[8,48,768]{2,1,0:T(8,128)(2,1)S(1)}, bf16[8,48,768]{2,1,0:T(8,128)(2,1)S(1)}, bf16[16,16,768]{2,1,0:T(8,128)(2,1)S(1)}) custom-call(bf16[16,64,768]{2,1,0:T(8,128)(2,1)S(1)} %copy-done.2, bf16[97,8,128]{2,1,0:T(8,128)(2,1)S(1)} %shard_map.65.after_ref), custom_call_target="tpu_custom_call" | custom-call | flops 1000000 | bytes 100000 | tf_op jit(solution)/shard_map/pallas_call | solution.py:48
  4.9 0.1 collective-permute-start
  5.0 0.0 copy-start
  5.0 0.0 copy-start.1
  5.0 0.0 copy-start.3
  5.1 0.0 copy-start.4
  5.1 0.1 shard_map.67
  5.2 3.9 %collective-permute-start.2 = (bf16[97,8,128]{2,1,0:T(8,128)(2,1)S(1)}, bf16[97,8,128]{2,1,0:T(8,128)(2,1)S(1)}, u32[]{:S(2)}, u32[]{:S(2)}) collective-permute-start(bf16[97,8,128]{2,1,0:T(8,128)(2,1)S(1)} %get-tuple-element.28), channel_id=1, source_target_pairs={{0,30},{2,4},{4,2},{6,8},{8,6},{10,12},{12,10},{14,16},{16,14},{18... | collective-permute-start | bytes 595976 | tf_op jit(solution)/shard_map/ppermute | solution.py:44
  9.1 0.0 collective-permute-start.3
  9.1 0.0 copy-done
  9.1 0.0 copy-done.1
  9.1 0.0 copy-done.3
  9.1 0.0 copy-done.4
  9.1 3.3 %shard_map.68 = (bf16[384,768]{1,0:T(8,128)(2,1)S(1)}, f32[6,128,128]{2,1,0:T(8,128)S(1)}) custom-call(bf16[8,48,768]{2,1,0:T(8,128)(2,1)S(1)} %get-tuple-element.21.middle_ref, f32[8,128]{1,0:T(8,128)S(1)} %shard_map.64.rows_ref, f32[6,465]{1,0:T(8,128)S(1)} %bitcast.1, s32[128,128]{1,0:T(8,128)S(1)} %copy-done.3, bf16[768,2304]{1,0:T(8,128)(2,1)S(1)} %copy-done, ...), custom_call_target="tpu_custom_call" | custom-call | flops 5000000000 | bytes 100000 | tf_op jit(solution)/shard_map/pallas_call | solution.py:48
  12.5 0.0 collective-permute-done.1.ends_ref
  12.5 0.1 shard_map.69
  12.6 2.2 %collective-permute-start.4 = (bf16[49,8,128]{2,1,0:T(8,128)(2,1)S(1)}, bf16[49,8,128]{2,1,0:T(8,128)(2,1)S(1)}, u32[]{:S(2)}, u32[]{:S(2)}) collective-permute-start(bf16[49,8,128]{2,1,0:T(8,128)(2,1)S(1)} %get-tuple-element.29), channel_id=1, source_target_pairs={{0,30},{2,4},{4,2},{6,8},{8,6},{10,12},{12,10},{14,16},{16,14},{18... | collective-permute-start | bytes 301064 | tf_op jit(solution)/shard_map/ppermute | solution.py:44
  14.7 0.0 collective-permute-start.5
  14.7 1.6 %shard_map.70.after_ref.own_ref = bf16[384,2304]{1,0:T(8,128)(2,1)S(1)} custom-call(bf16[8,48,768]{2,1,0:T(8,128)(2,1)S(1)} %get-tuple-element.20.inner_ref, bf16[768,2304]{1,0:T(8,128)(2,1)S(1)} %copy-done, bf16[49,8,128]{2,1,0:T(8,128)(2,1)S(1)} %get-tuple-element.25.after_ref), custom_call_target="tpu_custom_call" | custom-call | flops 1000000 | bytes 100000 | tf_op jit(solution)/shard_map/pallas_call | solution.py:48
  16.3 0.0 collective-permute-done.2.odd_even_ref
  16.3 0.0 collective-permute-done.3.even_odd_ref
  16.3 2.8 %shard_map.71 = (bf16[8,64,768]{2,1,0:T(8,128)(2,1)S(1)}, bf16[128,768]{1,0:T(8,128)(2,1)S(1)}, bf16[256,1536]{1,0:T(8,128)(2,1)S(1)}) custom-call(bf16[16,16,768]{2,1,0:T(8,128)(2,1)S(1)} %get-tuple-element.22.columns_ref, bf16[97,8,128]{2,1,0:T(8,128)(2,1)S(1)} %collective-permute-done.2.odd_even_ref, ...), custom_call_target="tpu_custom_call" | custom-call | flops 1000000 | bytes 100000 | tf_op jit(solution)/shard_map/pallas_call | solution.py:48
  19.2 0.2 collective-permute-done.4.corner_odd_even_ref
  19.4 0.0 collective-permute-done.5.corner_even_odd_ref
  19.4 2.0 %shard_map.72.corner_ref = bf16[8,16,768]{2,1,0:T(8,128)(2,1)S(1)} custom-call(bf16[16,16,768]{2,1,0:T(8,128)(2,1)S(1)} %get-tuple-element.22.columns_ref, bf16[97,8,128]{2,1,0:T(8,128)(2,1)S(1)} %collective-permute-done.2.odd_even_ref, bf16[97,8,128]{2,1,0:T(8,128)(2,1)S(1)} %collective-permute-done.3.even_odd_ref, ...), custom_call_target="tpu_custom_call" | custom-call | flops 1000000 | bytes 100000 | tf_op jit(solution)/shard_map/pallas_call | solution.py:48
  21.4 0.7 %collective-permute-done.halo_ref = bf16[8,48,768]{2,1,0:T(8,128)(2,1)S(1)} collective-permute-done((bf16[8,48,768]{2,1,0:T(8,128)(2,1)S(1)}, bf16[8,48,768]{2,1,0:T(8,128)(2,1)S(1)}, u32[]{:S(2)}, u32[]{:S(2)}) %collective-permute-start) | collective-permute-done | bytes 589856 | tf_op jit(solution)/shard_map/ppermute | solution.py:30
  22.1 3.6 %shard_map.73 = bf16[16,64,768]{2,1,0:T(8,128)(2,1)} custom-call(bf16[8,48,768]{2,1,0:T(8,128)(2,1)S(1)} %get-tuple-element.19.inner_ref, bf16[8,48,768]{2,1,0:T(8,128)(2,1)S(1)} %collective-permute-done.halo_ref, bf16[384,2304]{1,0:T(8,128)(2,1)S(1)} %shard_map.70.after_ref.own_ref, f32[16,128]{1,0:T(8,128)S(1)} %get-tuple-element.26.labels_ref, ...), custom_call_target="tpu_custom_call" | custom-call | flops 1000000 | bytes 100000 | tf_op jit(solution)/shard_map/pallas_call | solution.py:48
  (1 shorter events, 0.0 us)
Async XLA Ops:
  0.0 1.4 %copy-start.2 = (bf16[16,64,768]{2,1,0:T(8,128)(2,1)S(1)}, bf16[16,64,768]{2,1,0:T(8,128)(2,1)}, u32[]{:S(2)}) copy-start(bf16[16,64,768]{2,1,0:T(8,128)(2,1)} %tokens_ref.3) | copy-start | bytes 4718596
  0.0 0.8 %copy-start.5 = (s32[16,64]{1,0:T(8,128)S(1)}, s32[16,64]{1,0:T(8,128)}, u32[]{:S(2)}) copy-start(s32[16,64]{1,0:T(8,128)} %label_ref.1) | copy-start | bytes 12292
  1.5 11.0 %collective-permute-start.1 = (bf16[97,8,128]{2,1,0:T(8,128)(2,1)S(1)}, bf16[97,8,128]{2,1,0:T(8,128)(2,1)S(1)}, u32[]{:S(2)}, u32[]{:S(2)}) collective-permute-start(bf16[97,8,128]{2,1,0:T(8,128)(2,1)S(1)} %shard_map.65.after_ref), channel_id=1, source_target_pairs={{1,0},{0,1},{3,2},{2,3},{5,4},{4,5},{7,6},{6,7},{9,8},{8,9},{11,10... | collective-permute-start | bytes 595976 | tf_op jit(solution)/shard_map/ppermute | solution.py:30
  4.9 17.1 %collective-permute-start = (bf16[8,48,768]{2,1,0:T(8,128)(2,1)S(1)}, bf16[8,48,768]{2,1,0:T(8,128)(2,1)S(1)}, u32[]{:S(2)}, u32[]{:S(2)}) collective-permute-start(bf16[8,48,768]{2,1,0:T(8,128)(2,1)S(1)} %get-tuple-element.20.inner_ref), channel_id=1, source_target_pairs={{1,0},{0,1},{3,2},{2,3},{5,4},{4,5},{7,6},{6,7},{9,8},{8,9},{11,10... | collective-permute-start | bytes 1769480 | tf_op jit(solution)/shard_map/ppermute | solution.py:30
  5.0 4.1 %copy-start = (bf16[768,2304]{1,0:T(8,128)(2,1)S(1)}, bf16[768,2304]{1,0:T(8,128)(2,1)}, u32[]{:S(2)}) copy-start(bf16[768,2304]{1,0:T(8,128)(2,1)} %qkv_weight_ref.9) | copy-start | bytes 10616836
  5.0 4.1 %copy-start.1 = (bf16[768,768]{1,0:T(8,128)(2,1)S(1)}, bf16[768,768]{1,0:T(8,128)(2,1)}, u32[]{:S(2)}) copy-start(bf16[768,768]{1,0:T(8,128)(2,1)} %out_weight_ref.7) | copy-start | bytes 3538948
  5.0 4.1 %copy-start.3 = (s32[128,128]{1,0:T(8,128)S(1)}, s32[128,128]{1,0:T(8,128)}, u32[]{:S(2)}) copy-start(s32[128,128]{1,0:T(8,128)} %index_ref.1) | copy-start | bytes 196612
  5.1 4.1 %copy-start.4 = (f32[465,6]{0,1:T(8,128)S(1)}, f32[465,6]{0,1:T(8,128)}, u32[]{:S(2)}) copy-start(f32[465,6]{0,1:T(8,128)} %param.9) | copy-start | bytes 33484
  5.2 11.1 %collective-permute-start.2 = (bf16[97,8,128]{2,1,0:T(8,128)(2,1)S(1)}, bf16[97,8,128]{2,1,0:T(8,128)(2,1)S(1)}, u32[]{:S(2)}, u32[]{:S(2)}) collective-permute-start(bf16[97,8,128]{2,1,0:T(8,128)(2,1)S(1)} %get-tuple-element.28), channel_id=1, source_target_pairs={{0,30},{2,4},{4,2},{6,8},{8,6},{10,12},{12,10},{14,16},{16,14},{18... | collective-permute-start | bytes 595976 | tf_op jit(solution)/shard_map/ppermute | solution.py:44
  9.1 7.2 %collective-permute-start.3 = (bf16[97,8,128]{2,1,0:T(8,128)(2,1)S(1)}, bf16[97,8,128]{2,1,0:T(8,128)(2,1)S(1)}, u32[]{:S(2)}, u32[]{:S(2)}) collective-permute-start(bf16[97,8,128]{2,1,0:T(8,128)(2,1)S(1)} %get-tuple-element.23.after_ref), channel_id=1, source_target_pairs={{0,2},{2,0},{4,6},{6,4},{8,10},{10,8},{12,14},{14,12},{16,18},{18,... | collective-permute-start | bytes 595976 | tf_op jit(solution)/shard_map/ppermute | solution.py:43
  12.6 6.8 %collective-permute-start.4 = (bf16[49,8,128]{2,1,0:T(8,128)(2,1)S(1)}, bf16[49,8,128]{2,1,0:T(8,128)(2,1)S(1)}, u32[]{:S(2)}, u32[]{:S(2)}) collective-permute-start(bf16[49,8,128]{2,1,0:T(8,128)(2,1)S(1)} %get-tuple-element.29), channel_id=1, source_target_pairs={{0,30},{2,4},{4,2},{6,8},{8,6},{10,12},{12,10},{14,16},{16,14},{18... | collective-permute-start | bytes 301064 | tf_op jit(solution)/shard_map/ppermute | solution.py:44
  14.7 4.6 %collective-permute-start.5 = (bf16[49,8,128]{2,1,0:T(8,128)(2,1)S(1)}, bf16[49,8,128]{2,1,0:T(8,128)(2,1)S(1)}, u32[]{:S(2)}, u32[]{:S(2)}) collective-permute-start(bf16[49,8,128]{2,1,0:T(8,128)(2,1)S(1)} %get-tuple-element.25.after_ref), channel_id=1, source_target_pairs={{0,2},{2,0},{4,6},{6,4},{8,10},{10,8},{12,14},{14,12},{16,18},{18,... | collective-permute-start | bytes 301064 | tf_op jit(solution)/shard_map/ppermute | solution.py:43
